TPU v7x, 32 devices: a whole 2x2x4 slice. The times are simulated.
32 devices in a mesh: tm: 8 (over z, y), chan: 4 (over x, core).
Axes of the slice: x: 2, y: 2, z: 4, core: 2. Of those that a mesh axis runs over, the one named last changes fastest.
Arguments:
- signals: bfloat16 [32768, 2048], P('tm', 'chan')
- channel_node: int32 [2048], P('chan'), may hold values from 0 to 127, as said below
- lag_offsets: int32 [8], replicated, may hold values from 0 to 512, as said below
Outputs:
- r_factor: float32 [1024, 1024], replicated
Inputs may be any that keep to these rules, and one draw needn't show every extreme that they name: `channel_node`: every node is named by exactly 16 channels; which channels, and so which channel groups, is drawn. `lag_offsets`: strictly increasing; the first is 0 and the last is 512.
All inputs are finite; a program needn't handle non-finite values.
Results may differ from a plain program's by a relative error of at most 0.0003.
Values sent between devices are 32-bit elements; how exact they have to be, the bound alone decides.
No kernel may reach another device: no remote copies, remote signals or barrier semaphores. Data moves between devices by JAX's collectives and lax.ppermute only.
A program may use at most 64 MiB of HBM per device.

v0:
```python
import math

import jax
import jax.numpy as jnp
from jax import lax
from jax.sharding import PartitionSpec as P

NODES = 128
CH = 2048
MAXLAG = 512


def from_behind(value, axis, steps):
    count = lax.axis_size(axis)
    leading, last = (max(0, -steps), min(count, count - steps))
    return lax.ppermute(value, axis, [(source, source + steps) for source in range(leading, last)])


def on_device(signals, channel_node, lag_offsets):
    group_count = lax.axis_size("chan")
    lag_count = lag_offsets.shape[0]
    group_width = NODES // group_count
    onehot = (channel_node[:, None] == jnp.arange(NODES, dtype=jnp.int32)[None, :]).astype(
        jnp.bfloat16
    )
    partial_value = jnp.dot(signals, onehot, preferred_element_type=jnp.float32)
    node_scale = 1.0 / math.sqrt(CH // NODES)
    node_share = (
        lax.psum_scatter(partial_value, "chan", scatter_dimension=1, tiled=True) * node_scale
    )
    rim_rows = from_behind(node_share[:MAXLAG], "tm", -1)
    extended = jnp.concatenate([node_share, rim_rows], axis=0)
    time_rows = node_share.shape[0]
    columns = []
    for lag_index in range(lag_count):
        columns.append(
            lax.dynamic_slice(
                extended, (lag_offsets[lag_index], jnp.int32(0)), (time_rows, group_width)
            )
        )
    panel = jnp.concatenate(columns, axis=1)
    hankel = lax.all_to_all(panel, "chan", split_axis=0, concat_axis=1, tiled=True)
    row_total = hankel.shape[0] * lax.axis_size("tm") * group_count
    local_gram = lax.dot_general(
        hankel,
        hankel,
        (((0,), (0,)), ((), ())),
        precision=lax.Precision.HIGHEST,
        preferred_element_type=jnp.float32,
    )
    gram_matrix = lax.psum(local_gram, ("tm", "chan"))
    return jnp.linalg.cholesky(gram_matrix / row_total).T


def solution(mesh):
    in_specs = (P("tm", "chan"), P("chan"), P())
    out_specs = P()
    return jax.shard_map(
        on_device, mesh=mesh, in_specs=in_specs, out_specs=out_specs, check_vma=False
    )
```

profile of v0, /device:TPU:0, one launch (start us, length us, event | category | flops | bytes accessed | tf_op | source)
XLA Modules:
  0.0 513.8 jit_solution(9393404570053834198)
XLA Ops:
  6.5 5.2 %convolution_bitcast_fusion = f32[4096,128]{0,1:T(8,128)} fusion(bf16[4096,512]{1,0:T(8,128)(2,1)} %param.3, s32[512]{0:T(512)} %param.4), kind=kOutput, calls=%fused_computation | convolution fusion | flops 537001984 | bytes 6293504 | tf_op jit(solution)/shard_map/dot_general | solution.py:26
  11.8 34.2 %reduce-scatter.2.cloned.1.call-done = f32[4096,32]{0,1:T(8,128)} async-done(((f32[4096,128]{0,1:T(8,128)}), f32[4096,32]{0,1:T(8,128)}) %reduce-scatter.2.cloned.1.call-update) | async-done | bytes 524304 | tf_op jit(solution)/shard_map/reduce_scatter | solution.py:29
  67.4 51.0 %all_to_all.19 = f32[4,1024,256]{1,2,0:T(8,128)S(1)} all-to-all(f32[4,1024,256]{1,2,0:T(8,128)S(1)} %bitcast.64), channel_id=1, replica_groups=mesh['tm'=8,'chan'=4] {'chan'}, dimensions={0} | all-to-all | bytes 8388608 | tf_op jit(solution)/shard_map/all_to_all | solution.py:42
  118.4 14.9 %fusion.48 = f32[1024,1024]{0,1:T(8,128)} fusion(f32[1024,1024]{0,1:T(8,128)S(1)} %bitcast.66), kind=kOutput, calls=%fused_computation.117 | convolution fusion | flops 12884901888 | bytes 8388608 | tf_op jit(solution)/shard_map/dot_general | solution.py:44
  133.3 143.1 %all-reduce.3.cloned.1.call-done = f32[1024,1024]{0,1:T(8,128)} async-done(((f32[1024,1024]{0,1:T(8,128)}), f32[1024,1024]{0,1:T(8,128)}) %all-reduce.3.cloned.1.call-update) | async-done | bytes 4194320 | tf_op jit(solution)/shard_map/psum | solution.py:51
  276.3 5.0 broadcast_multiply_fusion
  281.4 5.8 %copy.9 = f32[1024,1024]{1,0:T(8,128)} copy(f32[1024,1024]{0,1:T(8,128)} %broadcast_multiply_fusion) | data formatting | bytes 8388608 | tf_op jit(solution)/shard_map/div | solution.py:52
  287.2 4.4 fusion
  293.6 11.7 %cholesky.223 = f32[128,128]{1,0:T(8,128)S(1)} custom-call(f32[128,128]{1,0:T(8,128)S(1)} %cholesky.580), custom_call_target="Cholesky" | custom-call | tf_op jit(solution)/shard_map/jit(cholesky)/cholesky | solution.py:52
  305.4 9.8 %custom-call.59 = f32[1,128,128]{1,2,0:T(8,128)S(1)} custom-call(f32[1,128,128]{2,1,0:T(8,128)S(1)} %get-tuple-element.26), custom_call_target="InvertDiagBlocksLowerTriangular" | custom-call | tf_op jit(solution)/shard_map/jit(cholesky)/cholesky | solution.py:52
  315.2 2.5 cholesky.255
  317.7 2.3 constant_dynamic-update-slice_fusion
  321.6 11.9 %cholesky.244 = f32[128,128]{1,0:T(8,128)S(1)} custom-call(f32[128,128]{1,0:T(8,128)S(1)} %cholesky.584), custom_call_target="Cholesky" | custom-call | tf_op jit(solution)/shard_map/jit(cholesky)/cholesky | solution.py:52
  334.1 9.8 %custom-call.60 = f32[1,128,128]{1,2,0:T(8,128)S(1)} custom-call(f32[1,128,128]{2,1,0:T(8,128)S(1)} %get-tuple-element.23), custom_call_target="InvertDiagBlocksLowerTriangular" | custom-call | tf_op jit(solution)/shard_map/jit(cholesky)/cholesky | solution.py:52
  345.1 2.1 convolution_subtract_fusion.1
  347.3 11.7 %cholesky.468 = f32[128,128]{1,0:T(8,128)S(1)} custom-call(f32[128,128]{1,0:T(8,128)S(1)} %cholesky.589), custom_call_target="Cholesky" | custom-call | tf_op jit(solution)/shard_map/jit(cholesky)/cholesky | solution.py:52
  360.2 9.8 %custom-call.61 = f32[1,128,128]{1,2,0:T(8,128)S(1)} custom-call(f32[1,128,128]{2,1,0:T(8,128)S(1)} %get-tuple-element.20), custom_call_target="InvertDiagBlocksLowerTriangular" | custom-call | tf_op jit(solution)/shard_map/jit(cholesky)/cholesky | solution.py:52
  371.2 2.3 convolution_subtract_fusion.2
  373.6 11.9 %cholesky.487 = f32[128,128]{1,0:T(8,128)S(1)} custom-call(f32[128,128]{1,0:T(8,128)S(1)} %cholesky.594), custom_call_target="Cholesky" | custom-call | tf_op jit(solution)/shard_map/jit(cholesky)/cholesky | solution.py:52
  386.8 9.8 %custom-call.62 = f32[1,128,128]{1,2,0:T(8,128)S(1)} custom-call(f32[1,128,128]{2,1,0:T(8,128)S(1)} %get-tuple-element.17), custom_call_target="InvertDiagBlocksLowerTriangular" | custom-call | tf_op jit(solution)/shard_map/jit(cholesky)/cholesky | solution.py:52
  397.7 2.4 convolution_subtract_fusion.3
  400.1 11.7 %cholesky.506 = f32[128,128]{1,0:T(8,128)S(1)} custom-call(f32[128,128]{1,0:T(8,128)S(1)} %cholesky.599), custom_call_target="Cholesky" | custom-call | tf_op jit(solution)/shard_map/jit(cholesky)/cholesky | solution.py:52
  413.1 10.2 %custom-call.63 = f32[1,128,128]{1,2,0:T(8,128)S(1)} custom-call(f32[1,128,128]{2,1,0:T(8,128)S(1)} %get-tuple-element.14), custom_call_target="InvertDiagBlocksLowerTriangular" | custom-call | tf_op jit(solution)/shard_map/jit(cholesky)/cholesky | solution.py:52
  424.3 2.3 convolution_subtract_fusion.4
  426.6 11.7 %cholesky.526 = f32[128,128]{1,0:T(8,128)S(1)} custom-call(f32[128,128]{1,0:T(8,128)S(1)} %cholesky.604), custom_call_target="Cholesky" | custom-call | tf_op jit(solution)/shard_map/jit(cholesky)/cholesky | solution.py:52
  439.6 9.8 %custom-call.64 = f32[1,128,128]{1,2,0:T(8,128)S(1)} custom-call(f32[1,128,128]{2,1,0:T(8,128)S(1)} %get-tuple-element.11), custom_call_target="InvertDiagBlocksLowerTriangular" | custom-call | tf_op jit(solution)/shard_map/jit(cholesky)/cholesky | solution.py:52
  450.3 2.0 convolution_subtract_fusion.5
  452.4 11.9 %cholesky.546 = f32[128,128]{1,0:T(8,128)S(1)} custom-call(f32[128,128]{1,0:T(8,128)S(1)} %cholesky.609), custom_call_target="Cholesky" | custom-call | tf_op jit(solution)/shard_map/jit(cholesky)/cholesky | solution.py:52
  465.5 9.8 %custom-call.65 = f32[1,128,128]{1,2,0:T(8,128)S(1)} custom-call(f32[1,128,128]{2,1,0:T(8,128)S(1)} %get-tuple-element.8), custom_call_target="InvertDiagBlocksLowerTriangular" | custom-call | tf_op jit(solution)/shard_map/jit(cholesky)/cholesky | solution.py:52
  478.0 11.7 %cholesky.564 = f32[128,128]{1,0:T(8,128)S(1)} custom-call(f32[128,128]{1,0:T(8,128)S(1)} %convolution_subtract_fusion.6), custom_call_target="Cholesky" | custom-call | tf_op jit(solution)/shard_map/jit(cholesky)/cholesky | solution.py:52
  496.6 4.8 select_bitcast_fusion
  501.4 5.3 %copy.10 = f32[1024,1024]{1,0:T(8,128)} copy(f32[1024,1024]{0,1:T(8,128)} %select_bitcast_fusion) | data formatting | bytes 8388608 | tf_op jit(solution)/shard_map/transpose | solution.py:52
  (52 shorter events, 27.1 us)
Async XLA Ops:
  6.5 41.9 %copy-start.1 = (s32[8]{0:T(128)S(1)}, s32[8]{0:T(128)}, u32[]{:S(2)}) copy-start(s32[8]{0:T(128)} %param.5) | copy-start | bytes 100
  6.5 39.5 %reduce-scatter.2.cloned.1.call-start = ((), (), s32[]{:S(2)}) async-start(), calls=%async_computation.2 | async-start | bytes 2621440 | tf_op jit(solution)/shard_map/reduce_scatter | solution.py:29
  11.7 264.6 %all-reduce.3.cloned.1.call-start = ((), (), s32[]{:S(2)}) async-start(), calls=%async_computation.3 | async-start | bytes 8388608 | tf_op jit(solution)/shard_map/psum | solution.py:51
  47.1 16.8 %collective-permute-start = (f32[512,32]{0,1:T(8,128)S(1)}, f32[512,32]{0,1:T(8,128)S(1)}, u32[]{:S(2)}, u32[]{:S(2)}) collective-permute-start(f32[512,32]{0,1:T(8,128)S(1)} %slice.213), channel_id=1, source_target_pairs={{4,0},{8,4},{12,8},{16,12},{20,16},{24,20},{28,24},{5,1},{9,5},{13... | collective-permute-start | bytes 196616 | tf_op jit(solution)/shard_map/ppermute | solution.py:16
  291.7 1.9 copy-start
Sparse Core Ops, SparseCore 0:
  11.9 34.1 reduce-scatter.1
  133.4 142.8 all-reduce.2
where the time goes:
time: 519 us; the launch traced here: 514 us
  other arithmetic  190 us (37%)
  waiting for transfers between devices  177 us (34%)
  blocking collectives  51 us (10%)
  matrix products  43 us (8%)
  between operations  33.6 us (6%)
  local copies, waits for them, and re-layouts  16.9 us (3%)
    another operation x30, other arithmetic, on_device(): return jnp.linalg.cholesky(gram_matrix / row_total).T  172 us
    psum x1, waiting for transfers between devices, on_device(): gram_matrix = lax.psum(local_gram, ('tm', 'chan'))  143 us
    all_to_all x1, blocking collectives, on_device(): lax.all_to_all(panel, 'chan', split_axis=0, concat_axis=1, tiled=True)  51 us
    reduce_scatter x1, waiting for transfers between devices, on_device(): lax.psum_scatter(partial_value, 'chan', scatter_dimension=1, tiled=True)  34.2 us
    another operation x14, matrix products, on_device(): return jnp.linalg.cholesky(gram_matrix / row_total).T  22.9 us
    dot_general x1, matrix products, on_device(): lax.dot_general(hankel, hankel, (((0,), (0,)), ((), ())), precision=lax.P...  14.9 us
  transfers between devices with their start and end apart: 3, of which 2 were waited for; matrix products, arithmetic and copies ran while one was open for 0% of the time, Pallas kernels for 0%

commit v1 on v0

v1 whole, which is shorter than its diff:
```python
import functools
import math

import jax
import jax.numpy as jnp
from jax import lax
from jax.experimental import pallas as pl
from jax.experimental.pallas import tpu as pltpu
from jax.sharding import PartitionSpec as P

NODES = 128
CH = 2048
MAXLAG = 512
BLOCK = 128
GROUP = 8
HIGHEST = lax.Precision.HIGHEST
CONTRACT_ROWS = (((0,), (0,)), ((), ()))


def swap(value, axis, bit):
    count = lax.axis_size(axis)
    return lax.ppermute(value, axis, [(i, i ^ bit) for i in range(count)])


def bits_of(axis):
    count = lax.axis_size(axis)
    return [1 << i for i in range(count.bit_length() - 1)]


def halve(value, axis, bit):
    half = value.shape[0] // 2
    mine = (lax.axis_index(axis) // bit) % 2
    send = lax.dynamic_slice_in_dim(value, (1 - mine) * half, half, 0)
    keep = lax.dynamic_slice_in_dim(value, mine * half, half, 0)
    return keep + swap(send, axis, bit)


def scatter_rows(value, axis):
    bits = bits_of(axis)
    parts = value.reshape((2,) * len(bits) + (value.shape[0] >> len(bits), value.shape[1]))
    for place, bit in enumerate(bits):
        dim = len(bits) - 1 - place
        mine = (lax.axis_index(axis) // bit) % 2
        send = lax.dynamic_index_in_dim(parts, 1 - mine, dim, keepdims=False)
        keep = lax.dynamic_index_in_dim(parts, mine, dim, keepdims=False)
        parts = keep + swap(send, axis, bit)
    return parts


def double(value, axis, bit):
    mine = (lax.axis_index(axis) // bit) % 2
    other = swap(value, axis, bit)
    low = jnp.where(mine == 0, value, other)
    high = jnp.where(mine == 0, other, value)
    return jnp.concatenate([low, high], axis=0)


def sum_over_devices(value):
    stages = [(axis, bit) for axis in ("chan", "tm") for bit in bits_of(axis)]
    rows = value.shape[0]
    padded = -rows % (1 << len(stages))
    if padded:
        value = jnp.pad(value, ((0, padded), (0, 0)))
    for axis, bit in stages:
        value = halve(value, axis, bit)
    for axis, bit in stages[::-1]:
        value = double(value, axis, bit)
    return value[:rows] if padded else value


def rows_after(first_rows):
    tm, chan = lax.axis_size("tm"), lax.axis_size("chan")
    total = tm * chan
    return lax.ppermute(first_rows, ("tm", "chan"), [(i, i - 1) for i in range(1, total)])


def gram_kernel(lags_ref, rows_ref, after_ref, out_ref, ext_ref, high_ref, low_ref):
    rows = rows_ref.shape[0]
    lag_count = lags_ref.shape[0]
    width = NODES // 4
    ext_ref[:rows, :] = rows_ref[...]
    ext_ref[rows:, :] = after_ref[...]
    lane_part = lax.broadcasted_iota(jnp.int32, (BLOCK, BLOCK), 1) // width

    def build(step, _):
        start = step * BLOCK
        here = pl.ds(pl.multiple_of(start, BLOCK), BLOCK)
        for half in range(2):
            lagged = [ext_ref[pl.ds(start + lags_ref[4 * half + i], BLOCK), :] for i in range(4)]
            for group in range(4):
                block = None
                for i in range(4):
                    shift = (i - group) % 4 * width
                    part = pltpu.roll(lagged[i], shift, 1) if shift else lagged[i]
                    block = part if block is None else jnp.where(lane_part == i, part, block)
                high = block.astype(jnp.bfloat16)
                low = (block - high.astype(jnp.float32)).astype(jnp.bfloat16)
                column = (2 * group + half) * BLOCK
                high_ref[here, column : column + BLOCK] = high
                low_ref[here, column : column + BLOCK] = low
        return 0

    lax.fori_loop(0, rows // BLOCK, build, 0)
    count = lag_count * NODES // BLOCK

    def product(left, right):
        return lax.dot_general(left, right, CONTRACT_ROWS, preferred_element_type=jnp.float32)

    index = 0
    for k in range(count):
        mine = slice(k * BLOCK, (k + 1) * BLOCK)
        rest = slice(k * BLOCK, None)
        panel = product(high_ref[:, mine], high_ref[:, rest])
        panel = panel + product(high_ref[:, mine], low_ref[:, rest])
        panel = panel + product(low_ref[:, mine], high_ref[:, rest])
        for j in range(count - k):
            out_ref[index * BLOCK : (index + 1) * BLOCK, :] = panel[:, j * BLOCK : (j + 1) * BLOCK]
            index += 1


def gram_blocks(rows, after, lags):
    size = lags.shape[0] * NODES
    count = size // BLOCK
    blocks = count * (count + 1) // 2
    return pl.pallas_call(
        gram_kernel,
        out_shape=jax.ShapeDtypeStruct((blocks * BLOCK, BLOCK), jnp.float32),
        in_specs=[
            pl.BlockSpec(memory_space=pltpu.SMEM),
            pl.BlockSpec(memory_space=pltpu.VMEM),
            pl.BlockSpec(memory_space=pltpu.VMEM),
        ],
        out_specs=pl.BlockSpec(memory_space=pltpu.VMEM),
        scratch_shapes=[
            pltpu.VMEM((rows.shape[0] + after.shape[0], NODES), jnp.float32),
            pltpu.VMEM((rows.shape[0], size), jnp.bfloat16),
            pltpu.VMEM((rows.shape[0], size), jnp.bfloat16),
        ],
        compiler_params=pltpu.CompilerParams(vmem_limit_bytes=40 << 20),
    )(lags, rows, after)


def row_of(value, index):
    return jnp.broadcast_to(value[index : index + 1, :], value.shape)


def column_of(value, index):
    return jnp.broadcast_to(value[:, index : index + 1], value.shape)


def factor_block(block):
    count = len(block)
    sub = lax.broadcasted_iota(jnp.int32, (GROUP, BLOCK), 0)
    lane = lax.broadcasted_iota(jnp.int32, (GROUP, BLOCK), 1)
    block = list(block)
    inverse = [jnp.where(lane == sub + GROUP * s, 1.0, 0.0) for s in range(count)]
    for g in range(count):
        columns = [column_of(block[g], GROUP * g + m) for m in range(GROUP)]
        top, top_inverse = block[g], inverse[g]
        scale, factors, rows, inverse_rows = [], {}, [], []
        for m in range(GROUP):
            scale.append(lax.rsqrt(row_of(columns[m], m)))
            rows.append(row_of(top, m) * scale[m])
            inverse_rows.append(row_of(top_inverse, m) * scale[m])
            left = columns[m] * scale[m]
            for n in range(m + 1, GROUP):
                factors[m, n] = row_of(left, n)
                columns[n] = columns[n] - left * factors[m, n]
            below = jnp.where(sub > m, left, 0.0)
            top = jnp.where(sub == m, rows[m], top - below * rows[m])
            top_inverse = jnp.where(sub == m, inverse_rows[m], top_inverse - below * inverse_rows[m])
        block[g] = jnp.where(lane >= sub + GROUP * g, top, 0.0)
        inverse[g] = top_inverse
        for s in range(g + 1, count):
            columns = [column_of(block[s], GROUP * g + m) for m in range(GROUP)]
            for m in range(GROUP):
                left = columns[m] * scale[m]
                for n in range(m + 1, GROUP):
                    columns[n] = columns[n] - left * factors[m, n]
                block[s] = block[s] - left * rows[m]
                inverse[s] = inverse[s] - left * inverse_rows[m]
    return block, inverse


def cholesky_kernel(scale, blocks_ref, out_ref, panel_ref, inverse_ref):
    size = out_ref.shape[0]
    count = size // BLOCK
    first = [k * count - k * (k - 1) // 2 for k in range(count)]
    out_ref[...] = jnp.zeros_like(out_ref)

    def step(k, _):
        start = pl.multiple_of(k * BLOCK, BLOCK)
        for kk in range(count):

            @pl.when(k == kk)
            def _():
                mine = slice(kk * BLOCK, (kk + 1) * BLOCK)
                for j in range(kk, count):
                    place = (first[kk] + j - kk) * BLOCK
                    panel_ref[:, j * BLOCK : (j + 1) * BLOCK] = blocks_ref[place : place + BLOCK, :] * scale
                if kk:
                    panel_ref[:, kk * BLOCK :] -= lax.dot_general(
                        out_ref[: kk * BLOCK, mine],
                        out_ref[: kk * BLOCK, kk * BLOCK :],
                        CONTRACT_ROWS,
                        precision=HIGHEST,
                        preferred_element_type=jnp.float32,
                    )

        block = [panel_ref[GROUP * s : GROUP * (s + 1), pl.ds(start, BLOCK)] for s in range(BLOCK // GROUP)]
        block, inverse = factor_block(block)
        for s in range(BLOCK // GROUP):
            out_ref[pl.ds(pl.multiple_of(start + GROUP * s, GROUP), GROUP), pl.ds(start, BLOCK)] = block[s]
            inverse_ref[GROUP * s : GROUP * (s + 1), :] = inverse[s]
        for kk in range(count - 1):

            @pl.when(k == kk)
            def _():
                out_ref[kk * BLOCK : (kk + 1) * BLOCK, (kk + 1) * BLOCK :] = jnp.dot(
                    inverse_ref[...],
                    panel_ref[:, (kk + 1) * BLOCK :],
                    precision=HIGHEST,
                    preferred_element_type=jnp.float32,
                )

        return 0

    lax.fori_loop(0, count, step, 0)


def cholesky(blocks, size, scale):
    return pl.pallas_call(
        functools.partial(cholesky_kernel, scale),
        out_shape=jax.ShapeDtypeStruct((size, size), jnp.float32),
        in_specs=[pl.BlockSpec(memory_space=pltpu.VMEM)],
        out_specs=pl.BlockSpec(memory_space=pltpu.VMEM),
        scratch_shapes=[pltpu.VMEM((BLOCK, size), jnp.float32), pltpu.VMEM((BLOCK, BLOCK), jnp.float32)],
        compiler_params=pltpu.CompilerParams(vmem_limit_bytes=40 << 20),
    )(blocks)


def on_device(signals, channel_node, lag_offsets):
    node_scale = 1.0 / math.sqrt(CH // NODES)
    onehot = jnp.where(channel_node[:, None] == jnp.arange(NODES, dtype=jnp.int32)[None, :], node_scale, 0.0)
    nodes = jnp.dot(signals, onehot.astype(jnp.bfloat16), preferred_element_type=jnp.float32)
    total_rows = nodes.shape[0] * lax.axis_size("tm")
    nodes = scatter_rows(nodes, "chan")
    after = rows_after(nodes[:MAXLAG])
    blocks = gram_blocks(nodes, after, lag_offsets)
    blocks = sum_over_devices(blocks)
    return cholesky(blocks, lag_offsets.shape[0] * NODES, 1.0 / total_rows)


def solution(mesh):
    return jax.shard_map(
        on_device, mesh=mesh, in_specs=(P("tm", "chan"), P("chan"), P()), out_specs=P(), check_vma=False
    )
```

time: 519 us -> 164 us (0.32)
  other arithmetic: 190 us -> 3.54 us
  waiting for transfers between devices: 177 us -> 66.8 us
  blocking collectives: 51 us -> 0 us
  Pallas kernels: 0 us -> 49.8 us
  matrix products: 43 us -> 5.16 us
  between operations: 33.6 us -> 0.23 us
  starting transfers between devices: 1.34 us -> 27.6 us
  local copies, waits for them, and re-layouts: 16.9 us -> 10.7 us
    another operation x30 -> x0, other arithmetic: 172 us -> none  [on_device(): return jnp.linalg.cholesky(gram_matrix / row_total).T]
    psum x1 -> x0, waiting for transfers between devices: 143 us -> none  [on_device(): gram_matrix = lax.psum(local_gram, ('tm', 'chan'))]
    ppermute x1 -> x13, waiting for transfers between devices: 0.01 us -> 66.8 us  [the longest x12 64.9 us: swap(): return lax.ppermute(value, axis, [(i, i ^ bit) for i in range(count)])]
    all_to_all x1 -> x0, blocking collectives: 51 us -> none  [on_device(): lax.all_to_all(panel, 'chan', split_axis=0, concat_axis=1, tiled=True)]
    pallas_call x0 -> x2, Pallas kernels: none -> 49.8 us  [the longest x1 40.8 us: cholesky(): pl.pallas_call(functools.partial(cholesky_kernel, scale), out_shape=jax.S...]
    reduce_scatter x1 -> x0, waiting for transfers between devices: 34.2 us -> none  [on_device(): lax.psum_scatter(partial_value, 'chan', scatter_dimension=1, tiled=True)]
    ppermute x1 -> x13, starting transfers between devices: 1.29 us -> 27.6 us  [the longest x12 26.1 us: swap(): return lax.ppermute(value, axis, [(i, i ^ bit) for i in range(count)])]
    another operation x14 -> x0, matrix products: 22.9 us -> none  [on_device(): return jnp.linalg.cholesky(gram_matrix / row_total).T]
  transfers between devices with their start and end apart: 3 -> 13, of which waited for: 2 -> 13; matrix products, arithmetic and copies ran while one was open for 0% -> 0% of each run, Pallas kernels for 0% -> 0%
where the time goes in v1:
time: 164 us
  waiting for transfers between devices  66.8 us (41%)
  Pallas kernels  49.8 us (30%)
  starting transfers between devices  27.6 us (17%)
  local copies, waits for them, and re-layouts  10.7 us (7%)
  matrix products  5.16 us (3%)
  other arithmetic  3.54 us (2%)
    ppermute x12, waiting for transfers between devices, swap(): return lax.ppermute(value, axis, [(i, i ^ bit) for i in range(count)])  64.9 us
    pallas_call x1, Pallas kernels, cholesky(): pl.pallas_call(functools.partial(cholesky_kernel, scale), out_shape=jax.S...  40.8 us
    ppermute x12, starting transfers between devices, swap(): return lax.ppermute(value, axis, [(i, i ^ bit) for i in range(count)])  26.1 us
    pallas_call x1, Pallas kernels, gram_blocks(): pl.pallas_call(gram_kernel, out_shape=jax.ShapeDtypeStruct((blocks * BLOC...  9 us
    dot_general x1, matrix products, on_device(): jnp.dot(signals, onehot.astype(jnp.bfloat16), preferred_element_type=jnp....  5.16 us
    dynamic_slice x2, local copies, waits for them, and re-layouts, scatter_rows(): keep = lax.dynamic_index_in_dim(parts, mine, dim, keepdims=False)  3.87 us
    dynamic_slice x1, local copies, waits for them, and re-layouts, scatter_rows(): send = lax.dynamic_index_in_dim(parts, 1 - mine, dim, keepdims=False)  3.57 us
  transfers between devices with their start and end apart: 13, of which 13 were waited for; matrix products, arithmetic and copies ran while one was open for 0% of the time, Pallas kernels for 0%

profile of v1, /device:TPU:0, one launch (start us, length us, event | category | flops | bytes accessed | tf_op | source)
XLA Modules:
  0.0 163.8 jit_solution(10139709944514982717)
XLA Ops:
  0.0 5.2 %convolution_bitcast_fusion = f32[4096,128]{0,1:T(8,128)} fusion(bf16[4096,512]{1,0:T(8,128)(2,1)} %param.3, s32[512]{0:T(512)} %param.4), kind=kOutput, calls=%fused_computation | convolution fusion | flops 537067520 | bytes 6293504 | tf_op jit(solution)/shard_map/dot_general | solution.py:245
  5.2 3.0 %reshape.4 = f32[2,2,1024,128]{2,1,0,3:T(2,128)S(1)} reshape(f32[4096,128]{0,1:T(8,128)} %convolution_bitcast_fusion) | data formatting | bytes 4194304 | tf_op jit(solution)/shard_map/reshape | solution.py:40
  8.2 3.1 %constant_dynamic-slice_fusion.6 = (f32[2,1,1024,128]{2,1,0,3:T(1,128)S(1)}, f32[2,1,1024,128]{2,1,0,3:T(1,128)}) fusion(f32[2,2,1024,128]{2,1,0,3:T(2,128)S(1)} %reshape.4, s32[]{:T(128)S(6)} %select_n.178, s32[]{:T(128)S(6)} %select_n.179), kind=kLoop, calls=%fused_computation.35 | loop fusion | bytes 4194312 | tf_op jit(solution)/shard_map/jit(dynamic_index_in_dim)/dynamic_slice | solution.py:45
  11.3 3.6 %copy.5 = f32[2,1,1024,128]{3,2,0,1:T(8,128)} copy(f32[2,1,1024,128]{2,1,0,3:T(1,128)} %get-tuple-element.8) | data formatting | bytes 2097152 | tf_op jit(solution)/shard_map/jit(dynamic_index_in_dim)/dynamic_slice | solution.py:44
  16.1 1.9 %collective-permute-done = f32[2,1024,128]{2,1,0:T(8,128)} collective-permute-done((f32[2,1024,128]{2,1,0:T(8,128)}, f32[2,1024,128]{2,1,0:T(8,128)}, u32[]{:S(2)}, u32[]{:S(2)}) %collective-permute-start) | collective-permute-done | bytes 1048608 | tf_op jit(solution)/shard_map/ppermute | solution.py:22
  18.0 1.4 bitcast_add_fusion
  19.4 2.9 %collective-permute-start.1 = (f32[1024,128]{1,0:T(8,128)S(1)}, f32[1024,128]{1,0:T(8,128)S(1)}, u32[]{:S(2)}, u32[]{:S(2)}) collective-permute-start(f32[1024,128]{1,0:T(8,128)S(1)} %dynamic-slice_bitcast_fusion), channel_id=1, source_target_pairs={{0,2},{1,3},{2,0},{3,1},{4,6},{5,7},{6,4},{7,5},{8,10},{9,11},{10,... | collective-permute-start | bytes 1572872 | tf_op jit(solution)/shard_map/ppermute | solution.py:22
  22.3 12.2 %collective-permute-done.1 = f32[1024,128]{1,0:T(8,128)S(1)} collective-permute-done((f32[1024,128]{1,0:T(8,128)S(1)}, f32[1024,128]{1,0:T(8,128)S(1)}, u32[]{:S(2)}, u32[]{:S(2)}) %collective-permute-start.1) | collective-permute-done | bytes 524320 | tf_op jit(solution)/shard_map/ppermute | solution.py:22
  34.6 1.5 collective-permute-start.2
  36.1 1.9 %collective-permute-done.2.after_ref = f32[512,128]{1,0:T(8,128)S(1)} collective-permute-done((f32[512,128]{1,0:T(8,128)S(1)}, f32[512,128]{1,0:T(8,128)S(1)}, u32[]{:S(2)}, u32[]{:S(2)}) %collective-permute-start.2) | collective-permute-done | bytes 262176 | tf_op jit(solution)/shard_map/ppermute | solution.py:74
  38.1 9.0 %shard_map.37 = f32[4608,128]{1,0:T(8,128)S(1)} custom-call(s32[8]{0:T(128)S(1)} %copy-done, f32[1024,128]{1,0:T(8,128)S(1)} %bitcast_add_fusion.1.rows_ref, f32[512,128]{1,0:T(8,128)S(1)} %collective-permute-done.2.after_ref), custom_call_target="tpu_custom_call" | custom-call | tf_op jit(solution)/shard_map/pallas_call | solution.py:125
  47.2 4.4 %collective-permute-start.3 = (f32[2304,128]{1,0:T(8,128)S(1)}, f32[2304,128]{1,0:T(8,128)}, u32[]{:S(2)}, u32[]{:S(2)}) collective-permute-start(f32[2304,128]{1,0:T(8,128)S(1)} %constant_dynamic-slice_fusion.4), channel_id=1, source_target_pairs={{0,1},{1,0},{2,3},{3,2},{4,5},{5,4},{6,7},{7,6},{8,9},{9,8},{10,11... | collective-permute-start | bytes 3538952 | tf_op jit(solution)/shard_map/ppermute | solution.py:22
  51.6 2.6 %collective-permute-done.3 = f32[2304,128]{1,0:T(8,128)} collective-permute-done((f32[2304,128]{1,0:T(8,128)S(1)}, f32[2304,128]{1,0:T(8,128)}, u32[]{:S(2)}, u32[]{:S(2)}) %collective-permute-start.3) | collective-permute-done | bytes 1179680 | tf_op jit(solution)/shard_map/ppermute | solution.py:22
  54.2 1.4 dynamic-slice_add_fusion
  55.7 1.9 %collective-permute-start.4 = (f32[1152,128]{1,0:T(8,128)S(1)}, f32[1152,128]{1,0:T(8,128)S(1)}, u32[]{:S(2)}, u32[]{:S(2)}) collective-permute-start(f32[1152,128]{1,0:T(8,128)S(1)} %constant_dynamic-slice_fusion.3), channel_id=1, source_target_pairs={{0,2},{1,3},{2,0},{3,1},{4,6},{5,7},{6,4},{7,5},{8,10},{9,11},{10,... | collective-permute-start | bytes 1769480 | tf_op jit(solution)/shard_map/ppermute | solution.py:22
  57.6 13.9 %collective-permute-done.4 = f32[1152,128]{1,0:T(8,128)S(1)} collective-permute-done((f32[1152,128]{1,0:T(8,128)S(1)}, f32[1152,128]{1,0:T(8,128)S(1)}, u32[]{:S(2)}, u32[]{:S(2)}) %collective-permute-start.4) | collective-permute-done | bytes 589856 | tf_op jit(solution)/shard_map/ppermute | solution.py:22
  71.5 2.5 %collective-permute-start.5 = (f32[576,128]{1,0:T(8,128)S(1)}, f32[576,128]{1,0:T(8,128)S(1)}, u32[]{:S(2)}, u32[]{:S(2)}) collective-permute-start(f32[576,128]{1,0:T(8,128)S(1)} %constant_dynamic-slice_fusion.2), channel_id=1, source_target_pairs={{0,4},{4,0},{8,12},{12,8},{16,20},{20,16},{24,28},{28,24},{1,5},{5... | collective-permute-start | bytes 884744 | tf_op jit(solution)/shard_map/ppermute | solution.py:22
  74.0 7.0 %collective-permute-done.5 = f32[576,128]{1,0:T(8,128)S(1)} collective-permute-done((f32[576,128]{1,0:T(8,128)S(1)}, f32[576,128]{1,0:T(8,128)S(1)}, u32[]{:S(2)}, u32[]{:S(2)}) %collective-permute-start.5) | collective-permute-done | bytes 294944 | tf_op jit(solution)/shard_map/ppermute | solution.py:22
  81.1 1.6 %collective-permute-start.6 = (f32[288,128]{1,0:T(8,128)S(1)}, f32[288,128]{1,0:T(8,128)S(1)}, u32[]{:S(2)}, u32[]{:S(2)}) collective-permute-start(f32[288,128]{1,0:T(8,128)S(1)} %constant_dynamic-slice_fusion.1), channel_id=1, source_target_pairs={{0,8},{4,12},{8,0},{12,4},{16,24},{20,28},{24,16},{28,20},{1,9},{5... | collective-permute-start | bytes 442376 | tf_op jit(solution)/shard_map/ppermute | solution.py:22
  82.7 3.6 %collective-permute-done.6 = f32[288,128]{1,0:T(8,128)S(1)} collective-permute-done((f32[288,128]{1,0:T(8,128)S(1)}, f32[288,128]{1,0:T(8,128)S(1)}, u32[]{:S(2)}, u32[]{:S(2)}) %collective-permute-start.6) | collective-permute-done | bytes 147488 | tf_op jit(solution)/shard_map/ppermute | solution.py:22
  86.3 2.7 %collective-permute-start.7 = (f32[144,128]{1,0:T(8,128)S(1)}, f32[144,128]{1,0:T(8,128)S(1)}, u32[]{:S(2)}, u32[]{:S(2)}) collective-permute-start(f32[144,128]{1,0:T(8,128)S(1)} %constant_dynamic-slice_fusion), channel_id=1, source_target_pairs={{0,16},{4,20},{8,24},{12,28},{16,0},{20,4},{24,8},{28,12},{1,17},{... | collective-permute-start | bytes 221192 | tf_op jit(solution)/shard_map/ppermute | solution.py:22
  89.0 2.7 %collective-permute-done.7 = f32[144,128]{1,0:T(8,128)S(1)} collective-permute-done((f32[144,128]{1,0:T(8,128)S(1)}, f32[144,128]{1,0:T(8,128)S(1)}, u32[]{:S(2)}, u32[]{:S(2)}) %collective-permute-start.7) | collective-permute-done | bytes 73760 | tf_op jit(solution)/shard_map/ppermute | solution.py:22
  91.6 2.8 %collective-permute-start.8 = (f32[144,128]{1,0:T(8,128)S(1)}, f32[144,128]{1,0:T(8,128)S(1)}, u32[]{:S(2)}, u32[]{:S(2)}) collective-permute-start(f32[144,128]{1,0:T(8,128)S(1)} %dynamic-slice_add_fusion.4), channel_id=1, source_target_pairs={{0,16},{4,20},{8,24},{12,28},{16,0},{20,4},{24,8},{28,12},{1,17},{... | collective-permute-start | bytes 221192 | tf_op jit(solution)/shard_map/ppermute | solution.py:22
  94.4 2.6 %collective-permute-done.8 = f32[144,128]{1,0:T(8,128)S(1)} collective-permute-done((f32[144,128]{1,0:T(8,128)S(1)}, f32[144,128]{1,0:T(8,128)S(1)}, u32[]{:S(2)}, u32[]{:S(2)}) %collective-permute-start.8) | collective-permute-done | bytes 73760 | tf_op jit(solution)/shard_map/ppermute | solution.py:22
  97.1 2.1 %collective-permute-start.9 = (f32[288,128]{1,0:T(8,128)S(1)}, f32[288,128]{1,0:T(8,128)S(1)}, u32[]{:S(2)}, u32[]{:S(2)}) collective-permute-start(f32[288,128]{1,0:T(8,128)S(1)} %pad_maximum_fusion.4), channel_id=1, source_target_pairs={{0,8},{4,12},{8,0},{12,4},{16,24},{20,28},{24,16},{28,20},{1,9},{5... | collective-permute-start | bytes 442376 | tf_op jit(solution)/shard_map/ppermute | solution.py:22
  99.1 3.1 %collective-permute-done.9 = f32[288,128]{1,0:T(8,128)S(1)} collective-permute-done((f32[288,128]{1,0:T(8,128)S(1)}, f32[288,128]{1,0:T(8,128)S(1)}, u32[]{:S(2)}, u32[]{:S(2)}) %collective-permute-start.9) | collective-permute-done | bytes 147488 | tf_op jit(solution)/shard_map/ppermute | solution.py:22
  102.3 2.2 %collective-permute-start.10 = (f32[576,128]{1,0:T(8,128)S(1)}, f32[576,128]{1,0:T(8,128)S(1)}, u32[]{:S(2)}, u32[]{:S(2)}) collective-permute-start(f32[576,128]{1,0:T(8,128)S(1)} %pad_maximum_fusion.3), channel_id=1, source_target_pairs={{0,4},{4,0},{8,12},{12,8},{16,20},{20,16},{24,28},{28,24},{1,5},{5... | collective-permute-start | bytes 884744 | tf_op jit(solution)/shard_map/ppermute | solution.py:22
  104.5 4.7 %collective-permute-done.10 = f32[576,128]{1,0:T(8,128)S(1)} collective-permute-done((f32[576,128]{1,0:T(8,128)S(1)}, f32[576,128]{1,0:T(8,128)S(1)}, u32[]{:S(2)}, u32[]{:S(2)}) %collective-permute-start.10) | collective-permute-done | bytes 294944 | tf_op jit(solution)/shard_map/ppermute | solution.py:22
  109.3 2.5 %collective-permute-start.11 = (f32[1152,128]{1,0:T(8,128)S(1)}, f32[1152,128]{1,0:T(8,128)S(1)}, u32[]{:S(2)}, u32[]{:S(2)}) collective-permute-start(f32[1152,128]{1,0:T(8,128)S(1)} %pad_maximum_fusion.2), channel_id=1, source_target_pairs={{0,2},{1,3},{2,0},{3,1},{4,6},{5,7},{6,4},{7,5},{8,10},{9,11},{10,... | collective-permute-start | bytes 1769480 | tf_op jit(solution)/shard_map/ppermute | solution.py:22
  111.8 7.9 %collective-permute-done.11 = f32[1152,128]{1,0:T(8,128)S(1)} collective-permute-done((f32[1152,128]{1,0:T(8,128)S(1)}, f32[1152,128]{1,0:T(8,128)S(1)}, u32[]{:S(2)}, u32[]{:S(2)}) %collective-permute-start.11) | collective-permute-done | bytes 589856 | tf_op jit(solution)/shard_map/ppermute | solution.py:22
  119.9 2.8 %collective-permute-done.12 = f32[2304,128]{1,0:T(8,128)S(1)} collective-permute-done((f32[2304,128]{1,0:T(8,128)S(1)}, f32[2304,128]{1,0:T(8,128)S(1)}, u32[]{:S(2)}, u32[]{:S(2)}) %collective-permute-start.12) | collective-permute-done | bytes 1179680 | tf_op jit(solution)/shard_map/ppermute | solution.py:22
  123.1 40.8 %shard_map.38 = f32[1024,1024]{1,0:T(8,128)} custom-call(f32[4608,128]{1,0:T(8,128)S(1)} %pad_maximum_fusion.blocks_ref), custom_call_target="tpu_custom_call" | custom-call | tf_op jit(solution)/shard_map/pallas_call | solution.py:232
  (27 shorter events, 2.3 us)
Async XLA Ops:
  14.9 3.1 %collective-permute-start = (f32[2,1024,128]{2,1,0:T(8,128)}, f32[2,1024,128]{2,1,0:T(8,128)}, u32[]{:S(2)}, u32[]{:S(2)}) collective-permute-start(f32[2,1024,128]{2,1,0:T(8,128)} %bitcast.2), channel_id=1, source_target_pairs={{0,1},{1,0},{2,3},{3,2},{4,5},{5,4},{6,7},{7,6},{8,9},{9,8},{10,11... | collective-permute-start | bytes 3145736 | tf_op jit(solution)/shard_map/ppermute | solution.py:22
  19.4 18.7 %copy-start = (s32[8]{0:T(128)S(1)}, s32[8]{0:T(128)}, u32[]{:S(2)}) copy-start(s32[8]{0:T(128)} %lags_ref.1) | copy-start | bytes 100
  19.4 15.2 %collective-permute-start.1 = (f32[1024,128]{1,0:T(8,128)S(1)}, f32[1024,128]{1,0:T(8,128)S(1)}, u32[]{:S(2)}, u32[]{:S(2)}) collective-permute-start(f32[1024,128]{1,0:T(8,128)S(1)} %dynamic-slice_bitcast_fusion), channel_id=1, source_target_pairs={{0,2},{1,3},{2,0},{3,1},{4,6},{5,7},{6,4},{7,5},{8,10},{9,11},{10,... | collective-permute-start | bytes 1572872 | tf_op jit(solution)/shard_map/ppermute | solution.py:22
  34.6 3.4 %collective-permute-start.2 = (f32[512,128]{1,0:T(8,128)S(1)}, f32[512,128]{1,0:T(8,128)S(1)}, u32[]{:S(2)}, u32[]{:S(2)}) collective-permute-start(f32[512,128]{1,0:T(8,128)S(1)} %slice.4), channel_id=1, source_target_pairs={{1,0},{2,1},{3,2},{4,3},{5,4},{6,5},{7,6},{8,7},{9,8},{10,9},{11,1... | collective-permute-start | bytes 786440 | tf_op jit(solution)/shard_map/ppermute | solution.py:74
  47.2 7.1 %collective-permute-start.3 = (f32[2304,128]{1,0:T(8,128)S(1)}, f32[2304,128]{1,0:T(8,128)}, u32[]{:S(2)}, u32[]{:S(2)}) collective-permute-start(f32[2304,128]{1,0:T(8,128)S(1)} %constant_dynamic-slice_fusion.4), channel_id=1, source_target_pairs={{0,1},{1,0},{2,3},{3,2},{4,5},{5,4},{6,7},{7,6},{8,9},{9,8},{10,11... | collective-permute-start | bytes 3538952 | tf_op jit(solution)/shard_map/ppermute | solution.py:22
  55.7 15.8 %collective-permute-start.4 = (f32[1152,128]{1,0:T(8,128)S(1)}, f32[1152,128]{1,0:T(8,128)S(1)}, u32[]{:S(2)}, u32[]{:S(2)}) collective-permute-start(f32[1152,128]{1,0:T(8,128)S(1)} %constant_dynamic-slice_fusion.3), channel_id=1, source_target_pairs={{0,2},{1,3},{2,0},{3,1},{4,6},{5,7},{6,4},{7,5},{8,10},{9,11},{10,... | collective-permute-start | bytes 1769480 | tf_op jit(solution)/shard_map/ppermute | solution.py:22
  71.5 9.5 %collective-permute-start.5 = (f32[576,128]{1,0:T(8,128)S(1)}, f32[576,128]{1,0:T(8,128)S(1)}, u32[]{:S(2)}, u32[]{:S(2)}) collective-permute-start(f32[576,128]{1,0:T(8,128)S(1)} %constant_dynamic-slice_fusion.2), channel_id=1, source_target_pairs={{0,4},{4,0},{8,12},{12,8},{16,20},{20,16},{24,28},{28,24},{1,5},{5... | collective-permute-start | bytes 884744 | tf_op jit(solution)/shard_map/ppermute | solution.py:22
  81.1 5.2 %collective-permute-start.6 = (f32[288,128]{1,0:T(8,128)S(1)}, f32[288,128]{1,0:T(8,128)S(1)}, u32[]{:S(2)}, u32[]{:S(2)}) collective-permute-start(f32[288,128]{1,0:T(8,128)S(1)} %constant_dynamic-slice_fusion.1), channel_id=1, source_target_pairs={{0,8},{4,12},{8,0},{12,4},{16,24},{20,28},{24,16},{28,20},{1,9},{5... | collective-permute-start | bytes 442376 | tf_op jit(solution)/shard_map/ppermute | solution.py:22
  86.3 5.3 %collective-permute-start.7 = (f32[144,128]{1,0:T(8,128)S(1)}, f32[144,128]{1,0:T(8,128)S(1)}, u32[]{:S(2)}, u32[]{:S(2)}) collective-permute-start(f32[144,128]{1,0:T(8,128)S(1)} %constant_dynamic-slice_fusion), channel_id=1, source_target_pairs={{0,16},{4,20},{8,24},{12,28},{16,0},{20,4},{24,8},{28,12},{1,17},{... | collective-permute-start | bytes 221192 | tf_op jit(solution)/shard_map/ppermute | solution.py:22
  91.6 5.4 %collective-permute-start.8 = (f32[144,128]{1,0:T(8,128)S(1)}, f32[144,128]{1,0:T(8,128)S(1)}, u32[]{:S(2)}, u32[]{:S(2)}) collective-permute-start(f32[144,128]{1,0:T(8,128)S(1)} %dynamic-slice_add_fusion.4), channel_id=1, source_target_pairs={{0,16},{4,20},{8,24},{12,28},{16,0},{20,4},{24,8},{28,12},{1,17},{... | collective-permute-start | bytes 221192 | tf_op jit(solution)/shard_map/ppermute | solution.py:22
  97.1 5.2 %collective-permute-start.9 = (f32[288,128]{1,0:T(8,128)S(1)}, f32[288,128]{1,0:T(8,128)S(1)}, u32[]{:S(2)}, u32[]{:S(2)}) collective-permute-start(f32[288,128]{1,0:T(8,128)S(1)} %pad_maximum_fusion.4), channel_id=1, source_target_pairs={{0,8},{4,12},{8,0},{12,4},{16,24},{20,28},{24,16},{28,20},{1,9},{5... | collective-permute-start | bytes 442376 | tf_op jit(solution)/shard_map/ppermute | solution.py:22
  102.3 6.9 %collective-permute-start.10 = (f32[576,128]{1,0:T(8,128)S(1)}, f32[576,128]{1,0:T(8,128)S(1)}, u32[]{:S(2)}, u32[]{:S(2)}) collective-permute-start(f32[576,128]{1,0:T(8,128)S(1)} %pad_maximum_fusion.3), channel_id=1, source_target_pairs={{0,4},{4,0},{8,12},{12,8},{16,20},{20,16},{24,28},{28,24},{1,5},{5... | collective-permute-start | bytes 884744 | tf_op jit(solution)/shard_map/ppermute | solution.py:22
  109.3 10.4 %collective-permute-start.11 = (f32[1152,128]{1,0:T(8,128)S(1)}, f32[1152,128]{1,0:T(8,128)S(1)}, u32[]{:S(2)}, u32[]{:S(2)}) collective-permute-start(f32[1152,128]{1,0:T(8,128)S(1)} %pad_maximum_fusion.2), channel_id=1, source_target_pairs={{0,2},{1,3},{2,0},{3,1},{4,6},{5,7},{6,4},{7,5},{8,10},{9,11},{10,... | collective-permute-start | bytes 1769480 | tf_op jit(solution)/shard_map/ppermute | solution.py:22
  119.8 2.9 %collective-permute-start.12 = (f32[2304,128]{1,0:T(8,128)S(1)}, f32[2304,128]{1,0:T(8,128)S(1)}, u32[]{:S(2)}, u32[]{:S(2)}) collective-permute-start(f32[2304,128]{1,0:T(8,128)S(1)} %pad_maximum_fusion.1), channel_id=1, source_target_pairs={{0,1},{1,0},{2,3},{3,2},{4,5},{5,4},{6,7},{7,6},{8,9},{9,8},{10,11... | collective-permute-start | bytes 3538952 | tf_op jit(solution)/shard_map/ppermute | solution.py:22

commit v2 on v1

v2 whole, which is shorter than its diff:
```python
import functools
import math

import jax
import jax.numpy as jnp
from jax import lax
from jax.experimental import pallas as pl
from jax.experimental.pallas import tpu as pltpu
from jax.sharding import PartitionSpec as P

NODES = 128
CH = 2048
MAXLAG = 512
BLOCK = 128
GROUP = 8
HIGHEST = lax.Precision.HIGHEST
CONTRACT_ROWS = (((0,), (0,)), ((), ()))


def swap(value, axis, bit):
    count = lax.axis_size(axis)
    return lax.ppermute(value, axis, [(i, i ^ bit) for i in range(count)])


def bits_of(axis):
    count = lax.axis_size(axis)
    return [1 << i for i in range(count.bit_length() - 1)]


def halve(value, axis, bit):
    half = value.shape[0] // 2
    mine = (lax.axis_index(axis) // bit) % 2
    send = lax.dynamic_slice_in_dim(value, (1 - mine) * half, half, 0)
    keep = lax.dynamic_slice_in_dim(value, mine * half, half, 0)
    return keep + swap(send, axis, bit)


def double(value, axis, bit):
    mine = (lax.axis_index(axis) // bit) % 2
    other = swap(value, axis, bit)
    low = jnp.where(mine == 0, value, other)
    high = jnp.where(mine == 0, other, value)
    return jnp.concatenate([low, high], axis=0)


def sum_over_time_blocks(value):
    for bit in bits_of("tm"):
        value = halve(value, "tm", bit)
    for bit in bits_of("tm")[::-1]:
        value = double(value, "tm", bit)
    return value


def first_rows_of_next(rows):
    count = lax.axis_size("tm")
    return lax.ppermute(rows, "tm", [(i, i - 1) for i in range(1, count)])


def project_kernel(half_ref, nodes_ref, signals_ref, out_ref, onehot_ref):
    @pl.when(pl.program_id(0) == 0)
    def _():
        node = lax.broadcasted_iota(jnp.int32, onehot_ref.shape, 0)
        scale = 1.0 / math.sqrt(CH // NODES)
        onehot_ref[...] = jnp.where(node == nodes_ref[...], scale, 0.0).astype(jnp.bfloat16)

    out_ref[...] = lax.dot_general(
        signals_ref[...], onehot_ref[...], (((1,), (1,)), ((), ())), preferred_element_type=jnp.float32
    )


def project(signals, channel_node, first, rows, half):
    channels = signals.shape[1]
    step = min(512, rows // 2)
    steps = rows // 2 // step
    grid_spec = pltpu.PrefetchScalarGridSpec(
        num_scalar_prefetch=1,
        grid=(steps,),
        in_specs=[
            pl.BlockSpec((1, channels), lambda i, half: (0, 0)),
            pl.BlockSpec((step, channels), lambda i, half: (first // step + half[0] * steps + i, 0)),
        ],
        out_specs=pl.BlockSpec((step, NODES), lambda i, half: (i, 0)),
        scratch_shapes=[pltpu.VMEM((NODES, channels), jnp.bfloat16)],
    )
    return pl.pallas_call(
        project_kernel,
        out_shape=jax.ShapeDtypeStruct((rows // 2, NODES), jnp.float32),
        grid_spec=grid_spec,
        cost_estimate=pl.CostEstimate(flops=rows * channels * NODES, bytes_accessed=rows * (channels + 2 * NODES), transcendentals=0),
    )(half, channel_node.reshape(1, channels), signals)


def gram_kernel(first, last, half_ref, lags_ref, *refs):
    refs = list(refs)
    mine_ref, other_ref = refs.pop(0), refs.pop(0)
    sum_in_ref, tail_in_ref = (None, None) if first else (refs.pop(0), refs.pop(0))
    after_ref = refs.pop(0) if last else None
    out_ref = refs.pop(0)
    tail_out_ref = None if last else refs.pop(0)
    ext_ref, high_ref, low_ref, sum_ref = refs
    half = mine_ref.shape[0]
    lead = 0 if first else MAXLAG
    lag_count = lags_ref.shape[0]
    step_rows = high_ref.shape[0]
    own = pl.multiple_of(lead + half_ref[0] * half, math.gcd(lead, half))
    others = pl.multiple_of(lead + (1 - half_ref[0]) * half, math.gcd(lead, half))
    ext_ref[pl.ds(own, half), :] = mine_ref[...]
    ext_ref[pl.ds(others, half), :] = other_ref[...]
    end = lead + 2 * half
    if not first:
        ext_ref[:lead, :] = tail_in_ref[...]
    if last:
        ext_ref[end:, :] = after_ref[...]
    else:
        tail_out_ref[...] = ext_ref[end - MAXLAG : end, :]
    steps = (end if last else end - MAXLAG) // step_rows
    sum_ref[...] = jnp.zeros_like(sum_ref) if first else sum_in_ref[...]
    part = 128

    def step(i, _):
        start = i * step_rows
        for lag in range(lag_count):
            for row in range(0, step_rows, part):
                value = ext_ref[pl.ds(start + row + lags_ref[lag], part), :]
                high = value.astype(jnp.bfloat16)
                high_ref[row : row + part, lag * NODES : (lag + 1) * NODES] = high
                low_ref[row : row + part, lag * NODES : (lag + 1) * NODES] = (
                    value - high.astype(jnp.float32)
                ).astype(jnp.bfloat16)

        def product(left, right):
            return lax.dot_general(left, right, CONTRACT_ROWS, preferred_element_type=jnp.float32)

        left = slice(0, 2 * NODES)
        total = product(high_ref[:, left], high_ref[...])
        total = total + product(high_ref[:, left], low_ref[...])
        total = total + product(low_ref[:, left], high_ref[...])
        sum_ref[...] += total
        return 0

    lax.fori_loop(0, steps, step, 0)
    if last:
        far = lag_count - 2
        for j in range(far):
            out_ref[j * NODES : (j + 1) * NODES, :] = sum_ref[:NODES, j * NODES : (j + 1) * NODES]
            place = (far + j) * NODES
            out_ref[place : place + NODES, :] = sum_ref[NODES:, (j + 1) * NODES : (j + 2) * NODES]
        which = half_ref[1]
        row = pl.multiple_of(which * NODES, NODES)
        column = pl.multiple_of((far + which) * NODES, NODES)
        out_ref[2 * far * NODES :, :] = sum_ref[pl.ds(row, NODES), pl.ds(column, NODES)]
    else:
        out_ref[...] = sum_ref[...]


def gram_part(half, lags, mine, other, carried, after):
    first, last = carried is None, after is not None
    count = lags.shape[0]
    blocks = 2 * (count - 2) + 1
    operands = [half, lags, mine, other]
    if not first:
        operands += list(carried)
    if last:
        operands.append(after)
    if last:
        out_shape = jax.ShapeDtypeStruct((blocks * NODES, NODES), jnp.float32)
    else:
        out_shape = (
            jax.ShapeDtypeStruct((2 * NODES, count * NODES), jnp.float32),
            jax.ShapeDtypeStruct((MAXLAG, NODES), jnp.float32),
        )
    rows = 2 * mine.shape[0] + (0 if first else MAXLAG) + (MAXLAG if last else 0)
    vmem = pl.BlockSpec(memory_space=pltpu.VMEM)
    smem = pl.BlockSpec(memory_space=pltpu.SMEM)
    step_rows = 512
    return pl.pallas_call(
        functools.partial(gram_kernel, first, last),
        out_shape=out_shape,
        in_specs=[smem, smem] + [vmem] * (len(operands) - 2),
        out_specs=vmem if last else (vmem, vmem),
        scratch_shapes=[
            pltpu.VMEM((rows, NODES), jnp.float32),
            pltpu.VMEM((step_rows, count * NODES), jnp.bfloat16),
            pltpu.VMEM((step_rows, count * NODES), jnp.bfloat16),
            pltpu.VMEM((2 * NODES, count * NODES), jnp.float32),
        ],
        compiler_params=pltpu.CompilerParams(vmem_limit_bytes=40 << 20),
        cost_estimate=pl.CostEstimate(flops=rows * NODES * NODES * count * 12, bytes_accessed=rows * NODES * 4, transcendentals=0),
    )(*operands)


def row_of(value, index):
    return jnp.broadcast_to(value[index : index + 1, :], value.shape)


def column_of(value, index):
    return jnp.broadcast_to(value[:, index : index + 1], value.shape)


def factor_block(block):
    count = len(block)
    sub = lax.broadcasted_iota(jnp.int32, (GROUP, BLOCK), 0)
    lane = lax.broadcasted_iota(jnp.int32, (GROUP, BLOCK), 1)
    block = list(block)
    inverse = [jnp.where(lane == sub + GROUP * s, 1.0, 0.0) for s in range(count)]
    for g in range(count):
        columns = [column_of(block[g], GROUP * g + m) for m in range(GROUP)]
        top, top_inverse = block[g], inverse[g]
        scale, factors, rows, inverse_rows = [], {}, [], []
        for m in range(GROUP):
            scale.append(lax.rsqrt(row_of(columns[m], m)))
            rows.append(row_of(top, m) * scale[m])
            inverse_rows.append(row_of(top_inverse, m) * scale[m])
            left = columns[m] * scale[m]
            for n in range(m + 1, GROUP):
                factors[m, n] = row_of(left, n)
                columns[n] = columns[n] - left * factors[m, n]
            below = jnp.where(sub > m, left, 0.0)
            top = jnp.where(sub == m, rows[m], top - below * rows[m])
            top_inverse = jnp.where(sub == m, inverse_rows[m], top_inverse - below * inverse_rows[m])
        block[g] = jnp.where(lane >= sub + GROUP * g, top, 0.0)
        inverse[g] = top_inverse
        for s in range(g + 1, count):
            columns = [column_of(block[s], GROUP * g + m) for m in range(GROUP)]
            for m in range(GROUP):
                left = columns[m] * scale[m]
                for n in range(m + 1, GROUP):
                    columns[n] = columns[n] - left * factors[m, n]
                block[s] = block[s] - left * rows[m]
                inverse[s] = inverse[s] - left * inverse_rows[m]
    return block, inverse


def arrange(half_ref, mine_ref, other_ref, natural_ref, ordered_ref):
    chan_count = 4
    lag_count = 2 * chan_count
    far = lag_count // 2
    width = NODES // chan_count
    each = (2 * far + 1) * NODES

    def place(ref, low):
        for high in range(2):
            chan = 2 * high + low
            pairs = [(2 * chan + i, (2 * chan + i + d) % lag_count) for i in range(2) for d in range(far)]
            odd = 2 * chan // far
            pairs.append((2 * chan + odd, (2 * chan + odd + far) % lag_count))
            for index, (left, right) in enumerate(pairs):
                start = high * each + index * NODES
                block = ref[start : start + NODES, :]
                natural_ref[left * NODES : (left + 1) * NODES, right * NODES : (right + 1) * NODES] = block
                if left != right:
                    natural_ref[right * NODES : (right + 1) * NODES, left * NODES : (left + 1) * NODES] = block.T

    for low in range(2):

        @pl.when(half_ref[0] == low)
        def _():
            place(mine_ref, low)
            place(other_ref, 1 - low)

    lane_part = lax.broadcasted_iota(jnp.int32, (width, NODES), 1) // width

    def rows_of_lag(lag, _):
        for group in range(chan_count):
            source = pl.ds(pl.multiple_of(lag * NODES + group * width, width), width)
            target = pl.ds(pl.multiple_of(group * lag_count * width + lag * width, width), width)
            for half in range(2):
                parts = [natural_ref[source, (4 * half + i) * NODES : (4 * half + i + 1) * NODES] for i in range(4)]
                for other in range(group, chan_count):
                    block = None
                    for i in range(4):
                        shift = (i - other) % 4 * width
                        part = pltpu.roll(parts[i], shift, 1) if shift else parts[i]
                        block = part if block is None else jnp.where(lane_part == i, part, block)
                    column = (2 * other + half) * BLOCK
                    ordered_ref[target, column : column + BLOCK] = block
        return 0

    lax.fori_loop(0, lag_count, rows_of_lag, 0)


def cholesky_kernel(scale, half_ref, mine_ref, other_ref, out_ref, natural_ref, ordered_ref, panel_ref, inverse_ref):
    arrange(half_ref, mine_ref, other_ref, natural_ref, ordered_ref)
    size = out_ref.shape[0]
    count = size // BLOCK
    out_ref[...] = jnp.zeros_like(out_ref)

    def step(k, _):
        start = pl.multiple_of(k * BLOCK, BLOCK)
        for kk in range(count):

            @pl.when(k == kk)
            def _():
                mine = slice(kk * BLOCK, (kk + 1) * BLOCK)
                panel = ordered_ref[mine, kk * BLOCK :] * scale
                if kk:
                    panel = panel - lax.dot_general(
                        out_ref[: kk * BLOCK, mine],
                        out_ref[: kk * BLOCK, kk * BLOCK :],
                        CONTRACT_ROWS,
                        precision=HIGHEST,
                        preferred_element_type=jnp.float32,
                    )
                panel_ref[:, kk * BLOCK :] = panel

        block = [panel_ref[GROUP * s : GROUP * (s + 1), pl.ds(start, BLOCK)] for s in range(BLOCK // GROUP)]
        block, inverse = factor_block(block)
        for s in range(BLOCK // GROUP):
            out_ref[pl.ds(pl.multiple_of(start + GROUP * s, GROUP), GROUP), pl.ds(start, BLOCK)] = block[s]
            inverse_ref[GROUP * s : GROUP * (s + 1), :] = inverse[s]
        for kk in range(count - 1):

            @pl.when(k == kk)
            def _():
                out_ref[kk * BLOCK : (kk + 1) * BLOCK, (kk + 1) * BLOCK :] = jnp.dot(
                    inverse_ref[...],
                    panel_ref[:, (kk + 1) * BLOCK :],
                    precision=HIGHEST,
                    preferred_element_type=jnp.float32,
                )

        return 0

    lax.fori_loop(0, count, step, 0)


def cholesky(half, mine, other, size, scale):
    vmem = pl.BlockSpec(memory_space=pltpu.VMEM)
    return pl.pallas_call(
        functools.partial(cholesky_kernel, scale),
        out_shape=jax.ShapeDtypeStruct((size, size), jnp.float32),
        in_specs=[pl.BlockSpec(memory_space=pltpu.SMEM), vmem, vmem],
        out_specs=vmem,
        scratch_shapes=[
            pltpu.VMEM((size, size), jnp.float32),
            pltpu.VMEM((size, size), jnp.float32),
            pltpu.VMEM((BLOCK, size), jnp.float32),
            pltpu.VMEM((BLOCK, BLOCK), jnp.float32),
        ],
        compiler_params=pltpu.CompilerParams(vmem_limit_bytes=48 << 20),
    )(half, mine, other)


CHUNKS = 2


def on_device(signals, channel_node, lag_offsets):
    rows = signals.shape[0]
    lag_count = lag_offsets.shape[0]
    chan = lax.axis_index("chan")
    half = jnp.stack([chan % 2, 4 * chan // lag_count])
    span = lag_count // 2 + 2
    lags = lag_offsets[(2 * chan + jnp.arange(span, dtype=jnp.int32)) % lag_count]
    size = rows // CHUNKS
    carried = after = None
    for index in range(CHUNKS):
        first, last = index == 0, index == CHUNKS - 1
        send = project(signals, channel_node, index * size, size, 1 - half)
        received = swap(send, "chan", 1)
        keep = project(signals, channel_node, index * size, size, half)
        value = keep + received
        value = value + swap(value, "chan", 2)
        other = swap(value, "chan", 1)
        if first:
            head = jnp.where(half[0] == 0, value[:MAXLAG], other[:MAXLAG])
            after = first_rows_of_next(head)
        carried = gram_part(half, lags, value, other, carried, after if last else None)
    blocks = sum_over_time_blocks(carried)
    blocks = double(blocks, "chan", 2)
    other = swap(blocks, "chan", 1)
    return cholesky(half, blocks, other, lag_count * NODES, 1.0 / (rows * lax.axis_size("tm")))


def solution(mesh):
    return jax.shard_map(
        on_device, mesh=mesh, in_specs=(P("tm", "chan"), P("chan"), P()), out_specs=P(), check_vma=False
    )
```

time: 164 us -> 150 us (0.915)
  Pallas kernels: 49.8 us -> 65.6 us
  local copies, waits for them, and re-layouts: 10.7 us -> 0.71 us
  waiting for transfers between devices: 66.8 us -> 58.7 us
  starting transfers between devices: 27.6 us -> 20.8 us
  matrix products: 5.16 us -> 0 us
    pallas_call x1 -> x6, Pallas kernels: 9 us -> 21.2 us  [the longest x4 12.3 us: project(): pl.pallas_call(project_kernel, out_shape=jax.ShapeDtypeStruct((rows // 2,...]
    ppermute x12 -> x14, waiting for transfers between devices: 64.9 us -> 53.7 us  [swap(): return lax.ppermute(value, axis, [(i, i ^ bit) for i in range(count)])]
    dynamic_slice x3 -> x0, local copies, waits for them, and re-layouts: 7.44 us -> none  [the longest x2 3.87 us: scatter_rows(): keep = lax.dynamic_index_in_dim(parts, mine, dim, keepdims=False)]
    ppermute x12 -> x14, starting transfers between devices: 26.1 us -> 19.6 us  [swap(): return lax.ppermute(value, axis, [(i, i ^ bit) for i in range(count)])]
    dot_general x1 -> x0, matrix products: 5.16 us -> none  [on_device(): jnp.dot(signals, onehot.astype(jnp.bfloat16), preferred_element_type=jnp....]
    pallas_call x1, Pallas kernels: 40.8 us -> 44.3 us  [cholesky(): pl.pallas_call(functools.partial(cholesky_kernel, scale), out_shape=jax.S...]
    ppermute x1, waiting for transfers between devices: 1.94 us -> 5.07 us  [first_rows_of_next(): return lax.ppermute(rows, 'tm', [(i, i - 1) for i in range(1, count)])]
    reshape x1 -> x0, local copies, waits for them, and re-layouts: 3.03 us -> none  [scatter_rows(): value.reshape((2,) * len(bits) + (value.shape[0] >> len(bits), value.shap...]
  transfers between devices with their start and end apart: 13 -> 15, of which waited for: 13 -> 11; matrix products, arithmetic and copies ran while one was open for 0% -> 2% of each run, Pallas kernels for 0% -> 9%
where the time goes in v2:
time: 150 us
  Pallas kernels  65.6 us (44%)
  waiting for transfers between devices  58.7 us (39%)
  starting transfers between devices  20.8 us (14%)
  other arithmetic  3.46 us (2%)
    ppermute x14, waiting for transfers between devices, swap(): return lax.ppermute(value, axis, [(i, i ^ bit) for i in range(count)])  53.7 us
    pallas_call x1, Pallas kernels, cholesky(): pl.pallas_call(functools.partial(cholesky_kernel, scale), out_shape=jax.S...  44.3 us
    ppermute x14, starting transfers between devices, swap(): return lax.ppermute(value, axis, [(i, i ^ bit) for i in range(count)])  19.6 us
    pallas_call x4, Pallas kernels, project(): pl.pallas_call(project_kernel, out_shape=jax.ShapeDtypeStruct((rows // 2,...  12.3 us
    pallas_call x2, Pallas kernels, gram_part(): pl.pallas_call(functools.partial(gram_kernel, first, last), out_shape=out...  8.98 us
    ppermute x1, waiting for transfers between devices, first_rows_of_next(): return lax.ppermute(rows, 'tm', [(i, i - 1) for i in range(1, count)])  5.07 us
  transfers between devices with their start and end apart: 15, of which 11 were waited for; matrix products, arithmetic and copies ran while one was open for 2% of the time, Pallas kernels for 9%

profile of v2, /device:TPU:0, one launch (start us, length us, event | category | flops | bytes accessed | tf_op | source)
XLA Modules:
  0.0 149.6 jit_solution(6914444978215684401)
XLA Ops:
  0.0 0.7 broadcast_subtract_fusion
  0.7 3.1 %shard_map.40 = f32[1024,128]{1,0:T(8,128)} custom-call(s32[2]{0:T(128)} %get-tuple-element.9.half_ref, s32[1,512]{1,0:T(1,128)} %bitcast.5, bf16[4096,512]{1,0:T(8,128)(2,1)} %signals_ref.7), custom_call_target="tpu_custom_call" | custom-call | flops 134217728 | bytes 1572864 | tf_op jit(solution)/shard_map/pallas_call | solution.py:85
  3.7 0.5 collective-permute-start.3
  4.2 3.1 %shard_map.38 = f32[1024,128]{1,0:T(8,128)} custom-call(s32[2]{0:T(128)} %get-tuple-element.9.half_ref, s32[1,512]{1,0:T(1,128)} %bitcast.6, bf16[4096,512]{1,0:T(8,128)(2,1)} %signals_ref.7), custom_call_target="tpu_custom_call" | custom-call | flops 134217728 | bytes 1572864 | tf_op jit(solution)/shard_map/pallas_call | solution.py:85
  7.3 3.1 %shard_map.39 = f32[1024,128]{1,0:T(8,128)} custom-call(s32[2]{0:T(128)} %get-tuple-element.10.half_ref, s32[1,512]{1,0:T(1,128)} %bitcast.7, bf16[4096,512]{1,0:T(8,128)(2,1)} %signals_ref.7), custom_call_target="tpu_custom_call" | custom-call | flops 134217728 | bytes 1572864 | tf_op jit(solution)/shard_map/pallas_call | solution.py:85
  10.4 1.1 add.110
  11.5 3.0 %collective-permute-start.4 = (f32[1024,128]{1,0:T(8,128)S(1)}, f32[1024,128]{1,0:T(8,128)S(1)}, u32[]{:S(2)}, u32[]{:S(2)}) collective-permute-start(f32[1024,128]{1,0:T(8,128)S(1)} %add.110), channel_id=1, source_target_pairs={{0,2},{1,3},{2,0},{3,1},{4,6},{5,7},{6,4},{7,5},{8,10},{9,11},{10,... | collective-permute-start | bytes 1572872 | tf_op jit(solution)/shard_map/ppermute | solution.py:22
  14.5 3.1 %shard_map.37 = f32[1024,128]{1,0:T(8,128)} custom-call(s32[2]{0:T(128)} %get-tuple-element.10.half_ref, s32[1,512]{1,0:T(1,128)} %bitcast.8, bf16[4096,512]{1,0:T(8,128)(2,1)} %signals_ref.7), custom_call_target="tpu_custom_call" | custom-call | flops 134217728 | bytes 1572864 | tf_op jit(solution)/shard_map/pallas_call | solution.py:85
  17.6 1.1 add.108
  18.8 8.4 %collective-permute-done.4 = f32[1024,128]{1,0:T(8,128)S(1)} collective-permute-done((f32[1024,128]{1,0:T(8,128)S(1)}, f32[1024,128]{1,0:T(8,128)S(1)}, u32[]{:S(2)}, u32[]{:S(2)}) %collective-permute-start.4) | collective-permute-done | bytes 524320 | tf_op jit(solution)/shard_map/ppermute | solution.py:22
  27.4 10.4 %collective-permute-done.1 = f32[1024,128]{1,0:T(8,128)S(1)} collective-permute-done((f32[1024,128]{1,0:T(8,128)S(1)}, f32[1024,128]{1,0:T(8,128)S(1)}, u32[]{:S(2)}, u32[]{:S(2)}) %collective-permute-start.1) | collective-permute-done | bytes 524320 | tf_op jit(solution)/shard_map/ppermute | solution.py:22
  38.0 1.3 collective-permute-start.6
  39.4 0.6 gather_fusion
  40.0 3.5 %shard_map.41 = (f32[256,768]{1,0:T(8,128)S(1)}, f32[512,128]{1,0:T(8,128)S(1)}) custom-call(s32[2]{0:T(128)S(1)} %copy-done.1, s32[6]{0:T(128)S(1)} %gather_fusion, f32[1024,128]{1,0:T(8,128)S(1)} %add.111.refs_0_, f32[1024,128]{1,0:T(8,128)S(1)} %collective-permute-done.5.refs_1_), custom_call_target="tpu_custom_call" | custom-call | flops 2415919104 | bytes 1048576 | tf_op jit(solution)/shard_map/pallas_call | solution.py:176
  43.6 5.1 %collective-permute-done.6.refs_4_ = f32[512,128]{1,0:T(8,128)S(1)} collective-permute-done((f32[512,128]{1,0:T(8,128)S(1)}, f32[512,128]{1,0:T(8,128)S(1)}, u32[]{:S(2)}, u32[]{:S(2)}) %collective-permute-start.6) | collective-permute-done | bytes 262176 | tf_op jit(solution)/shard_map/ppermute | solution.py:56
  48.6 5.4 %shard_map.42 = f32[1152,128]{1,0:T(8,128)S(1)} custom-call(s32[2]{0:T(128)S(1)} %copy-done.1, s32[6]{0:T(128)S(1)} %gather_fusion, f32[1024,128]{1,0:T(8,128)S(1)} %add.109.refs_0_, f32[1024,128]{1,0:T(8,128)S(1)} %collective-permute-done.2.refs_1_, f32[256,768]{1,0:T(8,128)S(1)} %get-tuple-element.7.refs_2_, f32[512,128]{1,0:T(8,128)S(1)} %get-tuple-element.8.refs_3_, ...), custom_call_target="tpu_custom_call" | custom-call | flops 3623878656 | bytes 1572864 | tf_op jit(solution)/shard_map/pallas_call | solution.py:176
  54.1 2.7 %collective-permute-start.7 = (f32[576,128]{1,0:T(8,128)S(1)}, f32[576,128]{1,0:T(8,128)S(1)}, u32[]{:S(2)}, u32[]{:S(2)}) collective-permute-start(f32[576,128]{1,0:T(8,128)S(1)} %constant_dynamic-slice_fusion.2), channel_id=1, source_target_pairs={{0,4},{4,0},{8,12},{12,8},{16,20},{20,16},{24,28},{28,24},{1,5},{5... | collective-permute-start | bytes 884744 | tf_op jit(solution)/shard_map/ppermute | solution.py:22
  56.8 6.9 %collective-permute-done.7 = f32[576,128]{1,0:T(8,128)S(1)} collective-permute-done((f32[576,128]{1,0:T(8,128)S(1)}, f32[576,128]{1,0:T(8,128)S(1)}, u32[]{:S(2)}, u32[]{:S(2)}) %collective-permute-start.7) | collective-permute-done | bytes 294944 | tf_op jit(solution)/shard_map/ppermute | solution.py:22
  63.7 1.7 %collective-permute-start.8 = (f32[288,128]{1,0:T(8,128)S(1)}, f32[288,128]{1,0:T(8,128)S(1)}, u32[]{:S(2)}, u32[]{:S(2)}) collective-permute-start(f32[288,128]{1,0:T(8,128)S(1)} %constant_dynamic-slice_fusion.1), channel_id=1, source_target_pairs={{0,8},{4,12},{8,0},{12,4},{16,24},{20,28},{24,16},{28,20},{1,9},{5... | collective-permute-start | bytes 442376 | tf_op jit(solution)/shard_map/ppermute | solution.py:22
  65.4 3.5 %collective-permute-done.8 = f32[288,128]{1,0:T(8,128)S(1)} collective-permute-done((f32[288,128]{1,0:T(8,128)S(1)}, f32[288,128]{1,0:T(8,128)S(1)}, u32[]{:S(2)}, u32[]{:S(2)}) %collective-permute-start.8) | collective-permute-done | bytes 147488 | tf_op jit(solution)/shard_map/ppermute | solution.py:22
  69.0 2.7 %collective-permute-start.9 = (f32[144,128]{1,0:T(8,128)S(1)}, f32[144,128]{1,0:T(8,128)S(1)}, u32[]{:S(2)}, u32[]{:S(2)}) collective-permute-start(f32[144,128]{1,0:T(8,128)S(1)} %constant_dynamic-slice_fusion), channel_id=1, source_target_pairs={{0,16},{4,20},{8,24},{12,28},{16,0},{20,4},{24,8},{28,12},{1,17},{... | collective-permute-start | bytes 221192 | tf_op jit(solution)/shard_map/ppermute | solution.py:22
  71.7 2.7 %collective-permute-done.9 = f32[144,128]{1,0:T(8,128)S(1)} collective-permute-done((f32[144,128]{1,0:T(8,128)S(1)}, f32[144,128]{1,0:T(8,128)S(1)}, u32[]{:S(2)}, u32[]{:S(2)}) %collective-permute-start.9) | collective-permute-done | bytes 73760 | tf_op jit(solution)/shard_map/ppermute | solution.py:22
  74.3 2.8 %collective-permute-start.10 = (f32[144,128]{1,0:T(8,128)S(1)}, f32[144,128]{1,0:T(8,128)S(1)}, u32[]{:S(2)}, u32[]{:S(2)}) collective-permute-start(f32[144,128]{1,0:T(8,128)S(1)} %dynamic-slice_add_fusion.2), channel_id=1, source_target_pairs={{0,16},{4,20},{8,24},{12,28},{16,0},{20,4},{24,8},{28,12},{1,17},{... | collective-permute-start | bytes 221192 | tf_op jit(solution)/shard_map/ppermute | solution.py:22
  77.1 2.6 %collective-permute-done.10 = f32[144,128]{1,0:T(8,128)S(1)} collective-permute-done((f32[144,128]{1,0:T(8,128)S(1)}, f32[144,128]{1,0:T(8,128)S(1)}, u32[]{:S(2)}, u32[]{:S(2)}) %collective-permute-start.10) | collective-permute-done | bytes 73760 | tf_op jit(solution)/shard_map/ppermute | solution.py:22
  79.7 2.2 %collective-permute-start.11 = (f32[288,128]{1,0:T(8,128)S(1)}, f32[288,128]{1,0:T(8,128)S(1)}, u32[]{:S(2)}, u32[]{:S(2)}) collective-permute-start(f32[288,128]{1,0:T(8,128)S(1)} %pad_maximum_fusion.3), channel_id=1, source_target_pairs={{0,8},{4,12},{8,0},{12,4},{16,24},{20,28},{24,16},{28,20},{1,9},{5... | collective-permute-start | bytes 442376 | tf_op jit(solution)/shard_map/ppermute | solution.py:22
  81.9 3.1 %collective-permute-done.11 = f32[288,128]{1,0:T(8,128)S(1)} collective-permute-done((f32[288,128]{1,0:T(8,128)S(1)}, f32[288,128]{1,0:T(8,128)S(1)}, u32[]{:S(2)}, u32[]{:S(2)}) %collective-permute-start.11) | collective-permute-done | bytes 147488 | tf_op jit(solution)/shard_map/ppermute | solution.py:22
  85.0 2.2 %collective-permute-start.12 = (f32[576,128]{1,0:T(8,128)S(1)}, f32[576,128]{1,0:T(8,128)S(1)}, u32[]{:S(2)}, u32[]{:S(2)}) collective-permute-start(f32[576,128]{1,0:T(8,128)S(1)} %pad_maximum_fusion.2), channel_id=1, source_target_pairs={{0,4},{4,0},{8,12},{12,8},{16,20},{20,16},{24,28},{28,24},{1,5},{5... | collective-permute-start | bytes 884744 | tf_op jit(solution)/shard_map/ppermute | solution.py:22
  87.2 4.7 %collective-permute-done.12 = f32[576,128]{1,0:T(8,128)S(1)} collective-permute-done((f32[576,128]{1,0:T(8,128)S(1)}, f32[576,128]{1,0:T(8,128)S(1)}, u32[]{:S(2)}, u32[]{:S(2)}) %collective-permute-start.12) | collective-permute-done | bytes 294944 | tf_op jit(solution)/shard_map/ppermute | solution.py:22
  92.0 1.6 %collective-permute-start.13 = (f32[1152,128]{1,0:T(8,128)S(1)}, f32[1152,128]{1,0:T(8,128)S(1)}, u32[]{:S(2)}, u32[]{:S(2)}) collective-permute-start(f32[1152,128]{1,0:T(8,128)S(1)} %pad_maximum_fusion.1), channel_id=1, source_target_pairs={{0,2},{1,3},{2,0},{3,1},{4,6},{5,7},{6,4},{7,5},{8,10},{9,11},{10,... | collective-permute-start | bytes 1769480 | tf_op jit(solution)/shard_map/ppermute | solution.py:22
  93.6 8.5 %collective-permute-done.13 = f32[1152,128]{1,0:T(8,128)S(1)} collective-permute-done((f32[1152,128]{1,0:T(8,128)S(1)}, f32[1152,128]{1,0:T(8,128)S(1)}, u32[]{:S(2)}, u32[]{:S(2)}) %collective-permute-start.13) | collective-permute-done | bytes 589856 | tf_op jit(solution)/shard_map/ppermute | solution.py:22
  102.4 2.8 %collective-permute-done.14.other_ref = f32[2304,128]{1,0:T(8,128)S(1)} collective-permute-done((f32[2304,128]{1,0:T(8,128)S(1)}, f32[2304,128]{1,0:T(8,128)S(1)}, u32[]{:S(2)}, u32[]{:S(2)}) %collective-permute-start.14) | collective-permute-done | bytes 1179680 | tf_op jit(solution)/shard_map/ppermute | solution.py:22
  105.2 44.3 %shard_map.43 = f32[1024,1024]{1,0:T(8,128)} custom-call(s32[2]{0:T(128)S(1)} %copy-done.1, f32[2304,128]{1,0:T(8,128)S(1)} %pad_maximum_fusion.mine_ref, f32[2304,128]{1,0:T(8,128)S(1)} %collective-permute-done.14.other_ref), custom_call_target="tpu_custom_call" | custom-call | tf_op jit(solution)/shard_map/pallas_call | solution.py:329
  (32 shorter events, 1.0 us)
Async XLA Ops:
  0.0 39.3 %copy-start = (s32[8]{0:T(128)S(1)}, s32[8]{0:T(128)}, u32[]{:S(2)}) copy-start(s32[8]{0:T(128)} %param.5) | copy-start | bytes 100
  3.7 6.6 %collective-permute-start.3 = (f32[1024,128]{1,0:T(8,128)}, f32[1024,128]{1,0:T(8,128)S(1)}, u32[]{:S(2)}, u32[]{:S(2)}) collective-permute-start(f32[1024,128]{1,0:T(8,128)} %shard_map.40), channel_id=1, source_target_pairs={{0,1},{1,0},{2,3},{3,2},{4,5},{5,4},{6,7},{7,6},{8,9},{9,8},{10,11... | collective-permute-start | bytes 1572872 | tf_op jit(solution)/shard_map/ppermute | solution.py:22
  7.2 10.3 %collective-permute-start = (f32[1024,128]{1,0:T(8,128)}, f32[1024,128]{1,0:T(8,128)S(1)}, u32[]{:S(2)}, u32[]{:S(2)}) collective-permute-start(f32[1024,128]{1,0:T(8,128)} %shard_map.38), channel_id=1, source_target_pairs={{0,1},{1,0},{2,3},{3,2},{4,5},{5,4},{6,7},{7,6},{8,9},{9,8},{10,11... | collective-permute-start | bytes 1572872 | tf_op jit(solution)/shard_map/ppermute | solution.py:22
  11.5 15.7 %collective-permute-start.4 = (f32[1024,128]{1,0:T(8,128)S(1)}, f32[1024,128]{1,0:T(8,128)S(1)}, u32[]{:S(2)}, u32[]{:S(2)}) collective-permute-start(f32[1024,128]{1,0:T(8,128)S(1)} %add.110), channel_id=1, source_target_pairs={{0,2},{1,3},{2,0},{3,1},{4,6},{5,7},{6,4},{7,5},{8,10},{9,11},{10,... | collective-permute-start | bytes 1572872 | tf_op jit(solution)/shard_map/ppermute | solution.py:22
  18.7 19.1 %collective-permute-start.1 = (f32[1024,128]{1,0:T(8,128)S(1)}, f32[1024,128]{1,0:T(8,128)S(1)}, u32[]{:S(2)}, u32[]{:S(2)}) collective-permute-start(f32[1024,128]{1,0:T(8,128)S(1)} %add.108), channel_id=1, source_target_pairs={{0,2},{1,3},{2,0},{3,1},{4,6},{5,7},{6,4},{7,5},{8,10},{9,11},{10,... | collective-permute-start | bytes 1572872 | tf_op jit(solution)/shard_map/ppermute | solution.py:22
  27.3 10.7 %collective-permute-start.5 = (f32[1024,128]{1,0:T(8,128)S(1)}, f32[1024,128]{1,0:T(8,128)S(1)}, u32[]{:S(2)}, u32[]{:S(2)}) collective-permute-start(f32[1024,128]{1,0:T(8,128)S(1)} %add.111.refs_0_), channel_id=1, source_target_pairs={{0,1},{1,0},{2,3},{3,2},{4,5},{5,4},{6,7},{7,6},{8,9},{9,8},{10,11... | collective-permute-start | bytes 1572872 | tf_op jit(solution)/shard_map/ppermute | solution.py:22
  27.4 12.6 %copy-start.1 = (s32[2]{0:T(128)S(1)}, s32[2]{0:T(128)}, u32[]{:S(2)}) copy-start(s32[2]{0:T(128)} %get-tuple-element.10.half_ref) | copy-start | bytes 28
  37.9 5.7 %collective-permute-start.2 = (f32[1024,128]{1,0:T(8,128)S(1)}, f32[1024,128]{1,0:T(8,128)S(1)}, u32[]{:S(2)}, u32[]{:S(2)}) collective-permute-start(f32[1024,128]{1,0:T(8,128)S(1)} %add.109.refs_0_), channel_id=1, source_target_pairs={{0,1},{1,0},{2,3},{3,2},{4,5},{5,4},{6,7},{7,6},{8,9},{9,8},{10,11... | collective-permute-start | bytes 1572872 | tf_op jit(solution)/shard_map/ppermute | solution.py:22
  38.0 10.6 %collective-permute-start.6 = (f32[512,128]{1,0:T(8,128)S(1)}, f32[512,128]{1,0:T(8,128)S(1)}, u32[]{:S(2)}, u32[]{:S(2)}) collective-permute-start(f32[512,128]{1,0:T(8,128)S(1)} %slice_select_fusion), channel_id=1, source_target_pairs={{4,0},{8,4},{12,8},{16,12},{20,16},{24,20},{28,24},{5,1},{9,5},{13... | collective-permute-start | bytes 786440 | tf_op jit(solution)/shard_map/ppermute | solution.py:56
  54.1 9.6 %collective-permute-start.7 = (f32[576,128]{1,0:T(8,128)S(1)}, f32[576,128]{1,0:T(8,128)S(1)}, u32[]{:S(2)}, u32[]{:S(2)}) collective-permute-start(f32[576,128]{1,0:T(8,128)S(1)} %constant_dynamic-slice_fusion.2), channel_id=1, source_target_pairs={{0,4},{4,0},{8,12},{12,8},{16,20},{20,16},{24,28},{28,24},{1,5},{5... | collective-permute-start | bytes 884744 | tf_op jit(solution)/shard_map/ppermute | solution.py:22
  63.7 5.2 %collective-permute-start.8 = (f32[288,128]{1,0:T(8,128)S(1)}, f32[288,128]{1,0:T(8,128)S(1)}, u32[]{:S(2)}, u32[]{:S(2)}) collective-permute-start(f32[288,128]{1,0:T(8,128)S(1)} %constant_dynamic-slice_fusion.1), channel_id=1, source_target_pairs={{0,8},{4,12},{8,0},{12,4},{16,24},{20,28},{24,16},{28,20},{1,9},{5... | collective-permute-start | bytes 442376 | tf_op jit(solution)/shard_map/ppermute | solution.py:22
  69.0 5.3 %collective-permute-start.9 = (f32[144,128]{1,0:T(8,128)S(1)}, f32[144,128]{1,0:T(8,128)S(1)}, u32[]{:S(2)}, u32[]{:S(2)}) collective-permute-start(f32[144,128]{1,0:T(8,128)S(1)} %constant_dynamic-slice_fusion), channel_id=1, source_target_pairs={{0,16},{4,20},{8,24},{12,28},{16,0},{20,4},{24,8},{28,12},{1,17},{... | collective-permute-start | bytes 221192 | tf_op jit(solution)/shard_map/ppermute | solution.py:22
  74.3 5.3 %collective-permute-start.10 = (f32[144,128]{1,0:T(8,128)S(1)}, f32[144,128]{1,0:T(8,128)S(1)}, u32[]{:S(2)}, u32[]{:S(2)}) collective-permute-start(f32[144,128]{1,0:T(8,128)S(1)} %dynamic-slice_add_fusion.2), channel_id=1, source_target_pairs={{0,16},{4,20},{8,24},{12,28},{16,0},{20,4},{24,8},{28,12},{1,17},{... | collective-permute-start | bytes 221192 | tf_op jit(solution)/shard_map/ppermute | solution.py:22
  79.7 5.3 %collective-permute-start.11 = (f32[288,128]{1,0:T(8,128)S(1)}, f32[288,128]{1,0:T(8,128)S(1)}, u32[]{:S(2)}, u32[]{:S(2)}) collective-permute-start(f32[288,128]{1,0:T(8,128)S(1)} %pad_maximum_fusion.3), channel_id=1, source_target_pairs={{0,8},{4,12},{8,0},{12,4},{16,24},{20,28},{24,16},{28,20},{1,9},{5... | collective-permute-start | bytes 442376 | tf_op jit(solution)/shard_map/ppermute | solution.py:22
  85.0 6.9 %collective-permute-start.12 = (f32[576,128]{1,0:T(8,128)S(1)}, f32[576,128]{1,0:T(8,128)S(1)}, u32[]{:S(2)}, u32[]{:S(2)}) collective-permute-start(f32[576,128]{1,0:T(8,128)S(1)} %pad_maximum_fusion.2), channel_id=1, source_target_pairs={{0,4},{4,0},{8,12},{12,8},{16,20},{20,16},{24,28},{28,24},{1,5},{5... | collective-permute-start | bytes 884744 | tf_op jit(solution)/shard_map/ppermute | solution.py:22
  92.0 10.1 %collective-permute-start.13 = (f32[1152,128]{1,0:T(8,128)S(1)}, f32[1152,128]{1,0:T(8,128)S(1)}, u32[]{:S(2)}, u32[]{:S(2)}) collective-permute-start(f32[1152,128]{1,0:T(8,128)S(1)} %pad_maximum_fusion.1), channel_id=1, source_target_pairs={{0,2},{1,3},{2,0},{3,1},{4,6},{5,7},{6,4},{7,5},{8,10},{9,11},{10,... | collective-permute-start | bytes 1769480 | tf_op jit(solution)/shard_map/ppermute | solution.py:22
  102.3 2.9 %collective-permute-start.14 = (f32[2304,128]{1,0:T(8,128)S(1)}, f32[2304,128]{1,0:T(8,128)S(1)}, u32[]{:S(2)}, u32[]{:S(2)}) collective-permute-start(f32[2304,128]{1,0:T(8,128)S(1)} %pad_maximum_fusion.mine_ref), channel_id=1, source_target_pairs={{0,1},{1,0},{2,3},{3,2},{4,5},{5,4},{6,7},{7,6},{8,9},{9,8},{10,11... | collective-permute-start | bytes 3538952 | tf_op jit(solution)/shard_map/ppermute | solution.py:22

commit v3 on v2

--- a/solution.py
+++ b/solution.py
@@ -13,6 +13,7 @@
 MAXLAG = 512
 BLOCK = 128
 GROUP = 8
+SPAN = 4
 HIGHEST = lax.Precision.HIGHEST
 CONTRACT_ROWS = (((0,), (0,)), ((), ()))
 
@@ -49,6 +50,20 @@
     for bit in bits_of("tm")[::-1]:
         value = double(value, "tm", bit)
     return value
+
+
+def add_kernel(left_ref, right_ref, *refs):
+    refs[-1][...] = left_ref[...] + right_ref[...]
+
+
+def add(left, right, *earlier):
+    vmem = pl.BlockSpec(memory_space=pltpu.VMEM)
+    return pl.pallas_call(
+        add_kernel,
+        out_shape=jax.ShapeDtypeStruct(left.shape, left.dtype),
+        in_specs=[vmem, vmem] + [pl.BlockSpec(memory_space=pl.ANY)] * len(earlier),
+        out_specs=vmem,
+    )(left, right, *earlier)
 
 
 def first_rows_of_next(rows):
@@ -90,11 +105,12 @@
     )(half, channel_node.reshape(1, channels), signals)
 
 
-def gram_kernel(first, last, half_ref, lags_ref, *refs):
+def gram_kernel(first, last, earlier, half_ref, lags_ref, *refs):
     refs = list(refs)
     mine_ref, other_ref = refs.pop(0), refs.pop(0)
     sum_in_ref, tail_in_ref = (None, None) if first else (refs.pop(0), refs.pop(0))
     after_ref = refs.pop(0) if last else None
+    del refs[:earlier]
     out_ref = refs.pop(0)
     tail_out_ref = None if last else refs.pop(0)
     ext_ref, high_ref, low_ref, sum_ref = refs
@@ -153,7 +169,7 @@
         out_ref[...] = sum_ref[...]
 
 
-def gram_part(half, lags, mine, other, carried, after):
+def gram_part(half, lags, mine, other, carried, after, earlier):
     first, last = carried is None, after is not None
     count = lags.shape[0]
     blocks = 2 * (count - 2) + 1
@@ -174,9 +190,9 @@
     smem = pl.BlockSpec(memory_space=pltpu.SMEM)
     step_rows = 512
     return pl.pallas_call(
-        functools.partial(gram_kernel, first, last),
+        functools.partial(gram_kernel, first, last, len(earlier)),
         out_shape=out_shape,
-        in_specs=[smem, smem] + [vmem] * (len(operands) - 2),
+        in_specs=[smem, smem] + [vmem] * (len(operands) - 2) + [pl.BlockSpec(memory_space=pl.ANY)] * len(earlier),
         out_specs=vmem if last else (vmem, vmem),
         scratch_shapes=[
             pltpu.VMEM((rows, NODES), jnp.float32),
@@ -186,7 +202,7 @@
         ],
         compiler_params=pltpu.CompilerParams(vmem_limit_bytes=40 << 20),
         cost_estimate=pl.CostEstimate(flops=rows * NODES * NODES * count * 12, bytes_accessed=rows * NODES * 4, transcendentals=0),
-    )(*operands)
+    )(*operands, *earlier)
 
 
 def row_of(value, index):
@@ -201,34 +217,76 @@
     count = len(block)
     sub = lax.broadcasted_iota(jnp.int32, (GROUP, BLOCK), 0)
     lane = lax.broadcasted_iota(jnp.int32, (GROUP, BLOCK), 1)
-    block = list(block)
-    inverse = [jnp.where(lane == sub + GROUP * s, 1.0, 0.0) for s in range(count)]
+    state = list(block)
+    result = [None] * count
+    full = [None] * count
+    columns = [column_of(state[0], m) for m in range(GROUP)]
     for g in range(count):
-        columns = [column_of(block[g], GROUP * g + m) for m in range(GROUP)]
-        top, top_inverse = block[g], inverse[g]
-        scale, factors, rows, inverse_rows = [], {}, [], []
+        first_lane, next_lane = GROUP * g, GROUP * (g + 1)
+        here = (lane >= first_lane) & (lane < next_lane)
+        span = g // SPAN
+        more = g + 1 < count
+        if more:
+            next_columns = [column_of(state[g + 1], next_lane + m) for m in range(GROUP)]
+            next_left = [column_of(state[g + 1], first_lane + m) for m in range(GROUP)]
+            state[g + 1] = jnp.where(here, 0.0, state[g + 1])
+        top = jnp.where(here, jnp.where(lane == sub + first_lane, 1.0, 0.0), state[g])
+        diagonal = jnp.zeros_like(top)
+        scale, factors, rows = [], {}, []
         for m in range(GROUP):
-            scale.append(lax.rsqrt(row_of(columns[m], m)))
-            rows.append(row_of(top, m) * scale[m])
-            inverse_rows.append(row_of(top_inverse, m) * scale[m])
+            pivot = row_of(columns[m], m)
+            scale.append(lax.rsqrt(pivot))
             left = columns[m] * scale[m]
             for n in range(m + 1, GROUP):
                 factors[m, n] = row_of(left, n)
                 columns[n] = columns[n] - left * factors[m, n]
+            if more:
+                next_left[m] = next_left[m] * scale[m]
+                for n in range(m + 1, GROUP):
+                    next_left[n] = next_left[n] - next_left[m] * factors[m, n]
+                for n in range(GROUP):
+                    next_columns[n] = next_columns[n] - next_left[m] * row_of(next_left[m], n)
+            rows.append(row_of(top, m) * scale[m])
             below = jnp.where(sub > m, left, 0.0)
             top = jnp.where(sub == m, rows[m], top - below * rows[m])
-            top_inverse = jnp.where(sub == m, inverse_rows[m], top_inverse - below * inverse_rows[m])
-        block[g] = jnp.where(lane >= sub + GROUP * g, top, 0.0)
-        inverse[g] = top_inverse
-        for s in range(g + 1, count):
-            columns = [column_of(block[s], GROUP * g + m) for m in range(GROUP)]
+            entries = pivot * scale[m]
+            for n in range(m + 1, GROUP):
+                entries = jnp.where(lane == first_lane + n, factors[m, n], entries)
+            diagonal = jnp.where(sub == m, entries, diagonal)
+            if more:
+                state[g + 1] = state[g + 1] - next_left[m] * rows[m]
+        full[g] = top
+        result[g] = jnp.where(lane >= next_lane, top, jnp.where(lane >= sub + first_lane, diagonal, 0.0))
+        state[g] = jnp.where(lane < next_lane, top, 0.0)
+        columns = next_columns
+        for s in range(g + 2, min(count, (span + 2) * SPAN)):
+            left = [column_of(state[s], first_lane + m) for m in range(GROUP)]
+            value = jnp.where(here, 0.0, state[s])
             for m in range(GROUP):
-                left = columns[m] * scale[m]
+                left[m] = left[m] * scale[m]
                 for n in range(m + 1, GROUP):
-                    columns[n] = columns[n] - left * factors[m, n]
-                block[s] = block[s] - left * rows[m]
-                inverse[s] = inverse[s] - left * inverse_rows[m]
-    return block, inverse
+                    left[n] = left[n] - left[m] * factors[m, n]
+                value = value - left[m] * rows[m]
+            state[s] = value
+        rest = (span + 2) * SPAN
+        if g % SPAN == SPAN - 1 and rest < count:
+            begin = span * SPAN
+            left = jnp.concatenate(full[begin : g + 1], axis=0)
+            right = [
+                jnp.where((lane >= GROUP * (i + 1)) & (lane < next_lane), 0.0, full[i]) for i in range(begin, g + 1)
+            ]
+            update = lax.dot_general(
+                left[:, GROUP * rest :],
+                jnp.concatenate(right, axis=0),
+                CONTRACT_ROWS,
+                precision=HIGHEST,
+                preferred_element_type=jnp.float32,
+            )
+            inside = (lane >= GROUP * begin) & (lane < next_lane)
+            for s in range(rest, count):
+                place = GROUP * (s - rest)
+                state[s] = jnp.where(inside, 0.0, state[s]) - update[place : place + GROUP]
+    return result, state
 
 
 def arrange(half_ref, mine_ref, other_ref, natural_ref, ordered_ref):
@@ -352,19 +410,23 @@
     span = lag_count // 2 + 2
     lags = lag_offsets[(2 * chan + jnp.arange(span, dtype=jnp.int32)) % lag_count]
     size = rows // CHUNKS
+    totals, sent = [], []
+    for index in range(CHUNKS):
+        send = project(signals, channel_node, index * size, size, 1 - half)
+        received = swap(send, "chan", 1)
+        keep = project(signals, channel_node, index * size, size, half)
+        totals.append(keep + received)
+        sent.append(swap(totals[-1], "chan", 2))
     carried = after = None
     for index in range(CHUNKS):
         first, last = index == 0, index == CHUNKS - 1
-        send = project(signals, channel_node, index * size, size, 1 - half)
-        received = swap(send, "chan", 1)
-        keep = project(signals, channel_node, index * size, size, half)
-        value = keep + received
-        value = value + swap(value, "chan", 2)
+        value = add(totals[index], sent[index], *(totals[1:] if first else (carried[1],)))
         other = swap(value, "chan", 1)
         if first:
             head = jnp.where(half[0] == 0, value[:MAXLAG], other[:MAXLAG])
             after = first_rows_of_next(head)
-        carried = gram_part(half, lags, value, other, carried, after if last else None)
+        earlier = (head,) if first else ()
+        carried = gram_part(half, lags, value, other, carried, after if last else None, earlier)
     blocks = sum_over_time_blocks(carried)
     blocks = double(blocks, "chan", 2)
     other = swap(blocks, "chan", 1)

time: 150 us -> 149 us (level)
  Pallas kernels: 65.6 us -> 59 us
  local copies, waits for them, and re-layouts: 0.71 us -> 3.27 us
  other arithmetic: 3.46 us -> 5.05 us
    pallas_call x1, Pallas kernels: 44.3 us -> 33.6 us  [cholesky(): pl.pallas_call(functools.partial(cholesky_kernel, scale), out_shape=jax.S...]
    ppermute x1, waiting for transfers between devices: 5.07 us -> 9.3 us  [first_rows_of_next(): return lax.ppermute(rows, 'tm', [(i, i - 1) for i in range(1, count)])]
    pallas_call x2 -> x4, Pallas kernels: 8.98 us -> 13.2 us  [the longest x2 8.98 us: gram_part(): pl.pallas_call(functools.partial(gram_kernel, first, last, len(earlier)),...]
    ppermute x14, waiting for transfers between devices: 53.7 us -> 50.3 us  [swap(): return lax.ppermute(value, axis, [(i, i ^ bit) for i in range(count)])]
    unnamed x4 -> x18, local copies, waits for them, and re-layouts: 0.01 us -> 2.56 us
    add x4 -> x2, other arithmetic: 2.39 us -> 3.07 us  [on_device(): totals.append(keep + received)]
  transfers between devices with their start and end apart: 15 -> 15, of which waited for: 11 -> 11; matrix products, arithmetic and copies ran while one was open for 2% -> 3% of each run, Pallas kernels for 9% -> 9%
where the time goes in v3:
time: 149 us
  waiting for transfers between devices  59.6 us (40%)
  Pallas kernels  59 us (40%)
  starting transfers between devices  21.5 us (14%)
  other arithmetic  5.05 us (3%)
  local copies, waits for them, and re-layouts  3.27 us (2%)
    ppermute x14, waiting for transfers between devices, swap(): return lax.ppermute(value, axis, [(i, i ^ bit) for i in range(count)])  50.3 us
    pallas_call x1, Pallas kernels, cholesky(): pl.pallas_call(functools.partial(cholesky_kernel, scale), out_shape=jax.S...  33.6 us
    ppermute x14, starting transfers between devices, swap(): return lax.ppermute(value, axis, [(i, i ^ bit) for i in range(count)])  20.2 us
    pallas_call x4, Pallas kernels, project(): pl.pallas_call(project_kernel, out_shape=jax.ShapeDtypeStruct((rows // 2,...  12.3 us
    ppermute x1, waiting for transfers between devices, first_rows_of_next(): return lax.ppermute(rows, 'tm', [(i, i - 1) for i in range(1, count)])  9.3 us
    pallas_call x2, Pallas kernels, gram_part(): pl.pallas_call(functools.partial(gram_kernel, first, last, len(earlier)),...  8.98 us
    pallas_call x2, Pallas kernels, add(): pl.pallas_call(add_kernel, out_shape=jax.ShapeDtypeStruct(left.shape, lef...  4.18 us
    add x2, other arithmetic, on_device(): totals.append(keep + received)  3.07 us
  transfers between devices with their start and end apart: 15, of which 11 were waited for; matrix products, arithmetic and copies ran while one was open for 3% of the time, Pallas kernels for 9%

profile of v3, /device:TPU:0, one launch (start us, length us, event | category | flops | bytes accessed | tf_op | source)
XLA Modules:
  0.0 148.7 jit_solution(7216014712078044475)
XLA Ops:
  0.6 3.1 %shard_map.40 = f32[1024,128]{1,0:T(8,128)} custom-call(s32[2]{0:T(128)} %get-tuple-element.9.half_ref, s32[1,512]{1,0:T(1,128)} %bitcast.5, bf16[4096,512]{1,0:T(8,128)(2,1)} %signals_ref.7), custom_call_target="tpu_custom_call" | custom-call | flops 134217728 | bytes 1572864 | tf_op jit(solution)/shard_map/pallas_call | solution.py:100
  4.1 3.1 %shard_map.38 = f32[1024,128]{1,0:T(8,128)} custom-call(s32[2]{0:T(128)} %get-tuple-element.9.half_ref, s32[1,512]{1,0:T(1,128)} %bitcast.6, bf16[4096,512]{1,0:T(8,128)(2,1)} %signals_ref.7), custom_call_target="tpu_custom_call" | custom-call | flops 134217728 | bytes 1572864 | tf_op jit(solution)/shard_map/pallas_call | solution.py:100
  7.2 3.1 %shard_map.39 = f32[1024,128]{1,0:T(8,128)} custom-call(s32[2]{0:T(128)} %get-tuple-element.10.half_ref, s32[1,512]{1,0:T(1,128)} %bitcast.7, bf16[4096,512]{1,0:T(8,128)(2,1)} %signals_ref.7), custom_call_target="tpu_custom_call" | custom-call | flops 134217728 | bytes 1572864 | tf_op jit(solution)/shard_map/pallas_call | solution.py:100
  10.3 1.1 add.103.left_ref
  11.4 3.0 %collective-permute-start.3 = (f32[1024,128]{1,0:T(8,128)S(1)}, f32[1024,128]{1,0:T(8,128)S(1)}, u32[]{:S(2)}, u32[]{:S(2)}) collective-permute-start(f32[1024,128]{1,0:T(8,128)S(1)} %add.103.left_ref), channel_id=1, source_target_pairs={{0,2},{1,3},{2,0},{3,1},{4,6},{5,7},{6,4},{7,5},{8,10},{9,11},{10,... | collective-permute-start | bytes 1572872 | tf_op jit(solution)/shard_map/ppermute | solution.py:23
  14.5 3.1 %shard_map.37 = f32[1024,128]{1,0:T(8,128)} custom-call(s32[2]{0:T(128)} %get-tuple-element.10.half_ref, s32[1,512]{1,0:T(1,128)} %bitcast.8, bf16[4096,512]{1,0:T(8,128)(2,1)} %signals_ref.7), custom_call_target="tpu_custom_call" | custom-call | flops 134217728 | bytes 1572864 | tf_op jit(solution)/shard_map/pallas_call | solution.py:100
  17.6 1.9 %add.102.refs_0_.left_ref = f32[1024,128]{1,0:T(8,128)} add(f32[1024,128]{1,0:T(8,128)} %shard_map.37, f32[1024,128]{1,0:T(8,128)S(1)} %collective-permute-done) | non-fusion elementwise | flops 131072 | bytes 1572864 | tf_op jit(solution)/shard_map/add | solution.py:418
  19.5 7.1 %collective-permute-done.3.right_ref = f32[1024,128]{1,0:T(8,128)S(1)} collective-permute-done((f32[1024,128]{1,0:T(8,128)S(1)}, f32[1024,128]{1,0:T(8,128)S(1)}, u32[]{:S(2)}, u32[]{:S(2)}) %collective-permute-start.3) | collective-permute-done | bytes 524320 | tf_op jit(solution)/shard_map/ppermute | solution.py:23
  27.4 2.1 %shard_map.41.refs_0_ = f32[1024,128]{1,0:T(8,128)} custom-call(f32[1024,128]{1,0:T(8,128)} %copy-done.7, f32[1024,128]{1,0:T(8,128)} %copy-done.8, f32[1024,128]{1,0:T(8,128)} %add.102.refs_0_.left_ref), custom_call_target="tpu_custom_call" | custom-call | tf_op jit(solution)/shard_map/pallas_call | solution.py:61
  29.5 1.8 %collective-permute-start.1 = (f32[1024,128]{1,0:T(8,128)S(1)}, f32[1024,128]{1,0:T(8,128)}, u32[]{:S(2)}, u32[]{:S(2)}) collective-permute-start(f32[1024,128]{1,0:T(8,128)S(1)} %copy-done.6), channel_id=1, source_target_pairs={{0,2},{1,3},{2,0},{3,1},{4,6},{5,7},{6,4},{7,5},{8,10},{9,11},{10,... | collective-permute-start | bytes 1572872 | tf_op jit(solution)/shard_map/ppermute | solution.py:23
  33.0 3.5 %shard_map.42 = (f32[256,768]{1,0:T(8,128)S(1)}, f32[512,128]{1,0:T(8,128)S(1)}) custom-call(s32[2]{0:T(128)S(1)} %copy-done.5, s32[6]{0:T(128)S(1)} %gather_fusion, f32[1024,128]{1,0:T(8,128)S(1)} %copy-done.1, f32[1024,128]{1,0:T(8,128)S(1)} %collective-permute-done.4.refs_1_, f32[512,128]{1,0:T(8,128)S(1)} %slice_select_fusion.refs_2_), custom_call_target="tpu_custom_call" | custom-call | flops 2415919104 | bytes 1048576 | tf_op jit(solution)/shard_map/pallas_call | solution.py:192
  37.2 6.8 %collective-permute-done.1.right_ref = f32[1024,128]{1,0:T(8,128)} collective-permute-done((f32[1024,128]{1,0:T(8,128)S(1)}, f32[1024,128]{1,0:T(8,128)}, u32[]{:S(2)}, u32[]{:S(2)}) %collective-permute-start.1) | collective-permute-done | bytes 524320 | tf_op jit(solution)/shard_map/ppermute | solution.py:23
  44.0 2.1 %shard_map.43.refs_0_ = f32[1024,128]{1,0:T(8,128)} custom-call(f32[1024,128]{1,0:T(8,128)} %add.102.refs_0_.left_ref, f32[1024,128]{1,0:T(8,128)} %collective-permute-done.1.right_ref, f32[512,128]{1,0:T(8,128)} %copy-done.3), custom_call_target="tpu_custom_call" | custom-call | tf_op jit(solution)/shard_map/pallas_call | solution.py:61
  46.1 1.3 collective-permute-start.6
  47.4 9.3 %collective-permute-done.6.refs_4_ = f32[512,128]{1,0:T(8,128)S(1)} collective-permute-done((f32[512,128]{1,0:T(8,128)S(1)}, f32[512,128]{1,0:T(8,128)S(1)}, u32[]{:S(2)}, u32[]{:S(2)}) %collective-permute-start.6) | collective-permute-done | bytes 262176 | tf_op jit(solution)/shard_map/ppermute | solution.py:71
  56.7 1.0 copy-done.2
  57.8 5.4 %shard_map.44 = f32[1152,128]{1,0:T(8,128)S(1)} custom-call(s32[2]{0:T(128)S(1)} %copy-done.5, s32[6]{0:T(128)S(1)} %gather_fusion, f32[1024,128]{1,0:T(8,128)S(1)} %copy-done.2, f32[1024,128]{1,0:T(8,128)S(1)} %collective-permute-done.5.refs_1_, f32[256,768]{1,0:T(8,128)S(1)} %get-tuple-element.8.refs_2_, f32[512,128]{1,0:T(8,128)S(1)} %copy-done.4, ...), custom_call_target="tpu_custom_call" | custom-call | flops 3623878656 | bytes 1572864 | tf_op jit(solution)/shard_map/pallas_call | solution.py:192
  63.2 2.7 %collective-permute-start.7 = (f32[576,128]{1,0:T(8,128)S(1)}, f32[576,128]{1,0:T(8,128)S(1)}, u32[]{:S(2)}, u32[]{:S(2)}) collective-permute-start(f32[576,128]{1,0:T(8,128)S(1)} %constant_dynamic-slice_fusion.2), channel_id=1, source_target_pairs={{0,4},{4,0},{8,12},{12,8},{16,20},{20,16},{24,28},{28,24},{1,5},{5... | collective-permute-start | bytes 884744 | tf_op jit(solution)/shard_map/ppermute | solution.py:23
  65.9 6.8 %collective-permute-done.7 = f32[576,128]{1,0:T(8,128)S(1)} collective-permute-done((f32[576,128]{1,0:T(8,128)S(1)}, f32[576,128]{1,0:T(8,128)S(1)}, u32[]{:S(2)}, u32[]{:S(2)}) %collective-permute-start.7) | collective-permute-done | bytes 294944 | tf_op jit(solution)/shard_map/ppermute | solution.py:23
  72.9 1.6 %collective-permute-start.8 = (f32[288,128]{1,0:T(8,128)S(1)}, f32[288,128]{1,0:T(8,128)S(1)}, u32[]{:S(2)}, u32[]{:S(2)}) collective-permute-start(f32[288,128]{1,0:T(8,128)S(1)} %constant_dynamic-slice_fusion.1), channel_id=1, source_target_pairs={{0,8},{4,12},{8,0},{12,4},{16,24},{20,28},{24,16},{28,20},{1,9},{5... | collective-permute-start | bytes 442376 | tf_op jit(solution)/shard_map/ppermute | solution.py:23
  74.5 3.6 %collective-permute-done.8 = f32[288,128]{1,0:T(8,128)S(1)} collective-permute-done((f32[288,128]{1,0:T(8,128)S(1)}, f32[288,128]{1,0:T(8,128)S(1)}, u32[]{:S(2)}, u32[]{:S(2)}) %collective-permute-start.8) | collective-permute-done | bytes 147488 | tf_op jit(solution)/shard_map/ppermute | solution.py:23
  78.1 2.7 %collective-permute-start.9 = (f32[144,128]{1,0:T(8,128)S(1)}, f32[144,128]{1,0:T(8,128)S(1)}, u32[]{:S(2)}, u32[]{:S(2)}) collective-permute-start(f32[144,128]{1,0:T(8,128)S(1)} %constant_dynamic-slice_fusion), channel_id=1, source_target_pairs={{0,16},{4,20},{8,24},{12,28},{16,0},{20,4},{24,8},{28,12},{1,17},{... | collective-permute-start | bytes 221192 | tf_op jit(solution)/shard_map/ppermute | solution.py:23
  80.8 2.7 %collective-permute-done.9 = f32[144,128]{1,0:T(8,128)S(1)} collective-permute-done((f32[144,128]{1,0:T(8,128)S(1)}, f32[144,128]{1,0:T(8,128)S(1)}, u32[]{:S(2)}, u32[]{:S(2)}) %collective-permute-start.9) | collective-permute-done | bytes 73760 | tf_op jit(solution)/shard_map/ppermute | solution.py:23
  83.4 2.8 %collective-permute-start.10 = (f32[144,128]{1,0:T(8,128)S(1)}, f32[144,128]{1,0:T(8,128)S(1)}, u32[]{:S(2)}, u32[]{:S(2)}) collective-permute-start(f32[144,128]{1,0:T(8,128)S(1)} %dynamic-slice_add_fusion.2), channel_id=1, source_target_pairs={{0,16},{4,20},{8,24},{12,28},{16,0},{20,4},{24,8},{28,12},{1,17},{... | collective-permute-start | bytes 221192 | tf_op jit(solution)/shard_map/ppermute | solution.py:23
  86.2 2.6 %collective-permute-done.10 = f32[144,128]{1,0:T(8,128)S(1)} collective-permute-done((f32[144,128]{1,0:T(8,128)S(1)}, f32[144,128]{1,0:T(8,128)S(1)}, u32[]{:S(2)}, u32[]{:S(2)}) %collective-permute-start.10) | collective-permute-done | bytes 73760 | tf_op jit(solution)/shard_map/ppermute | solution.py:23
  88.8 3.2 %collective-permute-start.11 = (f32[288,128]{1,0:T(8,128)S(1)}, f32[288,128]{1,0:T(8,128)S(1)}, u32[]{:S(2)}, u32[]{:S(2)}) collective-permute-start(f32[288,128]{1,0:T(8,128)S(1)} %pad_maximum_fusion.3), channel_id=1, source_target_pairs={{0,8},{4,12},{8,0},{12,4},{16,24},{20,28},{24,16},{28,20},{1,9},{5... | collective-permute-start | bytes 442376 | tf_op jit(solution)/shard_map/ppermute | solution.py:23
  92.0 3.1 %collective-permute-done.11 = f32[288,128]{1,0:T(8,128)S(1)} collective-permute-done((f32[288,128]{1,0:T(8,128)S(1)}, f32[288,128]{1,0:T(8,128)S(1)}, u32[]{:S(2)}, u32[]{:S(2)}) %collective-permute-start.11) | collective-permute-done | bytes 147488 | tf_op jit(solution)/shard_map/ppermute | solution.py:23
  95.1 1.2 collective-permute-start.12
  96.3 5.6 %collective-permute-done.12 = f32[576,128]{1,0:T(8,128)S(1)} collective-permute-done((f32[576,128]{1,0:T(8,128)S(1)}, f32[576,128]{1,0:T(8,128)S(1)}, u32[]{:S(2)}, u32[]{:S(2)}) %collective-permute-start.12) | collective-permute-done | bytes 294944 | tf_op jit(solution)/shard_map/ppermute | solution.py:23
  102.8 9.2 %collective-permute-done.13 = f32[1152,128]{1,0:T(8,128)S(1)} collective-permute-done((f32[1152,128]{1,0:T(8,128)S(1)}, f32[1152,128]{1,0:T(8,128)S(1)}, u32[]{:S(2)}, u32[]{:S(2)}) %collective-permute-start.13) | collective-permute-done | bytes 589856 | tf_op jit(solution)/shard_map/ppermute | solution.py:23
  112.2 2.8 %collective-permute-done.14.other_ref = f32[2304,128]{1,0:T(8,128)S(1)} collective-permute-done((f32[2304,128]{1,0:T(8,128)S(1)}, f32[2304,128]{1,0:T(8,128)S(1)}, u32[]{:S(2)}, u32[]{:S(2)}) %collective-permute-start.14) | collective-permute-done | bytes 1179680 | tf_op jit(solution)/shard_map/ppermute | solution.py:23
  115.1 33.6 %shard_map.45 = f32[1024,1024]{1,0:T(8,128)} custom-call(s32[2]{0:T(128)S(1)} %copy-done.5, f32[2304,128]{1,0:T(8,128)S(1)} %pad_maximum_fusion.mine_ref, f32[2304,128]{1,0:T(8,128)S(1)} %collective-permute-done.14.other_ref), custom_call_target="tpu_custom_call" | custom-call | tf_op jit(solution)/shard_map/pallas_call | solution.py:387
  (46 shorter events, 5.6 us)
Async XLA Ops:
  0.0 31.3 %copy-start = (s32[8]{0:T(128)S(1)}, s32[8]{0:T(128)}, u32[]{:S(2)}) copy-start(s32[8]{0:T(128)} %param.5) | copy-start | bytes 100
  3.7 6.6 %collective-permute-start.2 = (f32[1024,128]{1,0:T(8,128)}, f32[1024,128]{1,0:T(8,128)S(1)}, u32[]{:S(2)}, u32[]{:S(2)}) collective-permute-start(f32[1024,128]{1,0:T(8,128)} %shard_map.40), channel_id=1, source_target_pairs={{0,1},{1,0},{2,3},{3,2},{4,5},{5,4},{6,7},{7,6},{8,9},{9,8},{10,11... | collective-permute-start | bytes 1572872 | tf_op jit(solution)/shard_map/ppermute | solution.py:23
  7.2 10.4 %collective-permute-start = (f32[1024,128]{1,0:T(8,128)}, f32[1024,128]{1,0:T(8,128)S(1)}, u32[]{:S(2)}, u32[]{:S(2)}) collective-permute-start(f32[1024,128]{1,0:T(8,128)} %shard_map.38), channel_id=1, source_target_pairs={{0,1},{1,0},{2,3},{3,2},{4,5},{5,4},{6,7},{7,6},{8,9},{9,8},{10,11... | collective-permute-start | bytes 1572872 | tf_op jit(solution)/shard_map/ppermute | solution.py:23
  11.4 6.1 %copy-start.7 = (f32[1024,128]{1,0:T(8,128)}, f32[1024,128]{1,0:T(8,128)S(1)}, u32[]{:S(2)}) copy-start(f32[1024,128]{1,0:T(8,128)S(1)} %add.103.left_ref) | copy-start | bytes 1572868
  11.4 15.1 %collective-permute-start.3 = (f32[1024,128]{1,0:T(8,128)S(1)}, f32[1024,128]{1,0:T(8,128)S(1)}, u32[]{:S(2)}, u32[]{:S(2)}) collective-permute-start(f32[1024,128]{1,0:T(8,128)S(1)} %add.103.left_ref), channel_id=1, source_target_pairs={{0,2},{1,3},{2,0},{3,1},{4,6},{5,7},{6,4},{7,5},{8,10},{9,11},{10,... | collective-permute-start | bytes 1572872 | tf_op jit(solution)/shard_map/ppermute | solution.py:23
  19.5 10.0 %copy-start.6 = (f32[1024,128]{1,0:T(8,128)S(1)}, f32[1024,128]{1,0:T(8,128)}, u32[]{:S(2)}) copy-start(f32[1024,128]{1,0:T(8,128)} %add.102.refs_0_.left_ref) | copy-start | bytes 1572868
  26.6 0.8 copy-start.8
  29.5 3.5 %copy-start.1 = (f32[1024,128]{1,0:T(8,128)S(1)}, f32[1024,128]{1,0:T(8,128)}, u32[]{:S(2)}) copy-start(f32[1024,128]{1,0:T(8,128)} %shard_map.41.refs_0_) | copy-start | bytes 1572868
  29.5 3.5 %copy-start.5 = (s32[2]{0:T(128)S(1)}, s32[2]{0:T(128)}, u32[]{:S(2)}) copy-start(s32[2]{0:T(128)} %get-tuple-element.10.half_ref) | copy-start | bytes 28
  29.5 2.5 %collective-permute-start.4 = (f32[1024,128]{1,0:T(8,128)}, f32[1024,128]{1,0:T(8,128)S(1)}, u32[]{:S(2)}, u32[]{:S(2)}) collective-permute-start(f32[1024,128]{1,0:T(8,128)} %shard_map.41.refs_0_), channel_id=1, source_target_pairs={{0,1},{1,0},{2,3},{3,2},{4,5},{5,4},{6,7},{7,6},{8,9},{9,8},{10,11... | collective-permute-start | bytes 1572872 | tf_op jit(solution)/shard_map/ppermute | solution.py:23
  29.5 14.5 %collective-permute-start.1 = (f32[1024,128]{1,0:T(8,128)S(1)}, f32[1024,128]{1,0:T(8,128)}, u32[]{:S(2)}, u32[]{:S(2)}) collective-permute-start(f32[1024,128]{1,0:T(8,128)S(1)} %copy-done.6), channel_id=1, source_target_pairs={{0,2},{1,3},{2,0},{3,1},{4,6},{5,7},{6,4},{7,5},{8,10},{9,11},{10,... | collective-permute-start | bytes 1572872 | tf_op jit(solution)/shard_map/ppermute | solution.py:23
  36.5 0.7 copy-start.3
  44.0 12.7 %copy-start.4 = (f32[512,128]{1,0:T(8,128)S(1)}, f32[512,128]{1,0:T(8,128)}, u32[]{:S(2)}) copy-start(f32[512,128]{1,0:T(8,128)} %copy-done.3) | copy-start | bytes 786436
  46.1 10.6 %collective-permute-start.5 = (f32[1024,128]{1,0:T(8,128)}, f32[1024,128]{1,0:T(8,128)S(1)}, u32[]{:S(2)}, u32[]{:S(2)}) collective-permute-start(f32[1024,128]{1,0:T(8,128)} %shard_map.43.refs_0_), channel_id=1, source_target_pairs={{0,1},{1,0},{2,3},{3,2},{4,5},{5,4},{6,7},{7,6},{8,9},{9,8},{10,11... | collective-permute-start | bytes 1572872 | tf_op jit(solution)/shard_map/ppermute | solution.py:23
  46.1 10.6 %collective-permute-start.6 = (f32[512,128]{1,0:T(8,128)S(1)}, f32[512,128]{1,0:T(8,128)S(1)}, u32[]{:S(2)}, u32[]{:S(2)}) collective-permute-start(f32[512,128]{1,0:T(8,128)S(1)} %slice_select_fusion.refs_2_), channel_id=1, source_target_pairs={{4,0},{8,4},{12,8},{16,12},{20,16},{24,20},{28,24},{5,1},{9,5},{13... | collective-permute-start | bytes 786440 | tf_op jit(solution)/shard_map/ppermute | solution.py:71
  56.7 1.0 copy-start.2
  63.2 9.5 %collective-permute-start.7 = (f32[576,128]{1,0:T(8,128)S(1)}, f32[576,128]{1,0:T(8,128)S(1)}, u32[]{:S(2)}, u32[]{:S(2)}) collective-permute-start(f32[576,128]{1,0:T(8,128)S(1)} %constant_dynamic-slice_fusion.2), channel_id=1, source_target_pairs={{0,4},{4,0},{8,12},{12,8},{16,20},{20,16},{24,28},{28,24},{1,5},{5... | collective-permute-start | bytes 884744 | tf_op jit(solution)/shard_map/ppermute | solution.py:23
  72.9 5.2 %collective-permute-start.8 = (f32[288,128]{1,0:T(8,128)S(1)}, f32[288,128]{1,0:T(8,128)S(1)}, u32[]{:S(2)}, u32[]{:S(2)}) collective-permute-start(f32[288,128]{1,0:T(8,128)S(1)} %constant_dynamic-slice_fusion.1), channel_id=1, source_target_pairs={{0,8},{4,12},{8,0},{12,4},{16,24},{20,28},{24,16},{28,20},{1,9},{5... | collective-permute-start | bytes 442376 | tf_op jit(solution)/shard_map/ppermute | solution.py:23
  78.1 5.3 %collective-permute-start.9 = (f32[144,128]{1,0:T(8,128)S(1)}, f32[144,128]{1,0:T(8,128)S(1)}, u32[]{:S(2)}, u32[]{:S(2)}) collective-permute-start(f32[144,128]{1,0:T(8,128)S(1)} %constant_dynamic-slice_fusion), channel_id=1, source_target_pairs={{0,16},{4,20},{8,24},{12,28},{16,0},{20,4},{24,8},{28,12},{1,17},{... | collective-permute-start | bytes 221192 | tf_op jit(solution)/shard_map/ppermute | solution.py:23
  83.4 5.3 %collective-permute-start.10 = (f32[144,128]{1,0:T(8,128)S(1)}, f32[144,128]{1,0:T(8,128)S(1)}, u32[]{:S(2)}, u32[]{:S(2)}) collective-permute-start(f32[144,128]{1,0:T(8,128)S(1)} %dynamic-slice_add_fusion.2), channel_id=1, source_target_pairs={{0,16},{4,20},{8,24},{12,28},{16,0},{20,4},{24,8},{28,12},{1,17},{... | collective-permute-start | bytes 221192 | tf_op jit(solution)/shard_map/ppermute | solution.py:23
  88.8 6.3 %collective-permute-start.11 = (f32[288,128]{1,0:T(8,128)S(1)}, f32[288,128]{1,0:T(8,128)S(1)}, u32[]{:S(2)}, u32[]{:S(2)}) collective-permute-start(f32[288,128]{1,0:T(8,128)S(1)} %pad_maximum_fusion.3), channel_id=1, source_target_pairs={{0,8},{4,12},{8,0},{12,4},{16,24},{20,28},{24,16},{28,20},{1,9},{5... | collective-permute-start | bytes 442376 | tf_op jit(solution)/shard_map/ppermute | solution.py:23
  95.1 6.8 %collective-permute-start.12 = (f32[576,128]{1,0:T(8,128)S(1)}, f32[576,128]{1,0:T(8,128)S(1)}, u32[]{:S(2)}, u32[]{:S(2)}) collective-permute-start(f32[576,128]{1,0:T(8,128)S(1)} %pad_maximum_fusion.2), channel_id=1, source_target_pairs={{0,4},{4,0},{8,12},{12,8},{16,20},{20,16},{24,28},{28,24},{1,5},{5... | collective-permute-start | bytes 884744 | tf_op jit(solution)/shard_map/ppermute | solution.py:23
  102.0 9.9 %collective-permute-start.13 = (f32[1152,128]{1,0:T(8,128)S(1)}, f32[1152,128]{1,0:T(8,128)S(1)}, u32[]{:S(2)}, u32[]{:S(2)}) collective-permute-start(f32[1152,128]{1,0:T(8,128)S(1)} %pad_maximum_fusion.1), channel_id=1, source_target_pairs={{0,2},{1,3},{2,0},{3,1},{4,6},{5,7},{6,4},{7,5},{8,10},{9,11},{10,... | collective-permute-start | bytes 1769480 | tf_op jit(solution)/shard_map/ppermute | solution.py:23
  112.1 2.9 %collective-permute-start.14 = (f32[2304,128]{1,0:T(8,128)S(1)}, f32[2304,128]{1,0:T(8,128)S(1)}, u32[]{:S(2)}, u32[]{:S(2)}) collective-permute-start(f32[2304,128]{1,0:T(8,128)S(1)} %pad_maximum_fusion.mine_ref), channel_id=1, source_target_pairs={{0,1},{1,0},{2,3},{3,2},{4,5},{5,4},{6,7},{7,6},{8,9},{9,8},{10,11... | collective-permute-start | bytes 3538952 | tf_op jit(solution)/shard_map/ppermute | solution.py:23

commit v4 on v3

--- a/solution.py
+++ b/solution.py
@@ -14,6 +14,7 @@
 BLOCK = 128
 GROUP = 8
 SPAN = 4
+CHUNKS = 2
 HIGHEST = lax.Precision.HIGHEST
 CONTRACT_ROWS = (((0,), (0,)), ((), ()))
 
@@ -66,6 +67,25 @@
     )(left, right, *earlier)
 
 
+def add_parts_kernel(left_ref, right_ref, *out_refs):
+    start = 0
+    for out_ref in out_refs:
+        here = slice(start, start + out_ref.shape[0])
+        out_ref[...] = left_ref[here, :] + right_ref[here, :]
+        start += out_ref.shape[0]
+
+
+def add_parts(left, right, parts):
+    vmem = pl.BlockSpec(memory_space=pltpu.VMEM)
+    part = jax.ShapeDtypeStruct((left.shape[0] // parts, left.shape[1]), left.dtype)
+    return pl.pallas_call(
+        add_parts_kernel,
+        out_shape=(part,) * parts,
+        in_specs=[vmem, vmem],
+        out_specs=(vmem,) * parts,
+    )(left, right)
+
+
 def first_rows_of_next(rows):
     count = lax.axis_size("tm")
     return lax.ppermute(rows, "tm", [(i, i - 1) for i in range(1, count)])
@@ -83,16 +103,17 @@
     )
 
 
-def project(signals, channel_node, first, rows, half):
-    channels = signals.shape[1]
-    step = min(512, rows // 2)
-    steps = rows // 2 // step
+def project(signals, channel_node, half):
+    rows, channels = signals.shape
+    part = rows // CHUNKS // 2
+    step = min(512, part)
+    steps = part // step
     grid_spec = pltpu.PrefetchScalarGridSpec(
         num_scalar_prefetch=1,
-        grid=(steps,),
+        grid=(CHUNKS * steps,),
         in_specs=[
             pl.BlockSpec((1, channels), lambda i, half: (0, 0)),
-            pl.BlockSpec((step, channels), lambda i, half: (first // step + half[0] * steps + i, 0)),
+            pl.BlockSpec((step, channels), lambda i, half: ((i // steps * 2 + half[0]) * steps + i % steps, 0)),
         ],
         out_specs=pl.BlockSpec((step, NODES), lambda i, half: (i, 0)),
         scratch_shapes=[pltpu.VMEM((NODES, channels), jnp.bfloat16)],
@@ -101,11 +122,10 @@
         project_kernel,
         out_shape=jax.ShapeDtypeStruct((rows // 2, NODES), jnp.float32),
         grid_spec=grid_spec,
-        cost_estimate=pl.CostEstimate(flops=rows * channels * NODES, bytes_accessed=rows * (channels + 2 * NODES), transcendentals=0),
     )(half, channel_node.reshape(1, channels), signals)
 
 
-def gram_kernel(first, last, earlier, half_ref, lags_ref, *refs):
+def gram_kernel(first, last, earlier, chan_ref, all_lags_ref, *refs):
     refs = list(refs)
     mine_ref, other_ref = refs.pop(0), refs.pop(0)
     sum_in_ref, tail_in_ref = (None, None) if first else (refs.pop(0), refs.pop(0))
@@ -116,10 +136,13 @@
     ext_ref, high_ref, low_ref, sum_ref = refs
     half = mine_ref.shape[0]
     lead = 0 if first else MAXLAG
-    lag_count = lags_ref.shape[0]
+    total_lags = all_lags_ref.shape[0]
+    lag_count = sum_ref.shape[1] // NODES
+    lags = [all_lags_ref[lax.rem(2 * chan_ref[0] + i, total_lags)] for i in range(lag_count)]
+    own_half = lax.rem(chan_ref[0], 2)
     step_rows = high_ref.shape[0]
-    own = pl.multiple_of(lead + half_ref[0] * half, math.gcd(lead, half))
-    others = pl.multiple_of(lead + (1 - half_ref[0]) * half, math.gcd(lead, half))
+    own = pl.multiple_of(lead + own_half * half, math.gcd(lead, half))
+    others = pl.multiple_of(lead + (1 - own_half) * half, math.gcd(lead, half))
     ext_ref[pl.ds(own, half), :] = mine_ref[...]
     ext_ref[pl.ds(others, half), :] = other_ref[...]
     end = lead + 2 * half
@@ -137,7 +160,7 @@
         start = i * step_rows
         for lag in range(lag_count):
             for row in range(0, step_rows, part):
-                value = ext_ref[pl.ds(start + row + lags_ref[lag], part), :]
+                value = ext_ref[pl.ds(start + row + lags[lag], part), :]
                 high = value.astype(jnp.bfloat16)
                 high_ref[row : row + part, lag * NODES : (lag + 1) * NODES] = high
                 low_ref[row : row + part, lag * NODES : (lag + 1) * NODES] = (
@@ -161,7 +184,7 @@
             out_ref[j * NODES : (j + 1) * NODES, :] = sum_ref[:NODES, j * NODES : (j + 1) * NODES]
             place = (far + j) * NODES
             out_ref[place : place + NODES, :] = sum_ref[NODES:, (j + 1) * NODES : (j + 2) * NODES]
-        which = half_ref[1]
+        which = jnp.where(4 * chan_ref[0] >= total_lags, 1, 0)
         row = pl.multiple_of(which * NODES, NODES)
         column = pl.multiple_of((far + which) * NODES, NODES)
         out_ref[2 * far * NODES :, :] = sum_ref[pl.ds(row, NODES), pl.ds(column, NODES)]
@@ -169,11 +192,11 @@
         out_ref[...] = sum_ref[...]
 
 
-def gram_part(half, lags, mine, other, carried, after, earlier):
+def gram_part(chan, lags, mine, other, carried, after, earlier):
     first, last = carried is None, after is not None
-    count = lags.shape[0]
+    count = lags.shape[0] // 2 + 2
     blocks = 2 * (count - 2) + 1
-    operands = [half, lags, mine, other]
+    operands = [chan, lags, mine, other]
     if not first:
         operands += list(carried)
     if last:
@@ -201,7 +224,6 @@
             pltpu.VMEM((2 * NODES, count * NODES), jnp.float32),
         ],
         compiler_params=pltpu.CompilerParams(vmem_limit_bytes=40 << 20),
-        cost_estimate=pl.CostEstimate(flops=rows * NODES * NODES * count * 12, bytes_accessed=rows * NODES * 4, transcendentals=0),
     )(*operands, *earlier)
 
 
@@ -399,38 +421,29 @@
     )(half, mine, other)
 
 
-CHUNKS = 2
-
-
 def on_device(signals, channel_node, lag_offsets):
-    rows = signals.shape[0]
-    lag_count = lag_offsets.shape[0]
-    chan = lax.axis_index("chan")
-    half = jnp.stack([chan % 2, 4 * chan // lag_count])
-    span = lag_count // 2 + 2
-    lags = lag_offsets[(2 * chan + jnp.arange(span, dtype=jnp.int32)) % lag_count]
-    size = rows // CHUNKS
-    totals, sent = [], []
-    for index in range(CHUNKS):
-        send = project(signals, channel_node, index * size, size, 1 - half)
-        received = swap(send, "chan", 1)
-        keep = project(signals, channel_node, index * size, size, half)
-        totals.append(keep + received)
-        sent.append(swap(totals[-1], "chan", 2))
+    chan = lax.axis_index("chan").reshape(1)
+    half = chan % 2
+    send = project(signals, channel_node, 1 - half)
+    received = swap(send, "chan", 1)
+    keep = project(signals, channel_node, half)
+    totals = add_parts(keep, received, CHUNKS)
+    sent = [swap(total, "chan", 2) for total in totals]
     carried = after = None
     for index in range(CHUNKS):
         first, last = index == 0, index == CHUNKS - 1
-        value = add(totals[index], sent[index], *(totals[1:] if first else (carried[1],)))
+        value = add(totals[index], sent[index], *(() if first else (carried[1], after)))
         other = swap(value, "chan", 1)
         if first:
             head = jnp.where(half[0] == 0, value[:MAXLAG], other[:MAXLAG])
             after = first_rows_of_next(head)
         earlier = (head,) if first else ()
-        carried = gram_part(half, lags, value, other, carried, after if last else None, earlier)
+        carried = gram_part(chan, lag_offsets, value, other, carried, after if last else None, earlier)
     blocks = sum_over_time_blocks(carried)
     blocks = double(blocks, "chan", 2)
     other = swap(blocks, "chan", 1)
-    return cholesky(half, blocks, other, lag_count * NODES, 1.0 / (rows * lax.axis_size("tm")))
+    size = lag_offsets.shape[0] * NODES
+    return cholesky(half, blocks, other, size, 1.0 / (signals.shape[0] * lax.axis_size("tm")))
 
 
 def solution(mesh):

time: 149 us -> 143 us (0.960)
  other arithmetic: 5.05 us -> 1.35 us
  local copies, waits for them, and re-layouts: 3.27 us -> 6.48 us
  waiting for transfers between devices: 59.6 us -> 56.5 us
  Pallas kernels: 59 us -> 57.3 us
    ppermute x1, waiting for transfers between devices: 9.3 us -> 0.01 us  [first_rows_of_next(): return lax.ppermute(rows, 'tm', [(i, i - 1) for i in range(1, count)])]
    ppermute x14 -> x13, waiting for transfers between devices: 50.3 us -> 56.5 us  [swap(): return lax.ppermute(value, axis, [(i, i ^ bit) for i in range(count)])]
    pallas_call x4 -> x2, Pallas kernels: 12.3 us -> 8.32 us  [project(): pl.pallas_call(project_kernel, out_shape=jax.ShapeDtypeStruct((rows // 2,...]
    unnamed x18 -> x22, local copies, waits for them, and re-layouts: 2.56 us -> 6.42 us
    add x2 -> x0, other arithmetic: 3.07 us -> none  [on_device(): totals.append(keep + received)]
    pallas_call x0 -> x1, Pallas kernels: none -> 2.6 us  [add_parts(): pl.pallas_call(add_parts_kernel, out_shape=(part,) * parts, in_specs=[vme...]
    ppermute x14 -> x13, starting transfers between devices: 20.2 us -> 19.5 us  [swap(): return lax.ppermute(value, axis, [(i, i ^ bit) for i in range(count)])]
  transfers between devices with their start and end apart: 15 -> 14, of which waited for: 11 -> 12; matrix products, arithmetic and copies ran while one was open for 3% -> 1% of each run, Pallas kernels for 9% -> 5%
where the time goes in v4:
time: 143 us
  Pallas kernels  57.3 us (40%)
  waiting for transfers between devices  56.5 us (40%)
  starting transfers between devices  20.8 us (15%)
  local copies, waits for them, and re-layouts  6.48 us (5%)
    ppermute x13, waiting for transfers between devices, swap(): return lax.ppermute(value, axis, [(i, i ^ bit) for i in range(count)])  56.5 us
    pallas_call x1, Pallas kernels, cholesky(): pl.pallas_call(functools.partial(cholesky_kernel, scale), out_shape=jax.S...  33.1 us
    ppermute x13, starting transfers between devices, swap(): return lax.ppermute(value, axis, [(i, i ^ bit) for i in range(count)])  19.5 us
    pallas_call x2, Pallas kernels, gram_part(): pl.pallas_call(functools.partial(gram_kernel, first, last, len(earlier)),...  9.16 us
    pallas_call x2, Pallas kernels, project(): pl.pallas_call(project_kernel, out_shape=jax.ShapeDtypeStruct((rows // 2,...  8.32 us
    unnamed x22, local copies, waits for them, and re-layouts  6.42 us
    pallas_call x2, Pallas kernels, add(): pl.pallas_call(add_kernel, out_shape=jax.ShapeDtypeStruct(left.shape, lef...  4.15 us
  transfers between devices with their start and end apart: 14, of which 12 were waited for; matrix products, arithmetic and copies ran while one was open for 1% of the time, Pallas kernels for 5%

profile of v4, /device:TPU:0, one launch (start us, length us, event | category | flops | bytes accessed | tf_op | source)
XLA Modules:
  0.0 142.7 jit_solution(2061227726882126544)
XLA Ops:
  0.0 4.2 %shard_map.38 = f32[2048,128]{1,0:T(8,128)} custom-call(s32[1]{0:T(128)S(6)} %sub.29.half_ref, s32[1,512]{1,0:T(1,128)} %bitcast.3, bf16[4096,512]{1,0:T(8,128)(2,1)} %signals_ref.3), custom_call_target="tpu_custom_call" | custom-call | tf_op jit(solution)/shard_map/pallas_call | solution.py:121
  4.6 4.1 %shard_map.37.left_ref = f32[2048,128]{1,0:T(8,128)} custom-call(s32[1]{0:T(128)S(6)} %select_n.119.half_ref, s32[1,512]{1,0:T(1,128)} %bitcast.4, bf16[4096,512]{1,0:T(8,128)(2,1)} %signals_ref.3), custom_call_target="tpu_custom_call" | custom-call | tf_op jit(solution)/shard_map/pallas_call | solution.py:121
  8.8 1.0 copy-done.7
  9.8 2.6 %shard_map.39 = (f32[1024,128]{1,0:T(8,128)}, f32[1024,128]{1,0:T(8,128)}) custom-call(f32[2048,128]{1,0:T(8,128)} %shard_map.37.left_ref, f32[2048,128]{1,0:T(8,128)} %copy-done.7), custom_call_target="tpu_custom_call" | custom-call | tf_op jit(solution)/shard_map/pallas_call | solution.py:81
  12.4 2.5 %collective-permute-start.2 = (f32[1024,128]{1,0:T(8,128)}, f32[1024,128]{1,0:T(8,128)S(1)}, u32[]{:S(2)}, u32[]{:S(2)}) collective-permute-start(f32[1024,128]{1,0:T(8,128)} %get-tuple-element.10.left_ref), channel_id=1, source_target_pairs={{0,2},{1,3},{2,0},{3,1},{4,6},{5,7},{6,4},{7,5},{8,10},{9,11},{10,... | collective-permute-start | bytes 1572872 | tf_op jit(solution)/shard_map/ppermute | solution.py:24
  14.9 12.8 %collective-permute-done.2.right_ref = f32[1024,128]{1,0:T(8,128)S(1)} collective-permute-done((f32[1024,128]{1,0:T(8,128)}, f32[1024,128]{1,0:T(8,128)S(1)}, u32[]{:S(2)}, u32[]{:S(2)}) %collective-permute-start.2) | collective-permute-done | bytes 524320 | tf_op jit(solution)/shard_map/ppermute | solution.py:24
  28.5 2.1 %shard_map.40.refs_0_ = f32[1024,128]{1,0:T(8,128)} custom-call(f32[1024,128]{1,0:T(8,128)} %get-tuple-element.10.left_ref, f32[1024,128]{1,0:T(8,128)} %copy-done.8), custom_call_target="tpu_custom_call" | custom-call | tf_op jit(solution)/shard_map/pallas_call | solution.py:62
  30.5 1.7 %collective-permute-start.1 = (f32[1024,128]{1,0:T(8,128)S(1)}, f32[1024,128]{1,0:T(8,128)S(1)}, u32[]{:S(2)}, u32[]{:S(2)}) collective-permute-start(f32[1024,128]{1,0:T(8,128)S(1)} %copy-done.9), channel_id=1, source_target_pairs={{0,2},{1,3},{2,0},{3,1},{4,6},{5,7},{6,4},{7,5},{8,10},{9,11},{10,... | collective-permute-start | bytes 1572872 | tf_op jit(solution)/shard_map/ppermute | solution.py:24
  32.7 1.0 slice_select_fusion.refs_2_
  33.6 1.3 collective-permute-start.4
  35.0 1.0 copy-done
  36.0 3.6 %shard_map.41 = (f32[256,768]{1,0:T(8,128)S(1)}, f32[512,128]{1,0:T(8,128)S(1)}) custom-call(s32[1]{0:T(128)} %bitcast.chan_ref, s32[8]{0:T(128)S(1)} %copy-done.6, f32[1024,128]{1,0:T(8,128)S(1)} %copy-done, f32[1024,128]{1,0:T(8,128)S(1)} %collective-permute-done.3.refs_1_, f32[512,128]{1,0:T(8,128)S(1)} %slice_select_fusion.refs_2_), custom_call_target="tpu_custom_call" | custom-call | tf_op jit(solution)/shard_map/pallas_call | solution.py:215
  40.3 4.5 %collective-permute-done.1.right_ref = f32[1024,128]{1,0:T(8,128)S(1)} collective-permute-done((f32[1024,128]{1,0:T(8,128)S(1)}, f32[1024,128]{1,0:T(8,128)S(1)}, u32[]{:S(2)}, u32[]{:S(2)}) %collective-permute-start.1) | collective-permute-done | bytes 524320 | tf_op jit(solution)/shard_map/ppermute | solution.py:24
  45.8 2.1 %shard_map.42.refs_0_ = f32[1024,128]{1,0:T(8,128)} custom-call(f32[1024,128]{1,0:T(8,128)} %get-tuple-element.9.left_ref, f32[1024,128]{1,0:T(8,128)} %copy-done.10, f32[512,128]{1,0:T(8,128)} %copy-done.4, f32[512,128]{1,0:T(8,128)} %copy-done.2), custom_call_target="tpu_custom_call" | custom-call | tf_op jit(solution)/shard_map/pallas_call | solution.py:62
  47.8 2.1 %collective-permute-done.5.refs_1_ = f32[1024,128]{1,0:T(8,128)S(1)} collective-permute-done((f32[1024,128]{1,0:T(8,128)}, f32[1024,128]{1,0:T(8,128)S(1)}, u32[]{:S(2)}, u32[]{:S(2)}) %collective-permute-start.5) | collective-permute-done | bytes 524320 | tf_op jit(solution)/shard_map/ppermute | solution.py:24
  50.0 1.0 copy-done.1
  52.0 5.6 %shard_map.43 = f32[1152,128]{1,0:T(8,128)S(1)} custom-call(s32[1]{0:T(128)} %bitcast.chan_ref, s32[8]{0:T(128)S(1)} %copy-done.6, f32[1024,128]{1,0:T(8,128)S(1)} %copy-done.1, f32[1024,128]{1,0:T(8,128)S(1)} %collective-permute-done.5.refs_1_, f32[256,768]{1,0:T(8,128)S(1)} %get-tuple-element.12.refs_2_, f32[512,128]{1,0:T(8,128)S(1)} %copy-done.5, ...), custom_call_target="tpu_custom_call" | custom-call | tf_op jit(solution)/shard_map/pallas_call | solution.py:215
  57.6 1.8 %collective-permute-start.6 = (f32[576,128]{1,0:T(8,128)S(1)}, f32[576,128]{1,0:T(8,128)S(1)}, u32[]{:S(2)}, u32[]{:S(2)}) collective-permute-start(f32[576,128]{1,0:T(8,128)S(1)} %constant_dynamic-slice_fusion.2), channel_id=1, source_target_pairs={{0,4},{4,0},{8,12},{12,8},{16,20},{20,16},{24,28},{28,24},{1,5},{5... | collective-permute-start | bytes 884744 | tf_op jit(solution)/shard_map/ppermute | solution.py:24
  59.4 7.2 %collective-permute-done.6 = f32[576,128]{1,0:T(8,128)S(1)} collective-permute-done((f32[576,128]{1,0:T(8,128)S(1)}, f32[576,128]{1,0:T(8,128)S(1)}, u32[]{:S(2)}, u32[]{:S(2)}) %collective-permute-start.6) | collective-permute-done | bytes 294944 | tf_op jit(solution)/shard_map/ppermute | solution.py:24
  66.7 1.9 %collective-permute-start.7 = (f32[288,128]{1,0:T(8,128)S(1)}, f32[288,128]{1,0:T(8,128)S(1)}, u32[]{:S(2)}, u32[]{:S(2)}) collective-permute-start(f32[288,128]{1,0:T(8,128)S(1)} %constant_dynamic-slice_fusion.1), channel_id=1, source_target_pairs={{0,8},{4,12},{8,0},{12,4},{16,24},{20,28},{24,16},{28,20},{1,9},{5... | collective-permute-start | bytes 442376 | tf_op jit(solution)/shard_map/ppermute | solution.py:24
  68.6 3.3 %collective-permute-done.7 = f32[288,128]{1,0:T(8,128)S(1)} collective-permute-done((f32[288,128]{1,0:T(8,128)S(1)}, f32[288,128]{1,0:T(8,128)S(1)}, u32[]{:S(2)}, u32[]{:S(2)}) %collective-permute-start.7) | collective-permute-done | bytes 147488 | tf_op jit(solution)/shard_map/ppermute | solution.py:24
  72.0 2.9 %collective-permute-start.8 = (f32[144,128]{1,0:T(8,128)S(1)}, f32[144,128]{1,0:T(8,128)S(1)}, u32[]{:S(2)}, u32[]{:S(2)}) collective-permute-start(f32[144,128]{1,0:T(8,128)S(1)} %constant_dynamic-slice_fusion), channel_id=1, source_target_pairs={{0,16},{4,20},{8,24},{12,28},{16,0},{20,4},{24,8},{28,12},{1,17},{... | collective-permute-start | bytes 221192 | tf_op jit(solution)/shard_map/ppermute | solution.py:24
  74.9 2.4 %collective-permute-done.8 = f32[144,128]{1,0:T(8,128)S(1)} collective-permute-done((f32[144,128]{1,0:T(8,128)S(1)}, f32[144,128]{1,0:T(8,128)S(1)}, u32[]{:S(2)}, u32[]{:S(2)}) %collective-permute-start.8) | collective-permute-done | bytes 73760 | tf_op jit(solution)/shard_map/ppermute | solution.py:24
  77.3 2.9 %collective-permute-start.9 = (f32[144,128]{1,0:T(8,128)S(1)}, f32[144,128]{1,0:T(8,128)S(1)}, u32[]{:S(2)}, u32[]{:S(2)}) collective-permute-start(f32[144,128]{1,0:T(8,128)S(1)} %dynamic-slice_add_fusion.2), channel_id=1, source_target_pairs={{0,16},{4,20},{8,24},{12,28},{16,0},{20,4},{24,8},{28,12},{1,17},{... | collective-permute-start | bytes 221192 | tf_op jit(solution)/shard_map/ppermute | solution.py:24
  80.3 2.7 %collective-permute-done.9 = f32[144,128]{1,0:T(8,128)S(1)} collective-permute-done((f32[144,128]{1,0:T(8,128)S(1)}, f32[144,128]{1,0:T(8,128)S(1)}, u32[]{:S(2)}, u32[]{:S(2)}) %collective-permute-start.9) | collective-permute-done | bytes 73760 | tf_op jit(solution)/shard_map/ppermute | solution.py:24
  83.0 3.5 %collective-permute-start.10 = (f32[288,128]{1,0:T(8,128)S(1)}, f32[288,128]{1,0:T(8,128)S(1)}, u32[]{:S(2)}, u32[]{:S(2)}) collective-permute-start(f32[288,128]{1,0:T(8,128)S(1)} %pad_maximum_fusion.3), channel_id=1, source_target_pairs={{0,8},{4,12},{8,0},{12,4},{16,24},{20,28},{24,16},{28,20},{1,9},{5... | collective-permute-start | bytes 442376 | tf_op jit(solution)/shard_map/ppermute | solution.py:24
  86.5 3.1 %collective-permute-done.10 = f32[288,128]{1,0:T(8,128)S(1)} collective-permute-done((f32[288,128]{1,0:T(8,128)S(1)}, f32[288,128]{1,0:T(8,128)S(1)}, u32[]{:S(2)}, u32[]{:S(2)}) %collective-permute-start.10) | collective-permute-done | bytes 147488 | tf_op jit(solution)/shard_map/ppermute | solution.py:24
  89.7 1.6 %collective-permute-start.11 = (f32[576,128]{1,0:T(8,128)S(1)}, f32[576,128]{1,0:T(8,128)S(1)}, u32[]{:S(2)}, u32[]{:S(2)}) collective-permute-start(f32[576,128]{1,0:T(8,128)S(1)} %pad_maximum_fusion.2), channel_id=1, source_target_pairs={{0,4},{4,0},{8,12},{12,8},{16,20},{20,16},{24,28},{28,24},{1,5},{5... | collective-permute-start | bytes 884744 | tf_op jit(solution)/shard_map/ppermute | solution.py:24
  91.3 5.2 %collective-permute-done.11 = f32[576,128]{1,0:T(8,128)S(1)} collective-permute-done((f32[576,128]{1,0:T(8,128)S(1)}, f32[576,128]{1,0:T(8,128)S(1)}, u32[]{:S(2)}, u32[]{:S(2)}) %collective-permute-start.11) | collective-permute-done | bytes 294944 | tf_op jit(solution)/shard_map/ppermute | solution.py:24
  96.7 9.8 %collective-permute-done.12 = f32[1152,128]{1,0:T(8,128)S(1)} collective-permute-done((f32[1152,128]{1,0:T(8,128)S(1)}, f32[1152,128]{1,0:T(8,128)S(1)}, u32[]{:S(2)}, u32[]{:S(2)}) %collective-permute-start.12) | collective-permute-done | bytes 589856 | tf_op jit(solution)/shard_map/ppermute | solution.py:24
  106.8 2.8 %collective-permute-done.13.other_ref = f32[2304,128]{1,0:T(8,128)S(1)} collective-permute-done((f32[2304,128]{1,0:T(8,128)S(1)}, f32[2304,128]{1,0:T(8,128)S(1)}, u32[]{:S(2)}, u32[]{:S(2)}) %collective-permute-start.13) | collective-permute-done | bytes 1179680 | tf_op jit(solution)/shard_map/ppermute | solution.py:24
  109.6 33.1 %shard_map.44 = f32[1024,1024]{1,0:T(8,128)} custom-call(s32[1]{0:T(128)S(6)} %select_n.119.half_ref, f32[2304,128]{1,0:T(8,128)S(1)} %pad_maximum_fusion.mine_ref, f32[2304,128]{1,0:T(8,128)S(1)} %collective-permute-done.13.other_ref), custom_call_target="tpu_custom_call" | custom-call | tf_op jit(solution)/shard_map/pallas_call | solution.py:409
  (41 shorter events, 4.8 us)
Async XLA Ops:
  4.2 4.6 %collective-permute-start = (f32[2048,128]{1,0:T(8,128)}, f32[2048,128]{1,0:T(8,128)S(1)}, u32[]{:S(2)}, u32[]{:S(2)}) collective-permute-start(f32[2048,128]{1,0:T(8,128)} %shard_map.38), channel_id=1, source_target_pairs={{0,1},{1,0},{2,3},{3,2},{4,5},{5,4},{6,7},{7,6},{8,9},{9,8},{10,11... | collective-permute-start | bytes 3145736 | tf_op jit(solution)/shard_map/ppermute | solution.py:24
  8.8 1.0 copy-start.7
  12.4 18.2 %copy-start.9 = (f32[1024,128]{1,0:T(8,128)S(1)}, f32[1024,128]{1,0:T(8,128)}, u32[]{:S(2)}) copy-start(f32[1024,128]{1,0:T(8,128)} %get-tuple-element.9.left_ref) | copy-start | bytes 1572868
  12.4 22.6 %copy-start.6 = (s32[8]{0:T(128)S(1)}, s32[8]{0:T(128)}, u32[]{:S(2)}) copy-start(s32[8]{0:T(128)} %all_lags_ref.3) | copy-start | bytes 100
  12.4 15.3 %collective-permute-start.2 = (f32[1024,128]{1,0:T(8,128)}, f32[1024,128]{1,0:T(8,128)S(1)}, u32[]{:S(2)}, u32[]{:S(2)}) collective-permute-start(f32[1024,128]{1,0:T(8,128)} %get-tuple-element.10.left_ref), channel_id=1, source_target_pairs={{0,2},{1,3},{2,0},{3,1},{4,6},{5,7},{6,4},{7,5},{8,10},{9,11},{10,... | collective-permute-start | bytes 1572872 | tf_op jit(solution)/shard_map/ppermute | solution.py:24
  27.7 0.8 copy-start.8
  30.5 2.1 %collective-permute-start.3 = (f32[1024,128]{1,0:T(8,128)}, f32[1024,128]{1,0:T(8,128)S(1)}, u32[]{:S(2)}, u32[]{:S(2)}) collective-permute-start(f32[1024,128]{1,0:T(8,128)} %shard_map.40.refs_0_), channel_id=1, source_target_pairs={{0,1},{1,0},{2,3},{3,2},{4,5},{5,4},{6,7},{7,6},{8,9},{9,8},{10,11... | collective-permute-start | bytes 1572872 | tf_op jit(solution)/shard_map/ppermute | solution.py:24
  30.5 14.3 %collective-permute-start.1 = (f32[1024,128]{1,0:T(8,128)S(1)}, f32[1024,128]{1,0:T(8,128)S(1)}, u32[]{:S(2)}, u32[]{:S(2)}) collective-permute-start(f32[1024,128]{1,0:T(8,128)S(1)} %copy-done.9), channel_id=1, source_target_pairs={{0,2},{1,3},{2,0},{3,1},{4,6},{5,7},{6,4},{7,5},{8,10},{9,11},{10,... | collective-permute-start | bytes 1572872 | tf_op jit(solution)/shard_map/ppermute | solution.py:24
  33.6 11.2 %collective-permute-start.4 = (f32[512,128]{1,0:T(8,128)S(1)}, f32[512,128]{1,0:T(8,128)S(1)}, u32[]{:S(2)}, u32[]{:S(2)}) collective-permute-start(f32[512,128]{1,0:T(8,128)S(1)} %slice_select_fusion.refs_2_), channel_id=1, source_target_pairs={{4,0},{8,4},{12,8},{16,12},{20,16},{24,20},{28,24},{5,1},{9,5},{13... | collective-permute-start | bytes 786440 | tf_op jit(solution)/shard_map/ppermute | solution.py:91
  35.0 1.0 copy-start
  39.6 0.7 copy-start.4
  44.9 0.8 copy-start.10
  44.9 5.1 %copy-start.5 = (f32[512,128]{1,0:T(8,128)S(1)}, f32[512,128]{1,0:T(8,128)}, u32[]{:S(2)}) copy-start(f32[512,128]{1,0:T(8,128)} %copy-done.4) | copy-start | bytes 786436
  44.9 0.9 copy-start.2
  47.8 2.1 %collective-permute-start.5 = (f32[1024,128]{1,0:T(8,128)}, f32[1024,128]{1,0:T(8,128)S(1)}, u32[]{:S(2)}, u32[]{:S(2)}) collective-permute-start(f32[1024,128]{1,0:T(8,128)} %shard_map.42.refs_0_), channel_id=1, source_target_pairs={{0,1},{1,0},{2,3},{3,2},{4,5},{5,4},{6,7},{7,6},{8,9},{9,8},{10,11... | collective-permute-start | bytes 1572872 | tf_op jit(solution)/shard_map/ppermute | solution.py:24
  50.0 1.0 copy-start.1
  51.0 0.9 copy-start.3
  57.6 9.1 %collective-permute-start.6 = (f32[576,128]{1,0:T(8,128)S(1)}, f32[576,128]{1,0:T(8,128)S(1)}, u32[]{:S(2)}, u32[]{:S(2)}) collective-permute-start(f32[576,128]{1,0:T(8,128)S(1)} %constant_dynamic-slice_fusion.2), channel_id=1, source_target_pairs={{0,4},{4,0},{8,12},{12,8},{16,20},{20,16},{24,28},{28,24},{1,5},{5... | collective-permute-start | bytes 884744 | tf_op jit(solution)/shard_map/ppermute | solution.py:24
  66.7 5.2 %collective-permute-start.7 = (f32[288,128]{1,0:T(8,128)S(1)}, f32[288,128]{1,0:T(8,128)S(1)}, u32[]{:S(2)}, u32[]{:S(2)}) collective-permute-start(f32[288,128]{1,0:T(8,128)S(1)} %constant_dynamic-slice_fusion.1), channel_id=1, source_target_pairs={{0,8},{4,12},{8,0},{12,4},{16,24},{20,28},{24,16},{28,20},{1,9},{5... | collective-permute-start | bytes 442376 | tf_op jit(solution)/shard_map/ppermute | solution.py:24
  72.0 5.3 %collective-permute-start.8 = (f32[144,128]{1,0:T(8,128)S(1)}, f32[144,128]{1,0:T(8,128)S(1)}, u32[]{:S(2)}, u32[]{:S(2)}) collective-permute-start(f32[144,128]{1,0:T(8,128)S(1)} %constant_dynamic-slice_fusion), channel_id=1, source_target_pairs={{0,16},{4,20},{8,24},{12,28},{16,0},{20,4},{24,8},{28,12},{1,17},{... | collective-permute-start | bytes 221192 | tf_op jit(solution)/shard_map/ppermute | solution.py:24
  77.3 5.6 %collective-permute-start.9 = (f32[144,128]{1,0:T(8,128)S(1)}, f32[144,128]{1,0:T(8,128)S(1)}, u32[]{:S(2)}, u32[]{:S(2)}) collective-permute-start(f32[144,128]{1,0:T(8,128)S(1)} %dynamic-slice_add_fusion.2), channel_id=1, source_target_pairs={{0,16},{4,20},{8,24},{12,28},{16,0},{20,4},{24,8},{28,12},{1,17},{... | collective-permute-start | bytes 221192 | tf_op jit(solution)/shard_map/ppermute | solution.py:24
  83.0 6.7 %collective-permute-start.10 = (f32[288,128]{1,0:T(8,128)S(1)}, f32[288,128]{1,0:T(8,128)S(1)}, u32[]{:S(2)}, u32[]{:S(2)}) collective-permute-start(f32[288,128]{1,0:T(8,128)S(1)} %pad_maximum_fusion.3), channel_id=1, source_target_pairs={{0,8},{4,12},{8,0},{12,4},{16,24},{20,28},{24,16},{28,20},{1,9},{5... | collective-permute-start | bytes 442376 | tf_op jit(solution)/shard_map/ppermute | solution.py:24
  89.7 6.8 %collective-permute-start.11 = (f32[576,128]{1,0:T(8,128)S(1)}, f32[576,128]{1,0:T(8,128)S(1)}, u32[]{:S(2)}, u32[]{:S(2)}) collective-permute-start(f32[576,128]{1,0:T(8,128)S(1)} %pad_maximum_fusion.2), channel_id=1, source_target_pairs={{0,4},{4,0},{8,12},{12,8},{16,20},{20,16},{24,28},{28,24},{1,5},{5... | collective-permute-start | bytes 884744 | tf_op jit(solution)/shard_map/ppermute | solution.py:24
  96.6 9.9 %collective-permute-start.12 = (f32[1152,128]{1,0:T(8,128)S(1)}, f32[1152,128]{1,0:T(8,128)S(1)}, u32[]{:S(2)}, u32[]{:S(2)}) collective-permute-start(f32[1152,128]{1,0:T(8,128)S(1)} %pad_maximum_fusion.1), channel_id=1, source_target_pairs={{0,2},{1,3},{2,0},{3,1},{4,6},{5,7},{6,4},{7,5},{8,10},{9,11},{10,... | collective-permute-start | bytes 1769480 | tf_op jit(solution)/shard_map/ppermute | solution.py:24
  106.7 2.9 %collective-permute-start.13 = (f32[2304,128]{1,0:T(8,128)S(1)}, f32[2304,128]{1,0:T(8,128)S(1)}, u32[]{:S(2)}, u32[]{:S(2)}) collective-permute-start(f32[2304,128]{1,0:T(8,128)S(1)} %pad_maximum_fusion.mine_ref), channel_id=1, source_target_pairs={{0,1},{1,0},{2,3},{3,2},{4,5},{5,4},{6,7},{7,6},{8,9},{9,8},{10,11... | collective-permute-start | bytes 3538952 | tf_op jit(solution)/shard_map/ppermute | solution.py:24

commit v5 on v4

--- a/solution.py
+++ b/solution.py
@@ -64,6 +64,7 @@
         out_shape=jax.ShapeDtypeStruct(left.shape, left.dtype),
         in_specs=[vmem, vmem] + [pl.BlockSpec(memory_space=pl.ANY)] * len(earlier),
         out_specs=vmem,
+        compiler_params=pltpu.CompilerParams(vmem_limit_bytes=8 << 20),
     )(left, right, *earlier)
 
 
@@ -83,6 +84,7 @@
         out_shape=(part,) * parts,
         in_specs=[vmem, vmem],
         out_specs=(vmem,) * parts,
+        compiler_params=pltpu.CompilerParams(vmem_limit_bytes=8 << 20),
     )(left, right)
 
 
@@ -122,6 +124,7 @@
         project_kernel,
         out_shape=jax.ShapeDtypeStruct((rows // 2, NODES), jnp.float32),
         grid_spec=grid_spec,
+        compiler_params=pltpu.CompilerParams(vmem_limit_bytes=8 << 20),
     )(half, channel_node.reshape(1, channels), signals)
 
 
@@ -223,7 +226,7 @@
             pltpu.VMEM((step_rows, count * NODES), jnp.bfloat16),
             pltpu.VMEM((2 * NODES, count * NODES), jnp.float32),
         ],
-        compiler_params=pltpu.CompilerParams(vmem_limit_bytes=40 << 20),
+        compiler_params=pltpu.CompilerParams(vmem_limit_bytes=12 << 20),
     )(*operands, *earlier)
 
 
@@ -417,7 +420,7 @@
             pltpu.VMEM((BLOCK, size), jnp.float32),
             pltpu.VMEM((BLOCK, BLOCK), jnp.float32),
         ],
-        compiler_params=pltpu.CompilerParams(vmem_limit_bytes=48 << 20),
+        compiler_params=pltpu.CompilerParams(vmem_limit_bytes=24 << 20),
     )(half, mine, other)
 
 

time: 143 us -> 130 us (0.909)
  Pallas kernels: 57.3 us -> 45.1 us
  local copies, waits for them, and re-layouts: 6.48 us -> 3.33 us
  waiting for transfers between devices: 56.5 us -> 58.9 us
    pallas_call x2, Pallas kernels: 8.32 us -> 2.54 us  [project(): pl.pallas_call(project_kernel, out_shape=jax.ShapeDtypeStruct((rows // 2,...]
    pallas_call x2, Pallas kernels: 4.15 us -> 0.11 us  [add(): pl.pallas_call(add_kernel, out_shape=jax.ShapeDtypeStruct(left.shape, lef...]
    unnamed x22 -> x10, local copies, waits for them, and re-layouts: 6.42 us -> 3.27 us
    pallas_call x1, Pallas kernels: 2.6 us -> 0.14 us  [add_parts(): pl.pallas_call(add_parts_kernel, out_shape=(part,) * parts, in_specs=[vme...]
    ppermute x13, waiting for transfers between devices: 56.5 us -> 58.9 us  [swap(): return lax.ppermute(value, axis, [(i, i ^ bit) for i in range(count)])]
  transfers between devices with their start and end apart: 14 -> 14, of which waited for: 12 -> 13; matrix products, arithmetic and copies ran while one was open for 1% -> 0% of each run, Pallas kernels for 5% -> 4%
where the time goes in v5:
time: 130 us
  waiting for transfers between devices  58.9 us (45%)
  Pallas kernels  45.1 us (35%)
  starting transfers between devices  21.5 us (17%)
  local copies, waits for them, and re-layouts  3.33 us (3%)
    ppermute x13, waiting for transfers between devices, swap(): return lax.ppermute(value, axis, [(i, i ^ bit) for i in range(count)])  58.9 us
    pallas_call x1, Pallas kernels, cholesky(): pl.pallas_call(functools.partial(cholesky_kernel, scale), out_shape=jax.S...  33.1 us
    ppermute x13, starting transfers between devices, swap(): return lax.ppermute(value, axis, [(i, i ^ bit) for i in range(count)])  20.2 us
    pallas_call x2, Pallas kernels, gram_part(): pl.pallas_call(functools.partial(gram_kernel, first, last, len(earlier)),...  9.24 us
    unnamed x10, local copies, waits for them, and re-layouts  3.27 us
  transfers between devices with their start and end apart: 14, of which 13 were waited for; matrix products, arithmetic and copies ran while one was open for 0% of the time, Pallas kernels for 4%

profile of v5, /device:TPU:0, one launch (start us, length us, event | category | flops | bytes accessed | tf_op | source)
XLA Modules:
  0.0 129.5 jit_solution(13120822462981811591)
XLA Ops:
  0.0 2.2 %copy-done = bf16[4096,512]{1,0:T(8,128)(2,1)S(1)} copy-done((bf16[4096,512]{1,0:T(8,128)(2,1)S(1)}, bf16[4096,512]{1,0:T(8,128)(2,1)}, u32[]{:S(2)}) %copy-start) | copy-done | bytes 4194328
  2.2 0.7 copy-done.2
  2.9 1.3 shard_map.38
  4.2 0.5 collective-permute-start
  4.7 0.4 copy-done.1
  5.1 1.3 shard_map.37.left_ref
  6.3 0.6 collective-permute-done.right_ref
  7.0 0.1 shard_map.39
  7.1 2.9 %collective-permute-start.2 = (f32[1024,128]{1,0:T(8,128)S(1)}, f32[1024,128]{1,0:T(8,128)S(1)}, u32[]{:S(2)}, u32[]{:S(2)}) collective-permute-start(f32[1024,128]{1,0:T(8,128)S(1)} %get-tuple-element.10.left_ref), channel_id=1, source_target_pairs={{0,2},{1,3},{2,0},{3,1},{4,6},{5,7},{6,4},{7,5},{8,10},{9,11},{10,... | collective-permute-start | bytes 1572872 | tf_op jit(solution)/shard_map/ppermute | solution.py:24
  10.0 12.2 %collective-permute-done.2.right_ref = f32[1024,128]{1,0:T(8,128)S(1)} collective-permute-done((f32[1024,128]{1,0:T(8,128)S(1)}, f32[1024,128]{1,0:T(8,128)S(1)}, u32[]{:S(2)}, u32[]{:S(2)}) %collective-permute-start.2) | collective-permute-done | bytes 524320 | tf_op jit(solution)/shard_map/ppermute | solution.py:24
  22.4 1.8 %collective-permute-start.1 = (f32[1024,128]{1,0:T(8,128)S(1)}, f32[1024,128]{1,0:T(8,128)S(1)}, u32[]{:S(2)}, u32[]{:S(2)}) collective-permute-start(f32[1024,128]{1,0:T(8,128)S(1)} %get-tuple-element.9.left_ref), channel_id=1, source_target_pairs={{0,2},{1,3},{2,0},{3,1},{4,6},{5,7},{6,4},{7,5},{8,10},{9,11},{10,... | collective-permute-start | bytes 1572872 | tf_op jit(solution)/shard_map/ppermute | solution.py:24
  24.3 1.3 collective-permute-start.4
  25.6 3.6 %shard_map.41 = (f32[256,768]{1,0:T(8,128)S(1)}, f32[512,128]{1,0:T(8,128)S(1)}) custom-call(s32[1]{0:T(128)} %bitcast.chan_ref, s32[8]{0:T(128)S(1)} %copy-done.4, f32[1024,128]{1,0:T(8,128)S(1)} %shard_map.40.refs_0_, f32[1024,128]{1,0:T(8,128)S(1)} %collective-permute-done.3.refs_1_, f32[512,128]{1,0:T(8,128)S(1)} %slice_select_fusion.refs_2_), custom_call_target="tpu_custom_call" | custom-call | tf_op jit(solution)/shard_map/pallas_call | solution.py:218
  29.3 7.4 %collective-permute-done.1.right_ref = f32[1024,128]{1,0:T(8,128)S(1)} collective-permute-done((f32[1024,128]{1,0:T(8,128)S(1)}, f32[1024,128]{1,0:T(8,128)S(1)}, u32[]{:S(2)}, u32[]{:S(2)}) %collective-permute-start.1) | collective-permute-done | bytes 524320 | tf_op jit(solution)/shard_map/ppermute | solution.py:24
  36.9 1.9 %collective-permute-done.5.refs_1_ = f32[1024,128]{1,0:T(8,128)S(1)} collective-permute-done((f32[1024,128]{1,0:T(8,128)S(1)}, f32[1024,128]{1,0:T(8,128)S(1)}, u32[]{:S(2)}, u32[]{:S(2)}) %collective-permute-start.5) | collective-permute-done | bytes 524320 | tf_op jit(solution)/shard_map/ppermute | solution.py:24
  38.8 5.6 %shard_map.43 = f32[1152,128]{1,0:T(8,128)S(1)} custom-call(s32[1]{0:T(128)} %bitcast.chan_ref, s32[8]{0:T(128)S(1)} %copy-done.4, f32[1024,128]{1,0:T(8,128)S(1)} %shard_map.42.refs_0_, f32[1024,128]{1,0:T(8,128)S(1)} %collective-permute-done.5.refs_1_, f32[256,768]{1,0:T(8,128)S(1)} %get-tuple-element.12.refs_2_, ...), custom_call_target="tpu_custom_call" | custom-call | tf_op jit(solution)/shard_map/pallas_call | solution.py:218
  44.4 1.8 %collective-permute-start.6 = (f32[576,128]{1,0:T(8,128)S(1)}, f32[576,128]{1,0:T(8,128)S(1)}, u32[]{:S(2)}, u32[]{:S(2)}) collective-permute-start(f32[576,128]{1,0:T(8,128)S(1)} %constant_dynamic-slice_fusion.2), channel_id=1, source_target_pairs={{0,4},{4,0},{8,12},{12,8},{16,20},{20,16},{24,28},{28,24},{1,5},{5... | collective-permute-start | bytes 884744 | tf_op jit(solution)/shard_map/ppermute | solution.py:24
  46.2 7.2 %collective-permute-done.6 = f32[576,128]{1,0:T(8,128)S(1)} collective-permute-done((f32[576,128]{1,0:T(8,128)S(1)}, f32[576,128]{1,0:T(8,128)S(1)}, u32[]{:S(2)}, u32[]{:S(2)}) %collective-permute-start.6) | collective-permute-done | bytes 294944 | tf_op jit(solution)/shard_map/ppermute | solution.py:24
  53.5 1.9 %collective-permute-start.7 = (f32[288,128]{1,0:T(8,128)S(1)}, f32[288,128]{1,0:T(8,128)S(1)}, u32[]{:S(2)}, u32[]{:S(2)}) collective-permute-start(f32[288,128]{1,0:T(8,128)S(1)} %constant_dynamic-slice_fusion.1), channel_id=1, source_target_pairs={{0,8},{4,12},{8,0},{12,4},{16,24},{20,28},{24,16},{28,20},{1,9},{5... | collective-permute-start | bytes 442376 | tf_op jit(solution)/shard_map/ppermute | solution.py:24
  55.4 3.3 %collective-permute-done.7 = f32[288,128]{1,0:T(8,128)S(1)} collective-permute-done((f32[288,128]{1,0:T(8,128)S(1)}, f32[288,128]{1,0:T(8,128)S(1)}, u32[]{:S(2)}, u32[]{:S(2)}) %collective-permute-start.7) | collective-permute-done | bytes 147488 | tf_op jit(solution)/shard_map/ppermute | solution.py:24
  58.8 2.9 %collective-permute-start.8 = (f32[144,128]{1,0:T(8,128)S(1)}, f32[144,128]{1,0:T(8,128)S(1)}, u32[]{:S(2)}, u32[]{:S(2)}) collective-permute-start(f32[144,128]{1,0:T(8,128)S(1)} %constant_dynamic-slice_fusion), channel_id=1, source_target_pairs={{0,16},{4,20},{8,24},{12,28},{16,0},{20,4},{24,8},{28,12},{1,17},{... | collective-permute-start | bytes 221192 | tf_op jit(solution)/shard_map/ppermute | solution.py:24
  61.7 2.4 %collective-permute-done.8 = f32[144,128]{1,0:T(8,128)S(1)} collective-permute-done((f32[144,128]{1,0:T(8,128)S(1)}, f32[144,128]{1,0:T(8,128)S(1)}, u32[]{:S(2)}, u32[]{:S(2)}) %collective-permute-start.8) | collective-permute-done | bytes 73760 | tf_op jit(solution)/shard_map/ppermute | solution.py:24
  64.1 2.9 %collective-permute-start.9 = (f32[144,128]{1,0:T(8,128)S(1)}, f32[144,128]{1,0:T(8,128)S(1)}, u32[]{:S(2)}, u32[]{:S(2)}) collective-permute-start(f32[144,128]{1,0:T(8,128)S(1)} %dynamic-slice_add_fusion.2), channel_id=1, source_target_pairs={{0,16},{4,20},{8,24},{12,28},{16,0},{20,4},{24,8},{28,12},{1,17},{... | collective-permute-start | bytes 221192 | tf_op jit(solution)/shard_map/ppermute | solution.py:24
  67.1 2.7 %collective-permute-done.9 = f32[144,128]{1,0:T(8,128)S(1)} collective-permute-done((f32[144,128]{1,0:T(8,128)S(1)}, f32[144,128]{1,0:T(8,128)S(1)}, u32[]{:S(2)}, u32[]{:S(2)}) %collective-permute-start.9) | collective-permute-done | bytes 73760 | tf_op jit(solution)/shard_map/ppermute | solution.py:24
  69.8 3.6 %collective-permute-start.10 = (f32[288,128]{1,0:T(8,128)S(1)}, f32[288,128]{1,0:T(8,128)S(1)}, u32[]{:S(2)}, u32[]{:S(2)}) collective-permute-start(f32[288,128]{1,0:T(8,128)S(1)} %pad_maximum_fusion.3), channel_id=1, source_target_pairs={{0,8},{4,12},{8,0},{12,4},{16,24},{20,28},{24,16},{28,20},{1,9},{5... | collective-permute-start | bytes 442376 | tf_op jit(solution)/shard_map/ppermute | solution.py:24
  73.3 3.1 %collective-permute-done.10 = f32[288,128]{1,0:T(8,128)S(1)} collective-permute-done((f32[288,128]{1,0:T(8,128)S(1)}, f32[288,128]{1,0:T(8,128)S(1)}, u32[]{:S(2)}, u32[]{:S(2)}) %collective-permute-start.10) | collective-permute-done | bytes 147488 | tf_op jit(solution)/shard_map/ppermute | solution.py:24
  76.5 1.6 %collective-permute-start.11 = (f32[576,128]{1,0:T(8,128)S(1)}, f32[576,128]{1,0:T(8,128)S(1)}, u32[]{:S(2)}, u32[]{:S(2)}) collective-permute-start(f32[576,128]{1,0:T(8,128)S(1)} %pad_maximum_fusion.2), channel_id=1, source_target_pairs={{0,4},{4,0},{8,12},{12,8},{16,20},{20,16},{24,28},{28,24},{1,5},{5... | collective-permute-start | bytes 884744 | tf_op jit(solution)/shard_map/ppermute | solution.py:24
  78.1 5.2 %collective-permute-done.11 = f32[576,128]{1,0:T(8,128)S(1)} collective-permute-done((f32[576,128]{1,0:T(8,128)S(1)}, f32[576,128]{1,0:T(8,128)S(1)}, u32[]{:S(2)}, u32[]{:S(2)}) %collective-permute-start.11) | collective-permute-done | bytes 294944 | tf_op jit(solution)/shard_map/ppermute | solution.py:24
  83.4 0.1 collective-permute-start.12
  83.5 9.8 %collective-permute-done.12 = f32[1152,128]{1,0:T(8,128)S(1)} collective-permute-done((f32[1152,128]{1,0:T(8,128)S(1)}, f32[1152,128]{1,0:T(8,128)S(1)}, u32[]{:S(2)}, u32[]{:S(2)}) %collective-permute-start.12) | collective-permute-done | bytes 589856 | tf_op jit(solution)/shard_map/ppermute | solution.py:24
  93.6 2.8 %collective-permute-done.13.other_ref = f32[2304,128]{1,0:T(8,128)S(1)} collective-permute-done((f32[2304,128]{1,0:T(8,128)S(1)}, f32[2304,128]{1,0:T(8,128)S(1)}, u32[]{:S(2)}, u32[]{:S(2)}) %collective-permute-start.13) | collective-permute-done | bytes 1179680 | tf_op jit(solution)/shard_map/ppermute | solution.py:24
  96.4 33.1 %shard_map.44 = f32[1024,1024]{1,0:T(8,128)} custom-call(s32[1]{0:T(128)S(6)} %select_n.119.half_ref, f32[2304,128]{1,0:T(8,128)S(1)} %pad_maximum_fusion.mine_ref, f32[2304,128]{1,0:T(8,128)S(1)} %collective-permute-done.13.other_ref), custom_call_target="tpu_custom_call" | custom-call | tf_op jit(solution)/shard_map/pallas_call | solution.py:412
  (29 shorter events, 0.9 us)
Async XLA Ops:
  0.0 2.2 %copy-start = (bf16[4096,512]{1,0:T(8,128)(2,1)S(1)}, bf16[4096,512]{1,0:T(8,128)(2,1)}, u32[]{:S(2)}) copy-start(bf16[4096,512]{1,0:T(8,128)(2,1)} %signals_ref.3) | copy-start | bytes 12582916
  2.2 0.7 copy-start.2
  2.9 2.2 %copy-start.1 = (bf16[4096,512]{1,0:T(8,128)(2,1)S(1)}, bf16[4096,512]{1,0:T(8,128)(2,1)}, u32[]{:S(2)}) copy-start(bf16[4096,512]{1,0:T(8,128)(2,1)} %signals_ref.3) | copy-start | bytes 12582916
  2.9 2.2 %copy-start.3 = (s32[512]{0:T(512)S(1)}, s32[512]{0:T(512)}, u32[]{:S(2)}) copy-start(s32[512]{0:T(512)} %param.4) | copy-start | bytes 6148
  4.2 2.8 %collective-permute-start = (f32[2048,128]{1,0:T(8,128)S(1)}, f32[2048,128]{1,0:T(8,128)S(1)}, u32[]{:S(2)}, u32[]{:S(2)}) collective-permute-start(f32[2048,128]{1,0:T(8,128)S(1)} %shard_map.38), channel_id=1, source_target_pairs={{0,1},{1,0},{2,3},{3,2},{4,5},{5,4},{6,7},{7,6},{8,9},{9,8},{10,11... | collective-permute-start | bytes 3145736 | tf_op jit(solution)/shard_map/ppermute | solution.py:24
  7.1 18.5 %copy-start.4 = (s32[8]{0:T(128)S(1)}, s32[8]{0:T(128)}, u32[]{:S(2)}) copy-start(s32[8]{0:T(128)} %all_lags_ref.3) | copy-start | bytes 100
  7.1 15.2 %collective-permute-start.2 = (f32[1024,128]{1,0:T(8,128)S(1)}, f32[1024,128]{1,0:T(8,128)S(1)}, u32[]{:S(2)}, u32[]{:S(2)}) collective-permute-start(f32[1024,128]{1,0:T(8,128)S(1)} %get-tuple-element.10.left_ref), channel_id=1, source_target_pairs={{0,2},{1,3},{2,0},{3,1},{4,6},{5,7},{6,4},{7,5},{8,10},{9,11},{10,... | collective-permute-start | bytes 1572872 | tf_op jit(solution)/shard_map/ppermute | solution.py:24
  22.3 2.0 %collective-permute-start.3 = (f32[1024,128]{1,0:T(8,128)S(1)}, f32[1024,128]{1,0:T(8,128)S(1)}, u32[]{:S(2)}, u32[]{:S(2)}) collective-permute-start(f32[1024,128]{1,0:T(8,128)S(1)} %shard_map.40.refs_0_), channel_id=1, source_target_pairs={{0,1},{1,0},{2,3},{3,2},{4,5},{5,4},{6,7},{7,6},{8,9},{9,8},{10,11... | collective-permute-start | bytes 1572872 | tf_op jit(solution)/shard_map/ppermute | solution.py:24
  22.4 14.3 %collective-permute-start.1 = (f32[1024,128]{1,0:T(8,128)S(1)}, f32[1024,128]{1,0:T(8,128)S(1)}, u32[]{:S(2)}, u32[]{:S(2)}) collective-permute-start(f32[1024,128]{1,0:T(8,128)S(1)} %get-tuple-element.9.left_ref), channel_id=1, source_target_pairs={{0,2},{1,3},{2,0},{3,1},{4,6},{5,7},{6,4},{7,5},{8,10},{9,11},{10,... | collective-permute-start | bytes 1572872 | tf_op jit(solution)/shard_map/ppermute | solution.py:24
  24.3 12.4 %collective-permute-start.4 = (f32[512,128]{1,0:T(8,128)S(1)}, f32[512,128]{1,0:T(8,128)S(1)}, u32[]{:S(2)}, u32[]{:S(2)}) collective-permute-start(f32[512,128]{1,0:T(8,128)S(1)} %slice_select_fusion.refs_2_), channel_id=1, source_target_pairs={{4,0},{8,4},{12,8},{16,12},{20,16},{24,20},{28,24},{5,1},{9,5},{13... | collective-permute-start | bytes 786440 | tf_op jit(solution)/shard_map/ppermute | solution.py:93
  36.8 2.0 %collective-permute-start.5 = (f32[1024,128]{1,0:T(8,128)S(1)}, f32[1024,128]{1,0:T(8,128)S(1)}, u32[]{:S(2)}, u32[]{:S(2)}) collective-permute-start(f32[1024,128]{1,0:T(8,128)S(1)} %shard_map.42.refs_0_), channel_id=1, source_target_pairs={{0,1},{1,0},{2,3},{3,2},{4,5},{5,4},{6,7},{7,6},{8,9},{9,8},{10,11... | collective-permute-start | bytes 1572872 | tf_op jit(solution)/shard_map/ppermute | solution.py:24
  44.4 9.1 %collective-permute-start.6 = (f32[576,128]{1,0:T(8,128)S(1)}, f32[576,128]{1,0:T(8,128)S(1)}, u32[]{:S(2)}, u32[]{:S(2)}) collective-permute-start(f32[576,128]{1,0:T(8,128)S(1)} %constant_dynamic-slice_fusion.2), channel_id=1, source_target_pairs={{0,4},{4,0},{8,12},{12,8},{16,20},{20,16},{24,28},{28,24},{1,5},{5... | collective-permute-start | bytes 884744 | tf_op jit(solution)/shard_map/ppermute | solution.py:24
  53.5 5.2 %collective-permute-start.7 = (f32[288,128]{1,0:T(8,128)S(1)}, f32[288,128]{1,0:T(8,128)S(1)}, u32[]{:S(2)}, u32[]{:S(2)}) collective-permute-start(f32[288,128]{1,0:T(8,128)S(1)} %constant_dynamic-slice_fusion.1), channel_id=1, source_target_pairs={{0,8},{4,12},{8,0},{12,4},{16,24},{20,28},{24,16},{28,20},{1,9},{5... | collective-permute-start | bytes 442376 | tf_op jit(solution)/shard_map/ppermute | solution.py:24
  58.8 5.3 %collective-permute-start.8 = (f32[144,128]{1,0:T(8,128)S(1)}, f32[144,128]{1,0:T(8,128)S(1)}, u32[]{:S(2)}, u32[]{:S(2)}) collective-permute-start(f32[144,128]{1,0:T(8,128)S(1)} %constant_dynamic-slice_fusion), channel_id=1, source_target_pairs={{0,16},{4,20},{8,24},{12,28},{16,0},{20,4},{24,8},{28,12},{1,17},{... | collective-permute-start | bytes 221192 | tf_op jit(solution)/shard_map/ppermute | solution.py:24
  64.1 5.6 %collective-permute-start.9 = (f32[144,128]{1,0:T(8,128)S(1)}, f32[144,128]{1,0:T(8,128)S(1)}, u32[]{:S(2)}, u32[]{:S(2)}) collective-permute-start(f32[144,128]{1,0:T(8,128)S(1)} %dynamic-slice_add_fusion.2), channel_id=1, source_target_pairs={{0,16},{4,20},{8,24},{12,28},{16,0},{20,4},{24,8},{28,12},{1,17},{... | collective-permute-start | bytes 221192 | tf_op jit(solution)/shard_map/ppermute | solution.py:24
  69.8 6.7 %collective-permute-start.10 = (f32[288,128]{1,0:T(8,128)S(1)}, f32[288,128]{1,0:T(8,128)S(1)}, u32[]{:S(2)}, u32[]{:S(2)}) collective-permute-start(f32[288,128]{1,0:T(8,128)S(1)} %pad_maximum_fusion.3), channel_id=1, source_target_pairs={{0,8},{4,12},{8,0},{12,4},{16,24},{20,28},{24,16},{28,20},{1,9},{5... | collective-permute-start | bytes 442376 | tf_op jit(solution)/shard_map/ppermute | solution.py:24
  76.5 6.8 %collective-permute-start.11 = (f32[576,128]{1,0:T(8,128)S(1)}, f32[576,128]{1,0:T(8,128)S(1)}, u32[]{:S(2)}, u32[]{:S(2)}) collective-permute-start(f32[576,128]{1,0:T(8,128)S(1)} %pad_maximum_fusion.2), channel_id=1, source_target_pairs={{0,4},{4,0},{8,12},{12,8},{16,20},{20,16},{24,28},{28,24},{1,5},{5... | collective-permute-start | bytes 884744 | tf_op jit(solution)/shard_map/ppermute | solution.py:24
  83.4 9.9 %collective-permute-start.12 = (f32[1152,128]{1,0:T(8,128)S(1)}, f32[1152,128]{1,0:T(8,128)S(1)}, u32[]{:S(2)}, u32[]{:S(2)}) collective-permute-start(f32[1152,128]{1,0:T(8,128)S(1)} %pad_maximum_fusion.1), channel_id=1, source_target_pairs={{0,2},{1,3},{2,0},{3,1},{4,6},{5,7},{6,4},{7,5},{8,10},{9,11},{10,... | collective-permute-start | bytes 1769480 | tf_op jit(solution)/shard_map/ppermute | solution.py:24
  93.5 2.9 %collective-permute-start.13 = (f32[2304,128]{1,0:T(8,128)S(1)}, f32[2304,128]{1,0:T(8,128)S(1)}, u32[]{:S(2)}, u32[]{:S(2)}) collective-permute-start(f32[2304,128]{1,0:T(8,128)S(1)} %pad_maximum_fusion.mine_ref), channel_id=1, source_target_pairs={{0,1},{1,0},{2,3},{3,2},{4,5},{5,4},{6,7},{7,6},{8,9},{9,8},{10,11... | collective-permute-start | bytes 3538952 | tf_op jit(solution)/shard_map/ppermute | solution.py:24

commit v6 on v5

--- a/solution.py
+++ b/solution.py
@@ -14,7 +14,7 @@
 BLOCK = 128
 GROUP = 8
 SPAN = 4
-CHUNKS = 2
+CHUNK_QUARTERS = (1, 1)
 HIGHEST = lax.Precision.HIGHEST
 CONTRACT_ROWS = (((0,), (0,)), ((), ()))
 
@@ -45,12 +45,35 @@
     return jnp.concatenate([low, high], axis=0)
 
 
-def sum_over_time_blocks(value):
-    for bit in bits_of("tm"):
-        value = halve(value, "tm", bit)
-    for bit in bits_of("tm")[::-1]:
-        value = double(value, "tm", bit)
-    return value
+class Route:
+    def __init__(self, scatter, gather):
+        self.scatter, self.gather = scatter, gather
+
+    def reduce(self, value):
+        for bit in self.scatter:
+            value = halve(value, "tm", bit)
+        for axis, bit in self.gather:
+            value = double(value, axis, bit)
+        return value
+
+    def pieces(self, rows, high):
+        unit = rows >> len(self.scatter)
+        found = []
+        for index in range(1 << len(self.scatter)):
+            value = {("chan", 2): high}
+            for i, bit in enumerate(self.scatter):
+                value["tm", bit] = index >> (len(self.scatter) - 1 - i) & 1
+            place = sum(value[stage] << i for i, stage in enumerate(self.gather))
+            found.append((index * unit, unit, place * unit))
+        return found
+
+
+def routes():
+    bits = bits_of("tm")
+    upper = ("chan", 2)
+    first = Route(bits, [("tm", bit) for bit in bits[::-1]] + [upper])
+    second = Route(bits[1:] + bits[:1], [upper] + [("tm", bit) for bit in bits[:0:-1] + bits[:1]])
+    return first, second
 
 
 def add_kernel(left_ref, right_ref, *refs):
@@ -76,14 +99,13 @@
         start += out_ref.shape[0]
 
 
-def add_parts(left, right, parts):
+def add_parts(left, right, sizes):
     vmem = pl.BlockSpec(memory_space=pltpu.VMEM)
-    part = jax.ShapeDtypeStruct((left.shape[0] // parts, left.shape[1]), left.dtype)
     return pl.pallas_call(
         add_parts_kernel,
-        out_shape=(part,) * parts,
+        out_shape=tuple(jax.ShapeDtypeStruct((size, left.shape[1]), left.dtype) for size in sizes),
         in_specs=[vmem, vmem],
-        out_specs=(vmem,) * parts,
+        out_specs=(vmem,) * len(sizes),
         compiler_params=pltpu.CompilerParams(vmem_limit_bytes=8 << 20),
     )(left, right)
 
@@ -105,17 +127,30 @@
     )
 
 
+def chunk_sizes(rows):
+    return [rows * quarters // sum(CHUNK_QUARTERS) for quarters in CHUNK_QUARTERS]
+
+
 def project(signals, channel_node, half):
     rows, channels = signals.shape
-    part = rows // CHUNKS // 2
-    step = min(512, part)
-    steps = part // step
+    parts = [size // 2 for size in chunk_sizes(rows)]
+    step = math.gcd(512, *parts)
+    steps = sum(parts) // step
+
+    def block_of(i, half):
+        done, block = 0, i
+        for part in parts:
+            count = part // step
+            block = jnp.where(i >= done, done + i + half[0] * count, block)
+            done += count
+        return block, 0
+
     grid_spec = pltpu.PrefetchScalarGridSpec(
         num_scalar_prefetch=1,
-        grid=(CHUNKS * steps,),
+        grid=(steps,),
         in_specs=[
             pl.BlockSpec((1, channels), lambda i, half: (0, 0)),
-            pl.BlockSpec((step, channels), lambda i, half: ((i // steps * 2 + half[0]) * steps + i % steps, 0)),
+            pl.BlockSpec((step, channels), block_of),
         ],
         out_specs=pl.BlockSpec((step, NODES), lambda i, half: (i, 0)),
         scratch_shapes=[pltpu.VMEM((NODES, channels), jnp.bfloat16)],
@@ -314,22 +349,31 @@
     return result, state
 
 
-def arrange(half_ref, mine_ref, other_ref, natural_ref, ordered_ref):
+def arrange(layout, half_ref, mine_refs, other_refs, natural_ref, ordered_ref):
     chan_count = 4
     lag_count = 2 * chan_count
     far = lag_count // 2
     width = NODES // chan_count
-    each = (2 * far + 1) * NODES
-
-    def place(ref, low):
+
+    def rows_of(refs, high, start, stop):
+        found, base = [], 0
+        for ref, pieces in zip(refs, layout):
+            for first, count, place in pieces[high]:
+                low, end = max(start, base + first), min(stop, base + first + count)
+                if low < end:
+                    offset = place - base - first
+                    found.append(ref[low + offset : end + offset, :])
+            base += ref.shape[0] // 2
+        return found[0] if len(found) == 1 else jnp.concatenate(found, axis=0)
+
+    def place(refs, low):
         for high in range(2):
             chan = 2 * high + low
             pairs = [(2 * chan + i, (2 * chan + i + d) % lag_count) for i in range(2) for d in range(far)]
             odd = 2 * chan // far
             pairs.append((2 * chan + odd, (2 * chan + odd + far) % lag_count))
             for index, (left, right) in enumerate(pairs):
-                start = high * each + index * NODES
-                block = ref[start : start + NODES, :]
+                block = rows_of(refs, high, index * NODES, (index + 1) * NODES)
                 natural_ref[left * NODES : (left + 1) * NODES, right * NODES : (right + 1) * NODES] = block
                 if left != right:
                     natural_ref[right * NODES : (right + 1) * NODES, left * NODES : (left + 1) * NODES] = block.T
@@ -338,8 +382,8 @@
 
         @pl.when(half_ref[0] == low)
         def _():
-            place(mine_ref, low)
-            place(other_ref, 1 - low)
+            place(mine_refs, low)
+            place(other_refs, 1 - low)
 
     lane_part = lax.broadcasted_iota(jnp.int32, (width, NODES), 1) // width
 
@@ -362,8 +406,11 @@
     lax.fori_loop(0, lag_count, rows_of_lag, 0)
 
 
-def cholesky_kernel(scale, half_ref, mine_ref, other_ref, out_ref, natural_ref, ordered_ref, panel_ref, inverse_ref):
-    arrange(half_ref, mine_ref, other_ref, natural_ref, ordered_ref)
+def cholesky_kernel(scale, layout, half_ref, *refs):
+    parts = len(layout)
+    mine_refs, other_refs = refs[:parts], refs[parts : 2 * parts]
+    out_ref, natural_ref, ordered_ref, panel_ref, inverse_ref = refs[2 * parts :]
+    arrange(layout, half_ref, mine_refs, other_refs, natural_ref, ordered_ref)
     size = out_ref.shape[0]
     count = size // BLOCK
     out_ref[...] = jnp.zeros_like(out_ref)
@@ -407,12 +454,12 @@
     lax.fori_loop(0, count, step, 0)
 
 
-def cholesky(half, mine, other, size, scale):
+def cholesky(half, mine, other, layout, size, scale):
     vmem = pl.BlockSpec(memory_space=pltpu.VMEM)
     return pl.pallas_call(
-        functools.partial(cholesky_kernel, scale),
+        functools.partial(cholesky_kernel, scale, layout),
         out_shape=jax.ShapeDtypeStruct((size, size), jnp.float32),
-        in_specs=[pl.BlockSpec(memory_space=pltpu.SMEM), vmem, vmem],
+        in_specs=[pl.BlockSpec(memory_space=pltpu.SMEM)] + [vmem] * (2 * len(mine)),
         out_specs=vmem,
         scratch_shapes=[
             pltpu.VMEM((size, size), jnp.float32),
@@ -421,7 +468,7 @@
             pltpu.VMEM((BLOCK, BLOCK), jnp.float32),
         ],
         compiler_params=pltpu.CompilerParams(vmem_limit_bytes=24 << 20),
-    )(half, mine, other)
+    )(half, *mine, *other)
 
 
 def on_device(signals, channel_node, lag_offsets):
@@ -430,11 +477,12 @@
     send = project(signals, channel_node, 1 - half)
     received = swap(send, "chan", 1)
     keep = project(signals, channel_node, half)
-    totals = add_parts(keep, received, CHUNKS)
+    sizes = chunk_sizes(signals.shape[0])
+    totals = add_parts(keep, received, [size // 2 for size in sizes])
     sent = [swap(total, "chan", 2) for total in totals]
     carried = after = None
-    for index in range(CHUNKS):
-        first, last = index == 0, index == CHUNKS - 1
+    for index in range(len(sizes)):
+        first, last = index == 0, index == len(sizes) - 1
         value = add(totals[index], sent[index], *(() if first else (carried[1], after)))
         other = swap(value, "chan", 1)
         if first:
@@ -442,11 +490,12 @@
             after = first_rows_of_next(head)
         earlier = (head,) if first else ()
         carried = gram_part(chan, lag_offsets, value, other, carried, after if last else None, earlier)
-    blocks = sum_over_time_blocks(carried)
-    blocks = double(blocks, "chan", 2)
-    other = swap(blocks, "chan", 1)
+    rows = carried.shape[0] // 2
+    mine = [route.reduce(part) for route, part in zip(routes(), (carried[:rows], carried[rows:]))]
+    other = [swap(value, "chan", 1) for value in mine]
+    layout = [[route.pieces(rows, high) for high in range(2)] for route in routes()]
     size = lag_offsets.shape[0] * NODES
-    return cholesky(half, blocks, other, size, 1.0 / (signals.shape[0] * lax.axis_size("tm")))
+    return cholesky(half, mine, other, layout, size, 1.0 / (signals.shape[0] * lax.axis_size("tm")))
 
 
 def solution(mesh):

time: 130 us -> 122 us (0.938)
  waiting for transfers between devices: 58.9 us -> 39.3 us
  starting transfers between devices: 21.5 us -> 33.5 us
    ppermute x13 -> x21, waiting for transfers between devices: 58.9 us -> 39.2 us  [swap(): return lax.ppermute(value, axis, [(i, i ^ bit) for i in range(count)])]
    ppermute x13 -> x21, starting transfers between devices: 20.2 us -> 32.2 us  [swap(): return lax.ppermute(value, axis, [(i, i ^ bit) for i in range(count)])]
  transfers between devices with their start and end apart: 14 -> 22, of which waited for: 13 -> 14; matrix products, arithmetic and copies ran while one was open for 0% -> 0% of each run, Pallas kernels for 4% -> 4%
where the time goes in v6:
time: 122 us
  Pallas kernels  44.9 us (37%)
  waiting for transfers between devices  39.3 us (32%)
  starting transfers between devices  33.5 us (27%)
  local copies, waits for them, and re-layouts  3.41 us (3%)
    ppermute x21, waiting for transfers between devices, swap(): return lax.ppermute(value, axis, [(i, i ^ bit) for i in range(count)])  39.2 us
    pallas_call x1, Pallas kernels, cholesky(): pl.pallas_call(functools.partial(cholesky_kernel, scale, layout), out_sha...  33.1 us
    ppermute x21, starting transfers between devices, swap(): return lax.ppermute(value, axis, [(i, i ^ bit) for i in range(count)])  32.2 us
    pallas_call x2, Pallas kernels, gram_part(): pl.pallas_call(functools.partial(gram_kernel, first, last, len(earlier)),...  9.1 us
    unnamed x10, local copies, waits for them, and re-layouts  3.29 us
    pallas_call x2, Pallas kernels, project(): pl.pallas_call(project_kernel, out_shape=jax.ShapeDtypeStruct((rows // 2,...  2.51 us
  transfers between devices with their start and end apart: 22, of which 14 were waited for; matrix products, arithmetic and copies ran while one was open for 0% of the time, Pallas kernels for 4%

profile of v6, /device:TPU:0, one launch (start us, length us, event | category | flops | bytes accessed | tf_op | source)
XLA Modules:
  0.0 121.9 jit_solution(13262979781355186443)
XLA Ops:
  0.0 2.2 %copy-done = bf16[4096,512]{1,0:T(8,128)(2,1)S(1)} copy-done((bf16[4096,512]{1,0:T(8,128)(2,1)S(1)}, bf16[4096,512]{1,0:T(8,128)(2,1)}, u32[]{:S(2)}) %copy-start) | copy-done | bytes 4194328
  2.9 1.2 %shard_map.38 = f32[2048,128]{1,0:T(8,128)S(1)} custom-call(s32[1]{0:T(128)S(6)} %sub.39.half_ref, s32[1,512]{1,0:T(1,128)S(1)} %bitcast.3, bf16[4096,512]{1,0:T(8,128)(2,1)S(1)} %copy-done), custom_call_target="tpu_custom_call" | custom-call | tf_op jit(solution)/shard_map/pallas_call | solution.py:158
  5.1 1.3 %shard_map.37.left_ref = f32[2048,128]{1,0:T(8,128)S(1)} custom-call(s32[1]{0:T(128)S(6)} %select_n.198.half_ref, s32[1,512]{1,0:T(1,128)S(1)} %bitcast.4, bf16[4096,512]{1,0:T(8,128)(2,1)S(1)} %copy-done.1), custom_call_target="tpu_custom_call" | custom-call | tf_op jit(solution)/shard_map/pallas_call | solution.py:158
  7.1 2.9 %collective-permute-start.2 = (f32[1024,128]{1,0:T(8,128)S(1)}, f32[1024,128]{1,0:T(8,128)S(1)}, u32[]{:S(2)}, u32[]{:S(2)}) collective-permute-start(f32[1024,128]{1,0:T(8,128)S(1)} %get-tuple-element.10.left_ref), channel_id=1, source_target_pairs={{0,2},{1,3},{2,0},{3,1},{4,6},{5,7},{6,4},{7,5},{8,10},{9,11},{10,... | collective-permute-start | bytes 1572872 | tf_op jit(solution)/shard_map/ppermute | solution.py:24
  10.0 12.2 %collective-permute-done.2.right_ref = f32[1024,128]{1,0:T(8,128)S(1)} collective-permute-done((f32[1024,128]{1,0:T(8,128)S(1)}, f32[1024,128]{1,0:T(8,128)S(1)}, u32[]{:S(2)}, u32[]{:S(2)}) %collective-permute-start.2) | collective-permute-done | bytes 524320 | tf_op jit(solution)/shard_map/ppermute | solution.py:24
  22.4 1.8 %collective-permute-start.1 = (f32[1024,128]{1,0:T(8,128)S(1)}, f32[1024,128]{1,0:T(8,128)S(1)}, u32[]{:S(2)}, u32[]{:S(2)}) collective-permute-start(f32[1024,128]{1,0:T(8,128)S(1)} %get-tuple-element.9.left_ref), channel_id=1, source_target_pairs={{0,2},{1,3},{2,0},{3,1},{4,6},{5,7},{6,4},{7,5},{8,10},{9,11},{10,... | collective-permute-start | bytes 1572872 | tf_op jit(solution)/shard_map/ppermute | solution.py:24
  24.3 1.3 %collective-permute-start.4 = (f32[512,128]{1,0:T(8,128)S(1)}, f32[512,128]{1,0:T(8,128)S(1)}, u32[]{:S(2)}, u32[]{:S(2)}) collective-permute-start(f32[512,128]{1,0:T(8,128)S(1)} %slice_select_fusion.refs_2_), channel_id=1, source_target_pairs={{4,0},{8,4},{12,8},{16,12},{20,16},{24,20},{28,24},{5,1},{9,5},{13... | collective-permute-start | bytes 786440 | tf_op jit(solution)/shard_map/ppermute | solution.py:115
  25.6 3.6 %shard_map.41 = (f32[256,768]{1,0:T(8,128)S(1)}, f32[512,128]{1,0:T(8,128)S(1)}) custom-call(s32[1]{0:T(128)} %bitcast.chan_ref, s32[8]{0:T(128)S(1)} %copy-done.4, f32[1024,128]{1,0:T(8,128)S(1)} %shard_map.40.refs_0_, f32[1024,128]{1,0:T(8,128)S(1)} %collective-permute-done.3.refs_1_, f32[512,128]{1,0:T(8,128)S(1)} %slice_select_fusion.refs_2_), custom_call_target="tpu_custom_call" | custom-call | tf_op jit(solution)/shard_map/pallas_call | solution.py:253
  29.2 7.5 %collective-permute-done.1.right_ref = f32[1024,128]{1,0:T(8,128)S(1)} collective-permute-done((f32[1024,128]{1,0:T(8,128)S(1)}, f32[1024,128]{1,0:T(8,128)S(1)}, u32[]{:S(2)}, u32[]{:S(2)}) %collective-permute-start.1) | collective-permute-done | bytes 524320 | tf_op jit(solution)/shard_map/ppermute | solution.py:24
  36.9 1.9 %collective-permute-done.5.refs_1_ = f32[1024,128]{1,0:T(8,128)S(1)} collective-permute-done((f32[1024,128]{1,0:T(8,128)S(1)}, f32[1024,128]{1,0:T(8,128)S(1)}, u32[]{:S(2)}, u32[]{:S(2)}) %collective-permute-start.5) | collective-permute-done | bytes 524320 | tf_op jit(solution)/shard_map/ppermute | solution.py:24
  38.8 5.5 %shard_map.43 = f32[1152,128]{1,0:T(8,128)S(1)} custom-call(s32[1]{0:T(128)} %bitcast.chan_ref, s32[8]{0:T(128)S(1)} %copy-done.4, f32[1024,128]{1,0:T(8,128)S(1)} %shard_map.42.refs_0_, f32[1024,128]{1,0:T(8,128)S(1)} %collective-permute-done.5.refs_1_, f32[256,768]{1,0:T(8,128)S(1)} %get-tuple-element.12.refs_2_, ...), custom_call_target="tpu_custom_call" | custom-call | tf_op jit(solution)/shard_map/pallas_call | solution.py:253
  44.4 1.9 %collective-permute-start.13 = (f32[288,128]{1,0:T(8,128)S(1)}, f32[288,128]{1,0:T(8,128)S(1)}, u32[]{:S(2)}, u32[]{:S(2)}) collective-permute-start(f32[288,128]{1,0:T(8,128)S(1)} %constant_dynamic-slice_fusion.2), channel_id=1, source_target_pairs={{0,8},{4,12},{8,0},{12,4},{16,24},{20,28},{24,16},{28,20},{1,9},{5... | collective-permute-start | bytes 442376 | tf_op jit(solution)/shard_map/ppermute | solution.py:24
  46.3 1.6 %collective-permute-start.6 = (f32[288,128]{1,0:T(8,128)S(1)}, f32[288,128]{1,0:T(8,128)S(1)}, u32[]{:S(2)}, u32[]{:S(2)}) collective-permute-start(f32[288,128]{1,0:T(8,128)S(1)} %constant_dynamic-slice_fusion.5), channel_id=1, source_target_pairs={{0,4},{4,0},{8,12},{12,8},{16,20},{20,16},{24,28},{28,24},{1,5},{5... | collective-permute-start | bytes 442376 | tf_op jit(solution)/shard_map/ppermute | solution.py:24
  47.9 2.5 %collective-permute-done.13 = f32[288,128]{1,0:T(8,128)S(1)} collective-permute-done((f32[288,128]{1,0:T(8,128)S(1)}, f32[288,128]{1,0:T(8,128)S(1)}, u32[]{:S(2)}, u32[]{:S(2)}) %collective-permute-start.13) | collective-permute-done | bytes 147488 | tf_op jit(solution)/shard_map/ppermute | solution.py:24
  50.4 2.8 %collective-permute-start.14 = (f32[144,128]{1,0:T(8,128)S(1)}, f32[144,128]{1,0:T(8,128)S(1)}, u32[]{:S(2)}, u32[]{:S(2)}) collective-permute-start(f32[144,128]{1,0:T(8,128)S(1)} %constant_dynamic-slice_fusion.1), channel_id=1, source_target_pairs={{0,16},{4,20},{8,24},{12,28},{16,0},{20,4},{24,8},{28,12},{1,17},{... | collective-permute-start | bytes 221192 | tf_op jit(solution)/shard_map/ppermute | solution.py:24
  53.3 1.6 %collective-permute-start.7 = (f32[144,128]{1,0:T(8,128)S(1)}, f32[144,128]{1,0:T(8,128)S(1)}, u32[]{:S(2)}, u32[]{:S(2)}) collective-permute-start(f32[144,128]{1,0:T(8,128)S(1)} %constant_dynamic-slice_fusion.4), channel_id=1, source_target_pairs={{0,8},{4,12},{8,0},{12,4},{16,24},{20,28},{24,16},{28,20},{1,9},{5... | collective-permute-start | bytes 221192 | tf_op jit(solution)/shard_map/ppermute | solution.py:24
  55.0 1.2 collective-permute-done.14
  56.2 1.6 %collective-permute-start.15 = (f32[72,128]{1,0:T(8,128)S(1)}, f32[72,128]{1,0:T(8,128)S(1)}, u32[]{:S(2)}, u32[]{:S(2)}) collective-permute-start(f32[72,128]{1,0:T(8,128)S(1)} %constant_dynamic-slice_fusion), channel_id=1, source_target_pairs={{0,4},{4,0},{8,12},{12,8},{16,20},{20,16},{24,28},{28,24},{1,5},{5... | collective-permute-start | bytes 110600 | tf_op jit(solution)/shard_map/ppermute | solution.py:24
  57.8 3.0 %collective-permute-start.8 = (f32[72,128]{1,0:T(8,128)S(1)}, f32[72,128]{1,0:T(8,128)S(1)}, u32[]{:S(2)}, u32[]{:S(2)}) collective-permute-start(f32[72,128]{1,0:T(8,128)S(1)} %constant_dynamic-slice_fusion.3), channel_id=1, source_target_pairs={{0,16},{4,20},{8,24},{12,28},{16,0},{20,4},{24,8},{28,12},{1,17},{... | collective-permute-start | bytes 110600 | tf_op jit(solution)/shard_map/ppermute | solution.py:24
  60.9 1.6 %collective-permute-start.16 = (f32[72,128]{1,0:T(8,128)S(1)}, f32[72,128]{1,0:T(8,128)S(1)}, u32[]{:S(2)}, u32[]{:S(2)}) collective-permute-start(f32[72,128]{1,0:T(8,128)S(1)} %dynamic-slice_add_fusion.4), channel_id=1, source_target_pairs={{0,2},{1,3},{2,0},{3,1},{4,6},{5,7},{6,4},{7,5},{8,10},{9,11},{10,... | collective-permute-start | bytes 110600 | tf_op jit(solution)/shard_map/ppermute | solution.py:24
  62.8 3.3 %collective-permute-start.9 = (f32[72,128]{1,0:T(8,128)S(1)}, f32[72,128]{1,0:T(8,128)S(1)}, u32[]{:S(2)}, u32[]{:S(2)}) collective-permute-start(f32[72,128]{1,0:T(8,128)S(1)} %dynamic-slice_add_fusion.5), channel_id=1, source_target_pairs={{0,16},{4,20},{8,24},{12,28},{16,0},{20,4},{24,8},{28,12},{1,17},{... | collective-permute-start | bytes 110600 | tf_op jit(solution)/shard_map/ppermute | solution.py:24
  66.1 1.1 collective-permute-start.17
  67.3 0.8 collective-permute-done.9
  68.1 3.5 %collective-permute-start.10 = (f32[144,128]{1,0:T(8,128)S(1)}, f32[144,128]{1,0:T(8,128)S(1)}, u32[]{:S(2)}, u32[]{:S(2)}) collective-permute-start(f32[144,128]{1,0:T(8,128)S(1)} %pad_maximum_fusion.6), channel_id=1, source_target_pairs={{0,8},{4,12},{8,0},{12,4},{16,24},{20,28},{24,16},{28,20},{1,9},{5... | collective-permute-start | bytes 221192 | tf_op jit(solution)/shard_map/ppermute | solution.py:24
  71.6 3.0 %collective-permute-start.18 = (f32[288,128]{1,0:T(8,128)S(1)}, f32[288,128]{1,0:T(8,128)S(1)}, u32[]{:S(2)}, u32[]{:S(2)}) collective-permute-start(f32[288,128]{1,0:T(8,128)S(1)} %pad_maximum_fusion.5), channel_id=1, source_target_pairs={{0,8},{4,12},{8,0},{12,4},{16,24},{20,28},{24,16},{28,20},{1,9},{5... | collective-permute-start | bytes 442376 | tf_op jit(solution)/shard_map/ppermute | solution.py:24
  74.7 3.0 %collective-permute-done.18 = f32[288,128]{1,0:T(8,128)S(1)} collective-permute-done((f32[288,128]{1,0:T(8,128)S(1)}, f32[288,128]{1,0:T(8,128)S(1)}, u32[]{:S(2)}, u32[]{:S(2)}) %collective-permute-start.18) | collective-permute-done | bytes 147488 | tf_op jit(solution)/shard_map/ppermute | solution.py:24
  77.8 2.0 %collective-permute-done.11 = f32[288,128]{1,0:T(8,128)S(1)} collective-permute-done((f32[288,128]{1,0:T(8,128)S(1)}, f32[288,128]{1,0:T(8,128)S(1)}, u32[]{:S(2)}, u32[]{:S(2)}) %collective-permute-start.11) | collective-permute-done | bytes 147488 | tf_op jit(solution)/shard_map/ppermute | solution.py:24
  79.9 1.6 %collective-permute-start.12 = (f32[576,128]{1,0:T(8,128)S(1)}, f32[576,128]{1,0:T(8,128)S(1)}, u32[]{:S(2)}, u32[]{:S(2)}) collective-permute-start(f32[576,128]{1,0:T(8,128)S(1)} %pad_maximum_fusion.2), channel_id=1, source_target_pairs={{0,2},{1,3},{2,0},{3,1},{4,6},{5,7},{6,4},{7,5},{8,10},{9,11},{10,... | collective-permute-start | bytes 884744 | tf_op jit(solution)/shard_map/ppermute | solution.py:24
  81.4 3.1 %collective-permute-done.19 = f32[576,128]{1,0:T(8,128)S(1)} collective-permute-done((f32[576,128]{1,0:T(8,128)S(1)}, f32[576,128]{1,0:T(8,128)S(1)}, u32[]{:S(2)}, u32[]{:S(2)}) %collective-permute-start.19) | collective-permute-done | bytes 294944 | tf_op jit(solution)/shard_map/ppermute | solution.py:24
  84.7 2.0 %collective-permute-done.12 = f32[576,128]{1,0:T(8,128)S(1)} collective-permute-done((f32[576,128]{1,0:T(8,128)S(1)}, f32[576,128]{1,0:T(8,128)S(1)}, u32[]{:S(2)}, u32[]{:S(2)}) %collective-permute-start.12) | collective-permute-done | bytes 294944 | tf_op jit(solution)/shard_map/ppermute | solution.py:24
  86.8 2.0 %collective-permute-done.20.refs_2_ = f32[1152,128]{1,0:T(8,128)S(1)} collective-permute-done((f32[1152,128]{1,0:T(8,128)S(1)}, f32[1152,128]{1,0:T(8,128)S(1)}, u32[]{:S(2)}, u32[]{:S(2)}) %collective-permute-start.20) | collective-permute-done | bytes 589856 | tf_op jit(solution)/shard_map/ppermute | solution.py:24
  88.8 33.1 %shard_map.44 = f32[1024,1024]{1,0:T(8,128)} custom-call(s32[1]{0:T(128)S(6)} %select_n.198.half_ref, f32[1152,128]{1,0:T(8,128)S(1)} %pad_maximum_fusion.refs_0_, f32[1152,128]{1,0:T(8,128)S(1)} %pad_maximum_fusion.1.refs_1_, f32[1152,128]{1,0:T(8,128)S(1)} %collective-permute-done.20.refs_2_, f32[1152,128]{1,0:T(8,128)S(1)} %collective-permute-done.21.refs_3_), custom_call_target="tpu_custom_call" | custom-call | tf_op jit(solution)/shard_map/pallas_call | solution.py:459
  (60 shorter events, 3.9 us)
Async XLA Ops:
  0.0 4.7 %copy-start.3 = (s32[512]{0:T(512)S(1)}, s32[512]{0:T(512)}, u32[]{:S(2)}) copy-start(s32[512]{0:T(512)} %param.4) | copy-start | bytes 6148
  0.0 2.2 %copy-start = (bf16[4096,512]{1,0:T(8,128)(2,1)S(1)}, bf16[4096,512]{1,0:T(8,128)(2,1)}, u32[]{:S(2)}) copy-start(bf16[4096,512]{1,0:T(8,128)(2,1)} %signals_ref.3) | copy-start | bytes 12582916
  2.2 0.7 copy-start.2
  2.9 2.2 %copy-start.1 = (bf16[4096,512]{1,0:T(8,128)(2,1)S(1)}, bf16[4096,512]{1,0:T(8,128)(2,1)}, u32[]{:S(2)}) copy-start(bf16[4096,512]{1,0:T(8,128)(2,1)} %signals_ref.3) | copy-start | bytes 12582916
  4.1 21.5 %copy-start.4 = (s32[8]{0:T(128)S(1)}, s32[8]{0:T(128)}, u32[]{:S(2)}) copy-start(s32[8]{0:T(128)} %all_lags_ref.3) | copy-start | bytes 100
  4.2 2.8 %collective-permute-start = (f32[2048,128]{1,0:T(8,128)S(1)}, f32[2048,128]{1,0:T(8,128)S(1)}, u32[]{:S(2)}, u32[]{:S(2)}) collective-permute-start(f32[2048,128]{1,0:T(8,128)S(1)} %shard_map.38), channel_id=1, source_target_pairs={{0,1},{1,0},{2,3},{3,2},{4,5},{5,4},{6,7},{7,6},{8,9},{9,8},{10,11... | collective-permute-start | bytes 3145736 | tf_op jit(solution)/shard_map/ppermute | solution.py:24
  7.1 15.2 %collective-permute-start.2 = (f32[1024,128]{1,0:T(8,128)S(1)}, f32[1024,128]{1,0:T(8,128)S(1)}, u32[]{:S(2)}, u32[]{:S(2)}) collective-permute-start(f32[1024,128]{1,0:T(8,128)S(1)} %get-tuple-element.10.left_ref), channel_id=1, source_target_pairs={{0,2},{1,3},{2,0},{3,1},{4,6},{5,7},{6,4},{7,5},{8,10},{9,11},{10,... | collective-permute-start | bytes 1572872 | tf_op jit(solution)/shard_map/ppermute | solution.py:24
  22.3 2.0 %collective-permute-start.3 = (f32[1024,128]{1,0:T(8,128)S(1)}, f32[1024,128]{1,0:T(8,128)S(1)}, u32[]{:S(2)}, u32[]{:S(2)}) collective-permute-start(f32[1024,128]{1,0:T(8,128)S(1)} %shard_map.40.refs_0_), channel_id=1, source_target_pairs={{0,1},{1,0},{2,3},{3,2},{4,5},{5,4},{6,7},{7,6},{8,9},{9,8},{10,11... | collective-permute-start | bytes 1572872 | tf_op jit(solution)/shard_map/ppermute | solution.py:24
  22.4 14.3 %collective-permute-start.1 = (f32[1024,128]{1,0:T(8,128)S(1)}, f32[1024,128]{1,0:T(8,128)S(1)}, u32[]{:S(2)}, u32[]{:S(2)}) collective-permute-start(f32[1024,128]{1,0:T(8,128)S(1)} %get-tuple-element.9.left_ref), channel_id=1, source_target_pairs={{0,2},{1,3},{2,0},{3,1},{4,6},{5,7},{6,4},{7,5},{8,10},{9,11},{10,... | collective-permute-start | bytes 1572872 | tf_op jit(solution)/shard_map/ppermute | solution.py:24
  24.3 12.4 %collective-permute-start.4 = (f32[512,128]{1,0:T(8,128)S(1)}, f32[512,128]{1,0:T(8,128)S(1)}, u32[]{:S(2)}, u32[]{:S(2)}) collective-permute-start(f32[512,128]{1,0:T(8,128)S(1)} %slice_select_fusion.refs_2_), channel_id=1, source_target_pairs={{4,0},{8,4},{12,8},{16,12},{20,16},{24,20},{28,24},{5,1},{9,5},{13... | collective-permute-start | bytes 786440 | tf_op jit(solution)/shard_map/ppermute | solution.py:115
  36.8 2.0 %collective-permute-start.5 = (f32[1024,128]{1,0:T(8,128)S(1)}, f32[1024,128]{1,0:T(8,128)S(1)}, u32[]{:S(2)}, u32[]{:S(2)}) collective-permute-start(f32[1024,128]{1,0:T(8,128)S(1)} %shard_map.42.refs_0_), channel_id=1, source_target_pairs={{0,1},{1,0},{2,3},{3,2},{4,5},{5,4},{6,7},{7,6},{8,9},{9,8},{10,11... | collective-permute-start | bytes 1572872 | tf_op jit(solution)/shard_map/ppermute | solution.py:24
  44.4 6.0 %collective-permute-start.13 = (f32[288,128]{1,0:T(8,128)S(1)}, f32[288,128]{1,0:T(8,128)S(1)}, u32[]{:S(2)}, u32[]{:S(2)}) collective-permute-start(f32[288,128]{1,0:T(8,128)S(1)} %constant_dynamic-slice_fusion.2), channel_id=1, source_target_pairs={{0,8},{4,12},{8,0},{12,4},{16,24},{20,28},{24,16},{28,20},{1,9},{5... | collective-permute-start | bytes 442376 | tf_op jit(solution)/shard_map/ppermute | solution.py:24
  46.3 7.0 %collective-permute-start.6 = (f32[288,128]{1,0:T(8,128)S(1)}, f32[288,128]{1,0:T(8,128)S(1)}, u32[]{:S(2)}, u32[]{:S(2)}) collective-permute-start(f32[288,128]{1,0:T(8,128)S(1)} %constant_dynamic-slice_fusion.5), channel_id=1, source_target_pairs={{0,4},{4,0},{8,12},{12,8},{16,20},{20,16},{24,28},{28,24},{1,5},{5... | collective-permute-start | bytes 442376 | tf_op jit(solution)/shard_map/ppermute | solution.py:24
  50.4 5.7 %collective-permute-start.14 = (f32[144,128]{1,0:T(8,128)S(1)}, f32[144,128]{1,0:T(8,128)S(1)}, u32[]{:S(2)}, u32[]{:S(2)}) collective-permute-start(f32[144,128]{1,0:T(8,128)S(1)} %constant_dynamic-slice_fusion.1), channel_id=1, source_target_pairs={{0,16},{4,20},{8,24},{12,28},{16,0},{20,4},{24,8},{28,12},{1,17},{... | collective-permute-start | bytes 221192 | tf_op jit(solution)/shard_map/ppermute | solution.py:24
  53.3 4.5 %collective-permute-start.7 = (f32[144,128]{1,0:T(8,128)S(1)}, f32[144,128]{1,0:T(8,128)S(1)}, u32[]{:S(2)}, u32[]{:S(2)}) collective-permute-start(f32[144,128]{1,0:T(8,128)S(1)} %constant_dynamic-slice_fusion.4), channel_id=1, source_target_pairs={{0,8},{4,12},{8,0},{12,4},{16,24},{20,28},{24,16},{28,20},{1,9},{5... | collective-permute-start | bytes 221192 | tf_op jit(solution)/shard_map/ppermute | solution.py:24
  56.2 4.7 %collective-permute-start.15 = (f32[72,128]{1,0:T(8,128)S(1)}, f32[72,128]{1,0:T(8,128)S(1)}, u32[]{:S(2)}, u32[]{:S(2)}) collective-permute-start(f32[72,128]{1,0:T(8,128)S(1)} %constant_dynamic-slice_fusion), channel_id=1, source_target_pairs={{0,4},{4,0},{8,12},{12,8},{16,20},{20,16},{24,28},{28,24},{1,5},{5... | collective-permute-start | bytes 110600 | tf_op jit(solution)/shard_map/ppermute | solution.py:24
  57.8 5.0 %collective-permute-start.8 = (f32[72,128]{1,0:T(8,128)S(1)}, f32[72,128]{1,0:T(8,128)S(1)}, u32[]{:S(2)}, u32[]{:S(2)}) collective-permute-start(f32[72,128]{1,0:T(8,128)S(1)} %constant_dynamic-slice_fusion.3), channel_id=1, source_target_pairs={{0,16},{4,20},{8,24},{12,28},{16,0},{20,4},{24,8},{28,12},{1,17},{... | collective-permute-start | bytes 110600 | tf_op jit(solution)/shard_map/ppermute | solution.py:24
  60.9 5.2 %collective-permute-start.16 = (f32[72,128]{1,0:T(8,128)S(1)}, f32[72,128]{1,0:T(8,128)S(1)}, u32[]{:S(2)}, u32[]{:S(2)}) collective-permute-start(f32[72,128]{1,0:T(8,128)S(1)} %dynamic-slice_add_fusion.4), channel_id=1, source_target_pairs={{0,2},{1,3},{2,0},{3,1},{4,6},{5,7},{6,4},{7,5},{8,10},{9,11},{10,... | collective-permute-start | bytes 110600 | tf_op jit(solution)/shard_map/ppermute | solution.py:24
  62.8 5.2 %collective-permute-start.9 = (f32[72,128]{1,0:T(8,128)S(1)}, f32[72,128]{1,0:T(8,128)S(1)}, u32[]{:S(2)}, u32[]{:S(2)}) collective-permute-start(f32[72,128]{1,0:T(8,128)S(1)} %dynamic-slice_add_fusion.5), channel_id=1, source_target_pairs={{0,16},{4,20},{8,24},{12,28},{16,0},{20,4},{24,8},{28,12},{1,17},{... | collective-permute-start | bytes 110600 | tf_op jit(solution)/shard_map/ppermute | solution.py:24
  66.1 5.4 %collective-permute-start.17 = (f32[144,128]{1,0:T(8,128)S(1)}, f32[144,128]{1,0:T(8,128)S(1)}, u32[]{:S(2)}, u32[]{:S(2)}) collective-permute-start(f32[144,128]{1,0:T(8,128)S(1)} %pad_maximum_fusion.7), channel_id=1, source_target_pairs={{0,16},{4,20},{8,24},{12,28},{16,0},{20,4},{24,8},{28,12},{1,17},{... | collective-permute-start | bytes 221192 | tf_op jit(solution)/shard_map/ppermute | solution.py:24
  68.1 6.5 %collective-permute-start.10 = (f32[144,128]{1,0:T(8,128)S(1)}, f32[144,128]{1,0:T(8,128)S(1)}, u32[]{:S(2)}, u32[]{:S(2)}) collective-permute-start(f32[144,128]{1,0:T(8,128)S(1)} %pad_maximum_fusion.6), channel_id=1, source_target_pairs={{0,8},{4,12},{8,0},{12,4},{16,24},{20,28},{24,16},{28,20},{1,9},{5... | collective-permute-start | bytes 221192 | tf_op jit(solution)/shard_map/ppermute | solution.py:24
  71.6 6.1 %collective-permute-start.18 = (f32[288,128]{1,0:T(8,128)S(1)}, f32[288,128]{1,0:T(8,128)S(1)}, u32[]{:S(2)}, u32[]{:S(2)}) collective-permute-start(f32[288,128]{1,0:T(8,128)S(1)} %pad_maximum_fusion.5), channel_id=1, source_target_pairs={{0,8},{4,12},{8,0},{12,4},{16,24},{20,28},{24,16},{28,20},{1,9},{5... | collective-permute-start | bytes 442376 | tf_op jit(solution)/shard_map/ppermute | solution.py:24
  74.6 5.2 %collective-permute-start.11 = (f32[288,128]{1,0:T(8,128)S(1)}, f32[288,128]{1,0:T(8,128)S(1)}, u32[]{:S(2)}, u32[]{:S(2)}) collective-permute-start(f32[288,128]{1,0:T(8,128)S(1)} %pad_maximum_fusion.4), channel_id=1, source_target_pairs={{0,4},{4,0},{8,12},{12,8},{16,20},{20,16},{24,28},{28,24},{1,5},{5... | collective-permute-start | bytes 442376 | tf_op jit(solution)/shard_map/ppermute | solution.py:24
  77.7 6.8 %collective-permute-start.19 = (f32[576,128]{1,0:T(8,128)S(1)}, f32[576,128]{1,0:T(8,128)S(1)}, u32[]{:S(2)}, u32[]{:S(2)}) collective-permute-start(f32[576,128]{1,0:T(8,128)S(1)} %pad_maximum_fusion.3), channel_id=1, source_target_pairs={{0,4},{4,0},{8,12},{12,8},{16,20},{20,16},{24,28},{28,24},{1,5},{5... | collective-permute-start | bytes 884744 | tf_op jit(solution)/shard_map/ppermute | solution.py:24
  79.9 6.8 %collective-permute-start.12 = (f32[576,128]{1,0:T(8,128)S(1)}, f32[576,128]{1,0:T(8,128)S(1)}, u32[]{:S(2)}, u32[]{:S(2)}) collective-permute-start(f32[576,128]{1,0:T(8,128)S(1)} %pad_maximum_fusion.2), channel_id=1, source_target_pairs={{0,2},{1,3},{2,0},{3,1},{4,6},{5,7},{6,4},{7,5},{8,10},{9,11},{10,... | collective-permute-start | bytes 884744 | tf_op jit(solution)/shard_map/ppermute | solution.py:24
  84.6 2.2 %collective-permute-start.21 = (f32[1152,128]{1,0:T(8,128)S(1)}, f32[1152,128]{1,0:T(8,128)S(1)}, u32[]{:S(2)}, u32[]{:S(2)}) collective-permute-start(f32[1152,128]{1,0:T(8,128)S(1)} %pad_maximum_fusion.1.refs_1_), channel_id=1, source_target_pairs={{0,1},{1,0},{2,3},{3,2},{4,5},{5,4},{6,7},{7,6},{8,9},{9,8},{10,11... | collective-permute-start | bytes 1769480 | tf_op jit(solution)/shard_map/ppermute | solution.py:24
  86.7 2.1 %collective-permute-start.20 = (f32[1152,128]{1,0:T(8,128)S(1)}, f32[1152,128]{1,0:T(8,128)S(1)}, u32[]{:S(2)}, u32[]{:S(2)}) collective-permute-start(f32[1152,128]{1,0:T(8,128)S(1)} %pad_maximum_fusion.refs_0_), channel_id=1, source_target_pairs={{0,1},{1,0},{2,3},{3,2},{4,5},{5,4},{6,7},{7,6},{8,9},{9,8},{10,11... | collective-permute-start | bytes 1769480 | tf_op jit(solution)/shard_map/ppermute | solution.py:24

commit v7 on v6

--- a/solution.py
+++ b/solution.py
@@ -46,12 +46,14 @@
 
 
 class Route:
-    def __init__(self, scatter, gather):
-        self.scatter, self.gather = scatter, gather
+    def __init__(self, scatter, whole, gather):
+        self.scatter, self.whole, self.gather = scatter, whole, gather
 
     def reduce(self, value):
         for bit in self.scatter:
             value = halve(value, "tm", bit)
+        for bit in self.whole:
+            value = value + swap(value, "tm", bit)
         for axis, bit in self.gather:
             value = double(value, axis, bit)
         return value
@@ -71,8 +73,10 @@
 def routes():
     bits = bits_of("tm")
     upper = ("chan", 2)
-    first = Route(bits, [("tm", bit) for bit in bits[::-1]] + [upper])
-    second = Route(bits[1:] + bits[:1], [upper] + [("tm", bit) for bit in bits[:0:-1] + bits[:1]])
+    ahead, last = bits[:-1], bits[-1:]
+    first = Route(ahead, last, [("tm", bit) for bit in ahead[::-1]] + [upper])
+    turned = ahead[1:] + ahead[:1]
+    second = Route(turned, last, [("tm", bit) for bit in turned[:0:-1]] + [upper] + [("tm", turned[0])])
     return first, second
 
 

time: 122 us -> 116 us (0.951)
  starting transfers between devices: 33.5 us -> 25.8 us
  waiting for transfers between devices: 39.3 us -> 41 us
    ppermute x21 -> x19, starting transfers between devices: 32.2 us -> 24.5 us  [swap(): return lax.ppermute(value, axis, [(i, i ^ bit) for i in range(count)])]
    ppermute x21 -> x19, waiting for transfers between devices: 39.2 us -> 41 us  [swap(): return lax.ppermute(value, axis, [(i, i ^ bit) for i in range(count)])]
  transfers between devices with their start and end apart: 22 -> 20, of which waited for: 14 -> 16; matrix products, arithmetic and copies ran while one was open for 0% -> 0% of each run, Pallas kernels for 4% -> 4%
where the time goes in v7:
time: 116 us
  Pallas kernels  44.7 us (39%)
  waiting for transfers between devices  41 us (35%)
  starting transfers between devices  25.8 us (22%)
  local copies, waits for them, and re-layouts  3.39 us (3%)
    ppermute x19, waiting for transfers between devices, swap(): return lax.ppermute(value, axis, [(i, i ^ bit) for i in range(count)])  41 us
    pallas_call x1, Pallas kernels, cholesky(): pl.pallas_call(functools.partial(cholesky_kernel, scale, layout), out_sha...  33.1 us
    ppermute x19, starting transfers between devices, swap(): return lax.ppermute(value, axis, [(i, i ^ bit) for i in range(count)])  24.5 us
    pallas_call x2, Pallas kernels, gram_part(): pl.pallas_call(functools.partial(gram_kernel, first, last, len(earlier)),...  8.88 us
    unnamed x10, local copies, waits for them, and re-layouts  3.29 us
    pallas_call x2, Pallas kernels, project(): pl.pallas_call(project_kernel, out_shape=jax.ShapeDtypeStruct((rows // 2,...  2.51 us
  transfers between devices with their start and end apart: 20, of which 16 were waited for; matrix products, arithmetic and copies ran while one was open for 0% of the time, Pallas kernels for 4%

profile of v7, /device:TPU:0, one launch (start us, length us, event | category | flops | bytes accessed | tf_op | source)
XLA Modules:
  0.0 115.6 jit_solution(1586575065368151991)
XLA Ops:
  0.0 2.2 %copy-done = bf16[4096,512]{1,0:T(8,128)(2,1)S(1)} copy-done((bf16[4096,512]{1,0:T(8,128)(2,1)S(1)}, bf16[4096,512]{1,0:T(8,128)(2,1)}, u32[]{:S(2)}) %copy-start) | copy-done | bytes 4194328
  2.9 1.2 %shard_map.38 = f32[2048,128]{1,0:T(8,128)S(1)} custom-call(s32[1]{0:T(128)S(6)} %sub.28.half_ref, s32[1,512]{1,0:T(1,128)S(1)} %bitcast.3, bf16[4096,512]{1,0:T(8,128)(2,1)S(1)} %copy-done), custom_call_target="tpu_custom_call" | custom-call | tf_op jit(solution)/shard_map/pallas_call | solution.py:162
  5.1 1.3 %shard_map.37.left_ref = f32[2048,128]{1,0:T(8,128)S(1)} custom-call(s32[1]{0:T(128)S(6)} %select_n.148.half_ref, s32[1,512]{1,0:T(1,128)S(1)} %bitcast.4, bf16[4096,512]{1,0:T(8,128)(2,1)S(1)} %copy-done.1), custom_call_target="tpu_custom_call" | custom-call | tf_op jit(solution)/shard_map/pallas_call | solution.py:162
  7.1 2.9 %collective-permute-start.2 = (f32[1024,128]{1,0:T(8,128)S(1)}, f32[1024,128]{1,0:T(8,128)S(1)}, u32[]{:S(2)}, u32[]{:S(2)}) collective-permute-start(f32[1024,128]{1,0:T(8,128)S(1)} %get-tuple-element.10.left_ref), channel_id=1, source_target_pairs={{0,2},{1,3},{2,0},{3,1},{4,6},{5,7},{6,4},{7,5},{8,10},{9,11},{10,... | collective-permute-start | bytes 1572872 | tf_op jit(solution)/shard_map/ppermute | solution.py:24
  10.0 12.2 %collective-permute-done.2.right_ref = f32[1024,128]{1,0:T(8,128)S(1)} collective-permute-done((f32[1024,128]{1,0:T(8,128)S(1)}, f32[1024,128]{1,0:T(8,128)S(1)}, u32[]{:S(2)}, u32[]{:S(2)}) %collective-permute-start.2) | collective-permute-done | bytes 524320 | tf_op jit(solution)/shard_map/ppermute | solution.py:24
  22.4 1.8 %collective-permute-start.1 = (f32[1024,128]{1,0:T(8,128)S(1)}, f32[1024,128]{1,0:T(8,128)S(1)}, u32[]{:S(2)}, u32[]{:S(2)}) collective-permute-start(f32[1024,128]{1,0:T(8,128)S(1)} %get-tuple-element.9.left_ref), channel_id=1, source_target_pairs={{0,2},{1,3},{2,0},{3,1},{4,6},{5,7},{6,4},{7,5},{8,10},{9,11},{10,... | collective-permute-start | bytes 1572872 | tf_op jit(solution)/shard_map/ppermute | solution.py:24
  24.3 1.3 %collective-permute-start.4 = (f32[512,128]{1,0:T(8,128)S(1)}, f32[512,128]{1,0:T(8,128)S(1)}, u32[]{:S(2)}, u32[]{:S(2)}) collective-permute-start(f32[512,128]{1,0:T(8,128)S(1)} %slice_select_fusion.refs_2_), channel_id=1, source_target_pairs={{4,0},{8,4},{12,8},{16,12},{20,16},{24,20},{28,24},{5,1},{9,5},{13... | collective-permute-start | bytes 786440 | tf_op jit(solution)/shard_map/ppermute | solution.py:119
  25.6 3.5 %shard_map.41 = (f32[256,768]{1,0:T(8,128)S(1)}, f32[512,128]{1,0:T(8,128)S(1)}) custom-call(s32[1]{0:T(128)} %bitcast.chan_ref, s32[8]{0:T(128)S(1)} %copy-done.4, f32[1024,128]{1,0:T(8,128)S(1)} %shard_map.40.refs_0_, f32[1024,128]{1,0:T(8,128)S(1)} %collective-permute-done.3.refs_1_, f32[512,128]{1,0:T(8,128)S(1)} %slice_select_fusion.refs_2_), custom_call_target="tpu_custom_call" | custom-call | tf_op jit(solution)/shard_map/pallas_call | solution.py:257
  29.2 7.6 %collective-permute-done.1.right_ref = f32[1024,128]{1,0:T(8,128)S(1)} collective-permute-done((f32[1024,128]{1,0:T(8,128)S(1)}, f32[1024,128]{1,0:T(8,128)S(1)}, u32[]{:S(2)}, u32[]{:S(2)}) %collective-permute-start.1) | collective-permute-done | bytes 524320 | tf_op jit(solution)/shard_map/ppermute | solution.py:24
  36.9 1.9 %collective-permute-done.5.refs_1_ = f32[1024,128]{1,0:T(8,128)S(1)} collective-permute-done((f32[1024,128]{1,0:T(8,128)S(1)}, f32[1024,128]{1,0:T(8,128)S(1)}, u32[]{:S(2)}, u32[]{:S(2)}) %collective-permute-start.5) | collective-permute-done | bytes 524320 | tf_op jit(solution)/shard_map/ppermute | solution.py:24
  38.8 5.4 %shard_map.43 = f32[1152,128]{1,0:T(8,128)S(1)} custom-call(s32[1]{0:T(128)} %bitcast.chan_ref, s32[8]{0:T(128)S(1)} %copy-done.4, f32[1024,128]{1,0:T(8,128)S(1)} %shard_map.42.refs_0_, f32[1024,128]{1,0:T(8,128)S(1)} %collective-permute-done.5.refs_1_, f32[256,768]{1,0:T(8,128)S(1)} %get-tuple-element.12.refs_2_, ...), custom_call_target="tpu_custom_call" | custom-call | tf_op jit(solution)/shard_map/pallas_call | solution.py:257
  44.2 1.9 %collective-permute-start.12 = (f32[288,128]{1,0:T(8,128)S(1)}, f32[288,128]{1,0:T(8,128)S(1)}, u32[]{:S(2)}, u32[]{:S(2)}) collective-permute-start(f32[288,128]{1,0:T(8,128)S(1)} %constant_dynamic-slice_fusion.1), channel_id=1, source_target_pairs={{0,8},{4,12},{8,0},{12,4},{16,24},{20,28},{24,16},{28,20},{1,9},{5... | collective-permute-start | bytes 442376 | tf_op jit(solution)/shard_map/ppermute | solution.py:24
  46.1 1.6 %collective-permute-start.6 = (f32[288,128]{1,0:T(8,128)S(1)}, f32[288,128]{1,0:T(8,128)S(1)}, u32[]{:S(2)}, u32[]{:S(2)}) collective-permute-start(f32[288,128]{1,0:T(8,128)S(1)} %constant_dynamic-slice_fusion.3), channel_id=1, source_target_pairs={{0,4},{4,0},{8,12},{12,8},{16,20},{20,16},{24,28},{28,24},{1,5},{5... | collective-permute-start | bytes 442376 | tf_op jit(solution)/shard_map/ppermute | solution.py:24
  47.7 2.5 %collective-permute-done.12 = f32[288,128]{1,0:T(8,128)S(1)} collective-permute-done((f32[288,128]{1,0:T(8,128)S(1)}, f32[288,128]{1,0:T(8,128)S(1)}, u32[]{:S(2)}, u32[]{:S(2)}) %collective-permute-start.12) | collective-permute-done | bytes 147488 | tf_op jit(solution)/shard_map/ppermute | solution.py:24
  50.3 1.8 %collective-permute-start.13 = (f32[144,128]{1,0:T(8,128)S(1)}, f32[144,128]{1,0:T(8,128)S(1)}, u32[]{:S(2)}, u32[]{:S(2)}) collective-permute-start(f32[144,128]{1,0:T(8,128)S(1)} %constant_dynamic-slice_fusion), channel_id=1, source_target_pairs={{0,4},{4,0},{8,12},{12,8},{16,20},{20,16},{24,28},{28,24},{1,5},{5... | collective-permute-start | bytes 221192 | tf_op jit(solution)/shard_map/ppermute | solution.py:24
  52.1 1.6 %collective-permute-start.7 = (f32[144,128]{1,0:T(8,128)S(1)}, f32[144,128]{1,0:T(8,128)S(1)}, u32[]{:S(2)}, u32[]{:S(2)}) collective-permute-start(f32[144,128]{1,0:T(8,128)S(1)} %constant_dynamic-slice_fusion.2), channel_id=1, source_target_pairs={{0,8},{4,12},{8,0},{12,4},{16,24},{20,28},{24,16},{28,20},{1,9},{5... | collective-permute-start | bytes 221192 | tf_op jit(solution)/shard_map/ppermute | solution.py:24
  53.7 1.0 collective-permute-done.13
  54.7 2.8 %collective-permute-start.14 = (f32[144,128]{1,0:T(8,128)S(1)}, f32[144,128]{1,0:T(8,128)S(1)}, u32[]{:S(2)}, u32[]{:S(2)}) collective-permute-start(f32[144,128]{1,0:T(8,128)S(1)} %dynamic-slice_add_fusion.2), channel_id=1, source_target_pairs={{0,16},{4,20},{8,24},{12,28},{16,0},{20,4},{24,8},{28,12},{1,17},{... | collective-permute-start | bytes 221192 | tf_op jit(solution)/shard_map/ppermute | solution.py:24
  57.6 2.3 %collective-permute-start.8 = (f32[144,128]{1,0:T(8,128)S(1)}, f32[144,128]{1,0:T(8,128)S(1)}, u32[]{:S(2)}, u32[]{:S(2)}) collective-permute-start(f32[144,128]{1,0:T(8,128)S(1)} %dynamic-slice_add_fusion.3), channel_id=1, source_target_pairs={{0,16},{4,20},{8,24},{12,28},{16,0},{20,4},{24,8},{28,12},{1,17},{... | collective-permute-start | bytes 221192 | tf_op jit(solution)/shard_map/ppermute | solution.py:24
  59.8 2.3 %collective-permute-done.14 = f32[144,128]{1,0:T(8,128)S(1)} collective-permute-done((f32[144,128]{1,0:T(8,128)S(1)}, f32[144,128]{1,0:T(8,128)S(1)}, u32[]{:S(2)}, u32[]{:S(2)}) %collective-permute-start.14) | collective-permute-done | bytes 73760 | tf_op jit(solution)/shard_map/ppermute | solution.py:24
  62.2 1.6 %collective-permute-start.15 = (f32[144,128]{1,0:T(8,128)S(1)}, f32[144,128]{1,0:T(8,128)S(1)}, u32[]{:S(2)}, u32[]{:S(2)}) collective-permute-start(f32[144,128]{1,0:T(8,128)S(1)} %add.85), channel_id=1, source_target_pairs={{0,4},{4,0},{8,12},{12,8},{16,20},{20,16},{24,28},{28,24},{1,5},{5... | collective-permute-start | bytes 221192 | tf_op jit(solution)/shard_map/ppermute | solution.py:24
  63.8 0.7 collective-permute-start.9
  64.5 2.1 %collective-permute-done.15 = f32[144,128]{1,0:T(8,128)S(1)} collective-permute-done((f32[144,128]{1,0:T(8,128)S(1)}, f32[144,128]{1,0:T(8,128)S(1)}, u32[]{:S(2)}, u32[]{:S(2)}) %collective-permute-start.15) | collective-permute-done | bytes 73760 | tf_op jit(solution)/shard_map/ppermute | solution.py:24
  66.6 1.5 %collective-permute-start.16 = (f32[288,128]{1,0:T(8,128)S(1)}, f32[288,128]{1,0:T(8,128)S(1)}, u32[]{:S(2)}, u32[]{:S(2)}) collective-permute-start(f32[288,128]{1,0:T(8,128)S(1)} %pad_maximum_fusion.5), channel_id=1, source_target_pairs={{0,2},{1,3},{2,0},{3,1},{4,6},{5,7},{6,4},{7,5},{8,10},{9,11},{10,... | collective-permute-start | bytes 442376 | tf_op jit(solution)/shard_map/ppermute | solution.py:24
  68.3 1.5 %collective-permute-start.10 = (f32[288,128]{1,0:T(8,128)S(1)}, f32[288,128]{1,0:T(8,128)S(1)}, u32[]{:S(2)}, u32[]{:S(2)}) collective-permute-start(f32[288,128]{1,0:T(8,128)S(1)} %pad_maximum_fusion.4), channel_id=1, source_target_pairs={{0,4},{4,0},{8,12},{12,8},{16,20},{20,16},{24,28},{28,24},{1,5},{5... | collective-permute-start | bytes 442376 | tf_op jit(solution)/shard_map/ppermute | solution.py:24
  69.8 2.0 %collective-permute-done.16 = f32[288,128]{1,0:T(8,128)S(1)} collective-permute-done((f32[288,128]{1,0:T(8,128)S(1)}, f32[288,128]{1,0:T(8,128)S(1)}, u32[]{:S(2)}, u32[]{:S(2)}) %collective-permute-start.16) | collective-permute-done | bytes 147488 | tf_op jit(solution)/shard_map/ppermute | solution.py:24
  72.1 1.4 %collective-permute-done.10 = f32[288,128]{1,0:T(8,128)S(1)} collective-permute-done((f32[288,128]{1,0:T(8,128)S(1)}, f32[288,128]{1,0:T(8,128)S(1)}, u32[]{:S(2)}, u32[]{:S(2)}) %collective-permute-start.10) | collective-permute-done | bytes 147488 | tf_op jit(solution)/shard_map/ppermute | solution.py:24
  73.6 1.5 %collective-permute-start.11 = (f32[576,128]{1,0:T(8,128)S(1)}, f32[576,128]{1,0:T(8,128)S(1)}, u32[]{:S(2)}, u32[]{:S(2)}) collective-permute-start(f32[576,128]{1,0:T(8,128)S(1)} %pad_maximum_fusion.2), channel_id=1, source_target_pairs={{0,2},{1,3},{2,0},{3,1},{4,6},{5,7},{6,4},{7,5},{8,10},{9,11},{10,... | collective-permute-start | bytes 884744 | tf_op jit(solution)/shard_map/ppermute | solution.py:24
  75.1 3.6 %collective-permute-done.17 = f32[576,128]{1,0:T(8,128)S(1)} collective-permute-done((f32[576,128]{1,0:T(8,128)S(1)}, f32[576,128]{1,0:T(8,128)S(1)}, u32[]{:S(2)}, u32[]{:S(2)}) %collective-permute-start.17) | collective-permute-done | bytes 294944 | tf_op jit(solution)/shard_map/ppermute | solution.py:24
  78.9 1.5 %collective-permute-done.11 = f32[576,128]{1,0:T(8,128)S(1)} collective-permute-done((f32[576,128]{1,0:T(8,128)S(1)}, f32[576,128]{1,0:T(8,128)S(1)}, u32[]{:S(2)}, u32[]{:S(2)}) %collective-permute-start.11) | collective-permute-done | bytes 294944 | tf_op jit(solution)/shard_map/ppermute | solution.py:24
  80.9 1.7 %collective-permute-done.18.refs_2_ = f32[1152,128]{1,0:T(8,128)S(1)} collective-permute-done((f32[1152,128]{1,0:T(8,128)S(1)}, f32[1152,128]{1,0:T(8,128)S(1)}, u32[]{:S(2)}, u32[]{:S(2)}) %collective-permute-start.18) | collective-permute-done | bytes 589856 | tf_op jit(solution)/shard_map/ppermute | solution.py:24
  82.5 33.1 %shard_map.44 = f32[1024,1024]{1,0:T(8,128)} custom-call(s32[1]{0:T(128)S(6)} %select_n.148.half_ref, f32[1152,128]{1,0:T(8,128)S(1)} %pad_maximum_fusion.refs_0_, f32[1152,128]{1,0:T(8,128)S(1)} %pad_maximum_fusion.1.refs_1_, f32[1152,128]{1,0:T(8,128)S(1)} %collective-permute-done.18.refs_2_, f32[1152,128]{1,0:T(8,128)S(1)} %collective-permute-done.19.refs_3_), custom_call_target="tpu_custom_call" | custom-call | tf_op jit(solution)/shard_map/pallas_call | solution.py:463
  (50 shorter events, 4.0 us)
Async XLA Ops:
  0.0 4.7 %copy-start.3 = (s32[512]{0:T(512)S(1)}, s32[512]{0:T(512)}, u32[]{:S(2)}) copy-start(s32[512]{0:T(512)} %param.4) | copy-start | bytes 6148
  0.0 2.2 %copy-start = (bf16[4096,512]{1,0:T(8,128)(2,1)S(1)}, bf16[4096,512]{1,0:T(8,128)(2,1)}, u32[]{:S(2)}) copy-start(bf16[4096,512]{1,0:T(8,128)(2,1)} %signals_ref.3) | copy-start | bytes 12582916
  2.2 0.7 copy-start.2
  2.9 2.2 %copy-start.1 = (bf16[4096,512]{1,0:T(8,128)(2,1)S(1)}, bf16[4096,512]{1,0:T(8,128)(2,1)}, u32[]{:S(2)}) copy-start(bf16[4096,512]{1,0:T(8,128)(2,1)} %signals_ref.3) | copy-start | bytes 12582916
  4.1 21.5 %copy-start.4 = (s32[8]{0:T(128)S(1)}, s32[8]{0:T(128)}, u32[]{:S(2)}) copy-start(s32[8]{0:T(128)} %all_lags_ref.3) | copy-start | bytes 100
  4.2 2.8 %collective-permute-start = (f32[2048,128]{1,0:T(8,128)S(1)}, f32[2048,128]{1,0:T(8,128)S(1)}, u32[]{:S(2)}, u32[]{:S(2)}) collective-permute-start(f32[2048,128]{1,0:T(8,128)S(1)} %shard_map.38), channel_id=1, source_target_pairs={{0,1},{1,0},{2,3},{3,2},{4,5},{5,4},{6,7},{7,6},{8,9},{9,8},{10,11... | collective-permute-start | bytes 3145736 | tf_op jit(solution)/shard_map/ppermute | solution.py:24
  7.1 15.2 %collective-permute-start.2 = (f32[1024,128]{1,0:T(8,128)S(1)}, f32[1024,128]{1,0:T(8,128)S(1)}, u32[]{:S(2)}, u32[]{:S(2)}) collective-permute-start(f32[1024,128]{1,0:T(8,128)S(1)} %get-tuple-element.10.left_ref), channel_id=1, source_target_pairs={{0,2},{1,3},{2,0},{3,1},{4,6},{5,7},{6,4},{7,5},{8,10},{9,11},{10,... | collective-permute-start | bytes 1572872 | tf_op jit(solution)/shard_map/ppermute | solution.py:24
  22.3 2.0 %collective-permute-start.3 = (f32[1024,128]{1,0:T(8,128)S(1)}, f32[1024,128]{1,0:T(8,128)S(1)}, u32[]{:S(2)}, u32[]{:S(2)}) collective-permute-start(f32[1024,128]{1,0:T(8,128)S(1)} %shard_map.40.refs_0_), channel_id=1, source_target_pairs={{0,1},{1,0},{2,3},{3,2},{4,5},{5,4},{6,7},{7,6},{8,9},{9,8},{10,11... | collective-permute-start | bytes 1572872 | tf_op jit(solution)/shard_map/ppermute | solution.py:24
  22.4 14.3 %collective-permute-start.1 = (f32[1024,128]{1,0:T(8,128)S(1)}, f32[1024,128]{1,0:T(8,128)S(1)}, u32[]{:S(2)}, u32[]{:S(2)}) collective-permute-start(f32[1024,128]{1,0:T(8,128)S(1)} %get-tuple-element.9.left_ref), channel_id=1, source_target_pairs={{0,2},{1,3},{2,0},{3,1},{4,6},{5,7},{6,4},{7,5},{8,10},{9,11},{10,... | collective-permute-start | bytes 1572872 | tf_op jit(solution)/shard_map/ppermute | solution.py:24
  24.3 12.4 %collective-permute-start.4 = (f32[512,128]{1,0:T(8,128)S(1)}, f32[512,128]{1,0:T(8,128)S(1)}, u32[]{:S(2)}, u32[]{:S(2)}) collective-permute-start(f32[512,128]{1,0:T(8,128)S(1)} %slice_select_fusion.refs_2_), channel_id=1, source_target_pairs={{4,0},{8,4},{12,8},{16,12},{20,16},{24,20},{28,24},{5,1},{9,5},{13... | collective-permute-start | bytes 786440 | tf_op jit(solution)/shard_map/ppermute | solution.py:119
  36.8 2.0 %collective-permute-start.5 = (f32[1024,128]{1,0:T(8,128)S(1)}, f32[1024,128]{1,0:T(8,128)S(1)}, u32[]{:S(2)}, u32[]{:S(2)}) collective-permute-start(f32[1024,128]{1,0:T(8,128)S(1)} %shard_map.42.refs_0_), channel_id=1, source_target_pairs={{0,1},{1,0},{2,3},{3,2},{4,5},{5,4},{6,7},{7,6},{8,9},{9,8},{10,11... | collective-permute-start | bytes 1572872 | tf_op jit(solution)/shard_map/ppermute | solution.py:24
  44.2 6.0 %collective-permute-start.12 = (f32[288,128]{1,0:T(8,128)S(1)}, f32[288,128]{1,0:T(8,128)S(1)}, u32[]{:S(2)}, u32[]{:S(2)}) collective-permute-start(f32[288,128]{1,0:T(8,128)S(1)} %constant_dynamic-slice_fusion.1), channel_id=1, source_target_pairs={{0,8},{4,12},{8,0},{12,4},{16,24},{20,28},{24,16},{28,20},{1,9},{5... | collective-permute-start | bytes 442376 | tf_op jit(solution)/shard_map/ppermute | solution.py:24
  46.1 5.9 %collective-permute-start.6 = (f32[288,128]{1,0:T(8,128)S(1)}, f32[288,128]{1,0:T(8,128)S(1)}, u32[]{:S(2)}, u32[]{:S(2)}) collective-permute-start(f32[288,128]{1,0:T(8,128)S(1)} %constant_dynamic-slice_fusion.3), channel_id=1, source_target_pairs={{0,4},{4,0},{8,12},{12,8},{16,20},{20,16},{24,28},{28,24},{1,5},{5... | collective-permute-start | bytes 442376 | tf_op jit(solution)/shard_map/ppermute | solution.py:24
  50.3 4.4 %collective-permute-start.13 = (f32[144,128]{1,0:T(8,128)S(1)}, f32[144,128]{1,0:T(8,128)S(1)}, u32[]{:S(2)}, u32[]{:S(2)}) collective-permute-start(f32[144,128]{1,0:T(8,128)S(1)} %constant_dynamic-slice_fusion), channel_id=1, source_target_pairs={{0,4},{4,0},{8,12},{12,8},{16,20},{20,16},{24,28},{28,24},{1,5},{5... | collective-permute-start | bytes 221192 | tf_op jit(solution)/shard_map/ppermute | solution.py:24
  52.1 5.5 %collective-permute-start.7 = (f32[144,128]{1,0:T(8,128)S(1)}, f32[144,128]{1,0:T(8,128)S(1)}, u32[]{:S(2)}, u32[]{:S(2)}) collective-permute-start(f32[144,128]{1,0:T(8,128)S(1)} %constant_dynamic-slice_fusion.2), channel_id=1, source_target_pairs={{0,8},{4,12},{8,0},{12,4},{16,24},{20,28},{24,16},{28,20},{1,9},{5... | collective-permute-start | bytes 221192 | tf_op jit(solution)/shard_map/ppermute | solution.py:24
  54.7 7.4 %collective-permute-start.14 = (f32[144,128]{1,0:T(8,128)S(1)}, f32[144,128]{1,0:T(8,128)S(1)}, u32[]{:S(2)}, u32[]{:S(2)}) collective-permute-start(f32[144,128]{1,0:T(8,128)S(1)} %dynamic-slice_add_fusion.2), channel_id=1, source_target_pairs={{0,16},{4,20},{8,24},{12,28},{16,0},{20,4},{24,8},{28,12},{1,17},{... | collective-permute-start | bytes 221192 | tf_op jit(solution)/shard_map/ppermute | solution.py:24
  57.6 6.3 %collective-permute-start.8 = (f32[144,128]{1,0:T(8,128)S(1)}, f32[144,128]{1,0:T(8,128)S(1)}, u32[]{:S(2)}, u32[]{:S(2)}) collective-permute-start(f32[144,128]{1,0:T(8,128)S(1)} %dynamic-slice_add_fusion.3), channel_id=1, source_target_pairs={{0,16},{4,20},{8,24},{12,28},{16,0},{20,4},{24,8},{28,12},{1,17},{... | collective-permute-start | bytes 221192 | tf_op jit(solution)/shard_map/ppermute | solution.py:24
  62.2 4.4 %collective-permute-start.15 = (f32[144,128]{1,0:T(8,128)S(1)}, f32[144,128]{1,0:T(8,128)S(1)}, u32[]{:S(2)}, u32[]{:S(2)}) collective-permute-start(f32[144,128]{1,0:T(8,128)S(1)} %add.85), channel_id=1, source_target_pairs={{0,4},{4,0},{8,12},{12,8},{16,20},{20,16},{24,28},{28,24},{1,5},{5... | collective-permute-start | bytes 221192 | tf_op jit(solution)/shard_map/ppermute | solution.py:24
  63.8 4.4 %collective-permute-start.9 = (f32[144,128]{1,0:T(8,128)S(1)}, f32[144,128]{1,0:T(8,128)S(1)}, u32[]{:S(2)}, u32[]{:S(2)}) collective-permute-start(f32[144,128]{1,0:T(8,128)S(1)} %add.78), channel_id=1, source_target_pairs={{0,8},{4,12},{8,0},{12,4},{16,24},{20,28},{24,16},{28,20},{1,9},{5... | collective-permute-start | bytes 221192 | tf_op jit(solution)/shard_map/ppermute | solution.py:24
  66.6 5.2 %collective-permute-start.16 = (f32[288,128]{1,0:T(8,128)S(1)}, f32[288,128]{1,0:T(8,128)S(1)}, u32[]{:S(2)}, u32[]{:S(2)}) collective-permute-start(f32[288,128]{1,0:T(8,128)S(1)} %pad_maximum_fusion.5), channel_id=1, source_target_pairs={{0,2},{1,3},{2,0},{3,1},{4,6},{5,7},{6,4},{7,5},{8,10},{9,11},{10,... | collective-permute-start | bytes 442376 | tf_op jit(solution)/shard_map/ppermute | solution.py:24
  68.3 5.2 %collective-permute-start.10 = (f32[288,128]{1,0:T(8,128)S(1)}, f32[288,128]{1,0:T(8,128)S(1)}, u32[]{:S(2)}, u32[]{:S(2)}) collective-permute-start(f32[288,128]{1,0:T(8,128)S(1)} %pad_maximum_fusion.4), channel_id=1, source_target_pairs={{0,4},{4,0},{8,12},{12,8},{16,20},{20,16},{24,28},{28,24},{1,5},{5... | collective-permute-start | bytes 442376 | tf_op jit(solution)/shard_map/ppermute | solution.py:24
  71.9 6.8 %collective-permute-start.17 = (f32[576,128]{1,0:T(8,128)S(1)}, f32[576,128]{1,0:T(8,128)S(1)}, u32[]{:S(2)}, u32[]{:S(2)}) collective-permute-start(f32[576,128]{1,0:T(8,128)S(1)} %pad_maximum_fusion.3), channel_id=1, source_target_pairs={{0,8},{4,12},{8,0},{12,4},{16,24},{20,28},{24,16},{28,20},{1,9},{5... | collective-permute-start | bytes 884744 | tf_op jit(solution)/shard_map/ppermute | solution.py:24
  73.6 6.8 %collective-permute-start.11 = (f32[576,128]{1,0:T(8,128)S(1)}, f32[576,128]{1,0:T(8,128)S(1)}, u32[]{:S(2)}, u32[]{:S(2)}) collective-permute-start(f32[576,128]{1,0:T(8,128)S(1)} %pad_maximum_fusion.2), channel_id=1, source_target_pairs={{0,2},{1,3},{2,0},{3,1},{4,6},{5,7},{6,4},{7,5},{8,10},{9,11},{10,... | collective-permute-start | bytes 884744 | tf_op jit(solution)/shard_map/ppermute | solution.py:24
  78.8 2.1 %collective-permute-start.19 = (f32[1152,128]{1,0:T(8,128)S(1)}, f32[1152,128]{1,0:T(8,128)S(1)}, u32[]{:S(2)}, u32[]{:S(2)}) collective-permute-start(f32[1152,128]{1,0:T(8,128)S(1)} %pad_maximum_fusion.1.refs_1_), channel_id=1, source_target_pairs={{0,1},{1,0},{2,3},{3,2},{4,5},{5,4},{6,7},{7,6},{8,9},{9,8},{10,11... | collective-permute-start | bytes 1769480 | tf_op jit(solution)/shard_map/ppermute | solution.py:24
  80.4 2.1 %collective-permute-start.18 = (f32[1152,128]{1,0:T(8,128)S(1)}, f32[1152,128]{1,0:T(8,128)S(1)}, u32[]{:S(2)}, u32[]{:S(2)}) collective-permute-start(f32[1152,128]{1,0:T(8,128)S(1)} %pad_maximum_fusion.refs_0_), channel_id=1, source_target_pairs={{0,1},{1,0},{2,3},{3,2},{4,5},{5,4},{6,7},{7,6},{8,9},{9,8},{10,11... | collective-permute-start | bytes 1769480 | tf_op jit(solution)/shard_map/ppermute | solution.py:24

commit v8 on v7

--- a/solution.py
+++ b/solution.py
@@ -217,6 +217,7 @@
         total = total + product(high_ref[:, left], low_ref[...])
         total = total + product(low_ref[:, left], high_ref[...])
         sum_ref[...] += total
+        sum_ref[:, left] += product(low_ref[:, left], low_ref[:, left])
         return 0
 
     lax.fori_loop(0, steps, step, 0)
@@ -297,12 +298,14 @@
         top = jnp.where(here, jnp.where(lane == sub + first_lane, 1.0, 0.0), state[g])
         diagonal = jnp.zeros_like(top)
         scale, factors, rows = [], {}, []
+        pivots = [row_of(columns[m], m) for m in range(GROUP)]
         for m in range(GROUP):
-            pivot = row_of(columns[m], m)
+            pivot = pivots[m]
             scale.append(lax.rsqrt(pivot))
             left = columns[m] * scale[m]
             for n in range(m + 1, GROUP):
-                factors[m, n] = row_of(left, n)
+                factors[m, n] = row_of(columns[m], n) * scale[m]
+                pivots[n] = pivots[n] - factors[m, n] * factors[m, n]
                 columns[n] = columns[n] - left * factors[m, n]
             if more:
                 next_left[m] = next_left[m] * scale[m]
@@ -353,7 +356,7 @@
     return result, state
 
 
-def arrange(layout, half_ref, mine_refs, other_refs, natural_ref, ordered_ref):
+def arrange(scale, layout, half_ref, mine_refs, other_refs, natural_ref, ordered_ref):
     chan_count = 4
     lag_count = 2 * chan_count
     far = lag_count // 2
@@ -397,14 +400,18 @@
             target = pl.ds(pl.multiple_of(group * lag_count * width + lag * width, width), width)
             for half in range(2):
                 parts = [natural_ref[source, (4 * half + i) * NODES : (4 * half + i + 1) * NODES] for i in range(4)]
+                turned = []
+                for shift in range(4):
+                    value = parts[shift]
+                    for lane in range(1, 4):
+                        value = jnp.where(lane_part == lane, parts[(lane + shift) % 4], value)
+                    turned.append(pltpu.roll(value, shift * width, 1) if shift else value)
                 for other in range(group, chan_count):
-                    block = None
-                    for i in range(4):
-                        shift = (i - other) % 4 * width
-                        part = pltpu.roll(parts[i], shift, 1) if shift else parts[i]
-                        block = part if block is None else jnp.where(lane_part == i, part, block)
+                    block = turned[-other % 4]
+                    for i in range(1, 4):
+                        block = jnp.where(lane_part == i, turned[(i - other) % 4], block)
                     column = (2 * other + half) * BLOCK
-                    ordered_ref[target, column : column + BLOCK] = block
+                    ordered_ref[target, column : column + BLOCK] = block * scale
         return 0
 
     lax.fori_loop(0, lag_count, rows_of_lag, 0)
@@ -413,49 +420,49 @@
 def cholesky_kernel(scale, layout, half_ref, *refs):
     parts = len(layout)
     mine_refs, other_refs = refs[:parts], refs[parts : 2 * parts]
-    out_ref, natural_ref, ordered_ref, panel_ref, inverse_ref = refs[2 * parts :]
-    arrange(layout, half_ref, mine_refs, other_refs, natural_ref, ordered_ref)
-    size = out_ref.shape[0]
-    count = size // BLOCK
-    out_ref[...] = jnp.zeros_like(out_ref)
+    out_ref, natural_ref, ordered_ref, result_ref, panel_ref, inverse_ref, sent = refs[2 * parts :]
+    arrange(scale, layout, half_ref, mine_refs, other_refs, natural_ref, ordered_ref)
+    count = out_ref.shape[0] // BLOCK
+    result_ref[...] = jnp.zeros_like(result_ref)
+    panel_ref[...] = ordered_ref[:BLOCK, :]
+
+    def send(k):
+        rows = pl.ds(pl.multiple_of(k * BLOCK, BLOCK), BLOCK)
+        return pltpu.make_async_copy(result_ref.at[rows, :], out_ref.at[rows, :], sent.at[k])
 
     def step(k, _):
         start = pl.multiple_of(k * BLOCK, BLOCK)
-        for kk in range(count):
-
-            @pl.when(k == kk)
-            def _():
-                mine = slice(kk * BLOCK, (kk + 1) * BLOCK)
-                panel = ordered_ref[mine, kk * BLOCK :] * scale
-                if kk:
-                    panel = panel - lax.dot_general(
-                        out_ref[: kk * BLOCK, mine],
-                        out_ref[: kk * BLOCK, kk * BLOCK :],
-                        CONTRACT_ROWS,
-                        precision=HIGHEST,
-                        preferred_element_type=jnp.float32,
-                    )
-                panel_ref[:, kk * BLOCK :] = panel
-
         block = [panel_ref[GROUP * s : GROUP * (s + 1), pl.ds(start, BLOCK)] for s in range(BLOCK // GROUP)]
         block, inverse = factor_block(block)
         for s in range(BLOCK // GROUP):
-            out_ref[pl.ds(pl.multiple_of(start + GROUP * s, GROUP), GROUP), pl.ds(start, BLOCK)] = block[s]
+            result_ref[pl.ds(pl.multiple_of(start + GROUP * s, GROUP), GROUP), pl.ds(start, BLOCK)] = block[s]
             inverse_ref[GROUP * s : GROUP * (s + 1), :] = inverse[s]
         for kk in range(count - 1):
 
             @pl.when(k == kk)
             def _():
-                out_ref[kk * BLOCK : (kk + 1) * BLOCK, (kk + 1) * BLOCK :] = jnp.dot(
-                    inverse_ref[...],
-                    panel_ref[:, (kk + 1) * BLOCK :],
-                    precision=HIGHEST,
-                    preferred_element_type=jnp.float32,
+                now, later = kk * BLOCK, (kk + 1) * BLOCK
+                row = jnp.dot(
+                    inverse_ref[...], panel_ref[:, later:], precision=HIGHEST, preferred_element_type=jnp.float32
                 )
 
+                def product(left, right):
+                    return lax.dot_general(
+                        left, right, CONTRACT_ROWS, precision=HIGHEST, preferred_element_type=jnp.float32
+                    )
+
+                panel = ordered_ref[later : later + BLOCK, later:]
+                if kk:
+                    panel = panel - product(result_ref[:now, later : later + BLOCK], result_ref[:now, later:])
+                result_ref[now:later, later:] = row
+                panel_ref[:, later:] = panel - product(row[:, :BLOCK], row)
+
+        send(k).start()
         return 0
 
     lax.fori_loop(0, count, step, 0)
+    for k in range(count):
+        send(k).wait()
 
 
 def cholesky(half, mine, other, layout, size, scale):
@@ -464,12 +471,14 @@
         functools.partial(cholesky_kernel, scale, layout),
         out_shape=jax.ShapeDtypeStruct((size, size), jnp.float32),
         in_specs=[pl.BlockSpec(memory_space=pltpu.SMEM)] + [vmem] * (2 * len(mine)),
-        out_specs=vmem,
+        out_specs=pl.BlockSpec(memory_space=pl.ANY),
         scratch_shapes=[
+            pltpu.VMEM((size, size), jnp.float32),
             pltpu.VMEM((size, size), jnp.float32),
             pltpu.VMEM((size, size), jnp.float32),
             pltpu.VMEM((BLOCK, size), jnp.float32),
             pltpu.VMEM((BLOCK, BLOCK), jnp.float32),
+            pltpu.SemaphoreType.DMA((size // BLOCK,)),
         ],
         compiler_params=pltpu.CompilerParams(vmem_limit_bytes=24 << 20),
     )(half, *mine, *other)

time: 116 us -> 112 us (0.966)
  Pallas kernels: 44.7 us -> 41.3 us
    pallas_call x1, Pallas kernels: 33.1 us -> 29.2 us  [cholesky(): pl.pallas_call(functools.partial(cholesky_kernel, scale, layout), out_sha...]
  transfers between devices with their start and end apart: 20 -> 20, of which waited for: 16 -> 15; matrix products, arithmetic and copies ran while one was open for 0% -> 0% of each run, Pallas kernels for 4% -> 4%
where the time goes in v8:
time: 112 us
  Pallas kernels  41.3 us (37%)
  waiting for transfers between devices  40.8 us (36%)
  starting transfers between devices  25.8 us (23%)
  local copies, waits for them, and re-layouts  3.39 us (3%)
    ppermute x19, waiting for transfers between devices, swap(): return lax.ppermute(value, axis, [(i, i ^ bit) for i in range(count)])  40.8 us
    pallas_call x1, Pallas kernels, cholesky(): pl.pallas_call(functools.partial(cholesky_kernel, scale, layout), out_sha...  29.2 us
    ppermute x19, starting transfers between devices, swap(): return lax.ppermute(value, axis, [(i, i ^ bit) for i in range(count)])  24.5 us
    pallas_call x2, Pallas kernels, gram_part(): pl.pallas_call(functools.partial(gram_kernel, first, last, len(earlier)),...  9.39 us
    unnamed x10, local copies, waits for them, and re-layouts  3.29 us
    pallas_call x2, Pallas kernels, project(): pl.pallas_call(project_kernel, out_shape=jax.ShapeDtypeStruct((rows // 2,...  2.51 us
  transfers between devices with their start and end apart: 20, of which 15 were waited for; matrix products, arithmetic and copies ran while one was open for 0% of the time, Pallas kernels for 4%

profile of v8, /device:TPU:0, one launch (start us, length us, event | category | flops | bytes accessed | tf_op | source)
XLA Modules:
  0.0 112.1 jit_solution(11044687650576681890)
XLA Ops:
  0.0 2.2 %copy-done = bf16[4096,512]{1,0:T(8,128)(2,1)S(1)} copy-done((bf16[4096,512]{1,0:T(8,128)(2,1)S(1)}, bf16[4096,512]{1,0:T(8,128)(2,1)}, u32[]{:S(2)}) %copy-start) | copy-done | bytes 4194328
  2.9 1.2 %shard_map.38 = f32[2048,128]{1,0:T(8,128)S(1)} custom-call(s32[1]{0:T(128)S(6)} %sub.28.half_ref, s32[1,512]{1,0:T(1,128)S(1)} %bitcast.3, bf16[4096,512]{1,0:T(8,128)(2,1)S(1)} %copy-done), custom_call_target="tpu_custom_call" | custom-call | tf_op jit(solution)/shard_map/pallas_call | solution.py:162
  5.1 1.3 %shard_map.37.left_ref = f32[2048,128]{1,0:T(8,128)S(1)} custom-call(s32[1]{0:T(128)S(6)} %select_n.148.half_ref, s32[1,512]{1,0:T(1,128)S(1)} %bitcast.4, bf16[4096,512]{1,0:T(8,128)(2,1)S(1)} %copy-done.1), custom_call_target="tpu_custom_call" | custom-call | tf_op jit(solution)/shard_map/pallas_call | solution.py:162
  7.1 2.9 %collective-permute-start.2 = (f32[1024,128]{1,0:T(8,128)S(1)}, f32[1024,128]{1,0:T(8,128)S(1)}, u32[]{:S(2)}, u32[]{:S(2)}) collective-permute-start(f32[1024,128]{1,0:T(8,128)S(1)} %get-tuple-element.10.left_ref), channel_id=1, source_target_pairs={{0,2},{1,3},{2,0},{3,1},{4,6},{5,7},{6,4},{7,5},{8,10},{9,11},{10,... | collective-permute-start | bytes 1572872 | tf_op jit(solution)/shard_map/ppermute | solution.py:24
  10.0 12.2 %collective-permute-done.2.right_ref = f32[1024,128]{1,0:T(8,128)S(1)} collective-permute-done((f32[1024,128]{1,0:T(8,128)S(1)}, f32[1024,128]{1,0:T(8,128)S(1)}, u32[]{:S(2)}, u32[]{:S(2)}) %collective-permute-start.2) | collective-permute-done | bytes 524320 | tf_op jit(solution)/shard_map/ppermute | solution.py:24
  22.4 1.8 %collective-permute-start.1 = (f32[1024,128]{1,0:T(8,128)S(1)}, f32[1024,128]{1,0:T(8,128)S(1)}, u32[]{:S(2)}, u32[]{:S(2)}) collective-permute-start(f32[1024,128]{1,0:T(8,128)S(1)} %get-tuple-element.9.left_ref), channel_id=1, source_target_pairs={{0,2},{1,3},{2,0},{3,1},{4,6},{5,7},{6,4},{7,5},{8,10},{9,11},{10,... | collective-permute-start | bytes 1572872 | tf_op jit(solution)/shard_map/ppermute | solution.py:24
  24.3 1.3 %collective-permute-start.4 = (f32[512,128]{1,0:T(8,128)S(1)}, f32[512,128]{1,0:T(8,128)S(1)}, u32[]{:S(2)}, u32[]{:S(2)}) collective-permute-start(f32[512,128]{1,0:T(8,128)S(1)} %slice_select_fusion.refs_2_), channel_id=1, source_target_pairs={{4,0},{8,4},{12,8},{16,12},{20,16},{24,20},{28,24},{5,1},{9,5},{13... | collective-permute-start | bytes 786440 | tf_op jit(solution)/shard_map/ppermute | solution.py:119
  25.6 3.7 %shard_map.41 = (f32[256,768]{1,0:T(8,128)S(1)}, f32[512,128]{1,0:T(8,128)S(1)}) custom-call(s32[1]{0:T(128)} %bitcast.chan_ref, s32[8]{0:T(128)S(1)} %copy-done.4, f32[1024,128]{1,0:T(8,128)S(1)} %shard_map.40.refs_0_, f32[1024,128]{1,0:T(8,128)S(1)} %collective-permute-done.3.refs_1_, f32[512,128]{1,0:T(8,128)S(1)} %slice_select_fusion.refs_2_), custom_call_target="tpu_custom_call" | custom-call | tf_op jit(solution)/shard_map/pallas_call | solution.py:258
  29.4 7.4 %collective-permute-done.1.right_ref = f32[1024,128]{1,0:T(8,128)S(1)} collective-permute-done((f32[1024,128]{1,0:T(8,128)S(1)}, f32[1024,128]{1,0:T(8,128)S(1)}, u32[]{:S(2)}, u32[]{:S(2)}) %collective-permute-start.1) | collective-permute-done | bytes 524320 | tf_op jit(solution)/shard_map/ppermute | solution.py:24
  36.9 1.9 %collective-permute-done.5.refs_1_ = f32[1024,128]{1,0:T(8,128)S(1)} collective-permute-done((f32[1024,128]{1,0:T(8,128)S(1)}, f32[1024,128]{1,0:T(8,128)S(1)}, u32[]{:S(2)}, u32[]{:S(2)}) %collective-permute-start.5) | collective-permute-done | bytes 524320 | tf_op jit(solution)/shard_map/ppermute | solution.py:24
  38.8 5.7 %shard_map.43 = f32[1152,128]{1,0:T(8,128)S(1)} custom-call(s32[1]{0:T(128)} %bitcast.chan_ref, s32[8]{0:T(128)S(1)} %copy-done.4, f32[1024,128]{1,0:T(8,128)S(1)} %shard_map.42.refs_0_, f32[1024,128]{1,0:T(8,128)S(1)} %collective-permute-done.5.refs_1_, f32[256,768]{1,0:T(8,128)S(1)} %get-tuple-element.12.refs_2_, ...), custom_call_target="tpu_custom_call" | custom-call | tf_op jit(solution)/shard_map/pallas_call | solution.py:258
  44.5 1.9 %collective-permute-start.12 = (f32[288,128]{1,0:T(8,128)S(1)}, f32[288,128]{1,0:T(8,128)S(1)}, u32[]{:S(2)}, u32[]{:S(2)}) collective-permute-start(f32[288,128]{1,0:T(8,128)S(1)} %constant_dynamic-slice_fusion.1), channel_id=1, source_target_pairs={{0,8},{4,12},{8,0},{12,4},{16,24},{20,28},{24,16},{28,20},{1,9},{5... | collective-permute-start | bytes 442376 | tf_op jit(solution)/shard_map/ppermute | solution.py:24
  46.4 1.6 %collective-permute-start.6 = (f32[288,128]{1,0:T(8,128)S(1)}, f32[288,128]{1,0:T(8,128)S(1)}, u32[]{:S(2)}, u32[]{:S(2)}) collective-permute-start(f32[288,128]{1,0:T(8,128)S(1)} %constant_dynamic-slice_fusion.3), channel_id=1, source_target_pairs={{0,4},{4,0},{8,12},{12,8},{16,20},{20,16},{24,28},{28,24},{1,5},{5... | collective-permute-start | bytes 442376 | tf_op jit(solution)/shard_map/ppermute | solution.py:24
  48.0 2.5 %collective-permute-done.12 = f32[288,128]{1,0:T(8,128)S(1)} collective-permute-done((f32[288,128]{1,0:T(8,128)S(1)}, f32[288,128]{1,0:T(8,128)S(1)}, u32[]{:S(2)}, u32[]{:S(2)}) %collective-permute-start.12) | collective-permute-done | bytes 147488 | tf_op jit(solution)/shard_map/ppermute | solution.py:24
  50.6 1.8 %collective-permute-start.13 = (f32[144,128]{1,0:T(8,128)S(1)}, f32[144,128]{1,0:T(8,128)S(1)}, u32[]{:S(2)}, u32[]{:S(2)}) collective-permute-start(f32[144,128]{1,0:T(8,128)S(1)} %constant_dynamic-slice_fusion), channel_id=1, source_target_pairs={{0,4},{4,0},{8,12},{12,8},{16,20},{20,16},{24,28},{28,24},{1,5},{5... | collective-permute-start | bytes 221192 | tf_op jit(solution)/shard_map/ppermute | solution.py:24
  52.4 1.6 %collective-permute-start.7 = (f32[144,128]{1,0:T(8,128)S(1)}, f32[144,128]{1,0:T(8,128)S(1)}, u32[]{:S(2)}, u32[]{:S(2)}) collective-permute-start(f32[144,128]{1,0:T(8,128)S(1)} %constant_dynamic-slice_fusion.2), channel_id=1, source_target_pairs={{0,8},{4,12},{8,0},{12,4},{16,24},{20,28},{24,16},{28,20},{1,9},{5... | collective-permute-start | bytes 221192 | tf_op jit(solution)/shard_map/ppermute | solution.py:24
  54.0 1.0 collective-permute-done.13
  55.0 2.8 %collective-permute-start.14 = (f32[144,128]{1,0:T(8,128)S(1)}, f32[144,128]{1,0:T(8,128)S(1)}, u32[]{:S(2)}, u32[]{:S(2)}) collective-permute-start(f32[144,128]{1,0:T(8,128)S(1)} %dynamic-slice_add_fusion.2), channel_id=1, source_target_pairs={{0,16},{4,20},{8,24},{12,28},{16,0},{20,4},{24,8},{28,12},{1,17},{... | collective-permute-start | bytes 221192 | tf_op jit(solution)/shard_map/ppermute | solution.py:24
  57.9 2.3 %collective-permute-start.8 = (f32[144,128]{1,0:T(8,128)S(1)}, f32[144,128]{1,0:T(8,128)S(1)}, u32[]{:S(2)}, u32[]{:S(2)}) collective-permute-start(f32[144,128]{1,0:T(8,128)S(1)} %dynamic-slice_add_fusion.3), channel_id=1, source_target_pairs={{0,16},{4,20},{8,24},{12,28},{16,0},{20,4},{24,8},{28,12},{1,17},{... | collective-permute-start | bytes 221192 | tf_op jit(solution)/shard_map/ppermute | solution.py:24
  60.1 2.3 %collective-permute-done.14 = f32[144,128]{1,0:T(8,128)S(1)} collective-permute-done((f32[144,128]{1,0:T(8,128)S(1)}, f32[144,128]{1,0:T(8,128)S(1)}, u32[]{:S(2)}, u32[]{:S(2)}) %collective-permute-start.14) | collective-permute-done | bytes 73760 | tf_op jit(solution)/shard_map/ppermute | solution.py:24
  62.5 1.6 %collective-permute-start.15 = (f32[144,128]{1,0:T(8,128)S(1)}, f32[144,128]{1,0:T(8,128)S(1)}, u32[]{:S(2)}, u32[]{:S(2)}) collective-permute-start(f32[144,128]{1,0:T(8,128)S(1)} %add.85), channel_id=1, source_target_pairs={{0,4},{4,0},{8,12},{12,8},{16,20},{20,16},{24,28},{28,24},{1,5},{5... | collective-permute-start | bytes 221192 | tf_op jit(solution)/shard_map/ppermute | solution.py:24
  64.1 0.7 collective-permute-start.9
  64.8 2.1 %collective-permute-done.15 = f32[144,128]{1,0:T(8,128)S(1)} collective-permute-done((f32[144,128]{1,0:T(8,128)S(1)}, f32[144,128]{1,0:T(8,128)S(1)}, u32[]{:S(2)}, u32[]{:S(2)}) %collective-permute-start.15) | collective-permute-done | bytes 73760 | tf_op jit(solution)/shard_map/ppermute | solution.py:24
  66.9 1.6 %collective-permute-start.16 = (f32[288,128]{1,0:T(8,128)S(1)}, f32[288,128]{1,0:T(8,128)S(1)}, u32[]{:S(2)}, u32[]{:S(2)}) collective-permute-start(f32[288,128]{1,0:T(8,128)S(1)} %pad_maximum_fusion.5), channel_id=1, source_target_pairs={{0,2},{1,3},{2,0},{3,1},{4,6},{5,7},{6,4},{7,5},{8,10},{9,11},{10,... | collective-permute-start | bytes 442376 | tf_op jit(solution)/shard_map/ppermute | solution.py:24
  68.6 1.5 %collective-permute-start.10 = (f32[288,128]{1,0:T(8,128)S(1)}, f32[288,128]{1,0:T(8,128)S(1)}, u32[]{:S(2)}, u32[]{:S(2)}) collective-permute-start(f32[288,128]{1,0:T(8,128)S(1)} %pad_maximum_fusion.4), channel_id=1, source_target_pairs={{0,4},{4,0},{8,12},{12,8},{16,20},{20,16},{24,28},{28,24},{1,5},{5... | collective-permute-start | bytes 442376 | tf_op jit(solution)/shard_map/ppermute | solution.py:24
  70.1 2.1 %collective-permute-done.16 = f32[288,128]{1,0:T(8,128)S(1)} collective-permute-done((f32[288,128]{1,0:T(8,128)S(1)}, f32[288,128]{1,0:T(8,128)S(1)}, u32[]{:S(2)}, u32[]{:S(2)}) %collective-permute-start.16) | collective-permute-done | bytes 147488 | tf_op jit(solution)/shard_map/ppermute | solution.py:24
  72.3 1.5 %collective-permute-done.10 = f32[288,128]{1,0:T(8,128)S(1)} collective-permute-done((f32[288,128]{1,0:T(8,128)S(1)}, f32[288,128]{1,0:T(8,128)S(1)}, u32[]{:S(2)}, u32[]{:S(2)}) %collective-permute-start.10) | collective-permute-done | bytes 147488 | tf_op jit(solution)/shard_map/ppermute | solution.py:24
  73.9 1.5 %collective-permute-start.11 = (f32[576,128]{1,0:T(8,128)S(1)}, f32[576,128]{1,0:T(8,128)S(1)}, u32[]{:S(2)}, u32[]{:S(2)}) collective-permute-start(f32[576,128]{1,0:T(8,128)S(1)} %pad_maximum_fusion.2), channel_id=1, source_target_pairs={{0,2},{1,3},{2,0},{3,1},{4,6},{5,7},{6,4},{7,5},{8,10},{9,11},{10,... | collective-permute-start | bytes 884744 | tf_op jit(solution)/shard_map/ppermute | solution.py:24
  75.3 3.7 %collective-permute-done.17 = f32[576,128]{1,0:T(8,128)S(1)} collective-permute-done((f32[576,128]{1,0:T(8,128)S(1)}, f32[576,128]{1,0:T(8,128)S(1)}, u32[]{:S(2)}, u32[]{:S(2)}) %collective-permute-start.17) | collective-permute-done | bytes 294944 | tf_op jit(solution)/shard_map/ppermute | solution.py:24
  79.2 1.5 %collective-permute-done.11 = f32[576,128]{1,0:T(8,128)S(1)} collective-permute-done((f32[576,128]{1,0:T(8,128)S(1)}, f32[576,128]{1,0:T(8,128)S(1)}, u32[]{:S(2)}, u32[]{:S(2)}) %collective-permute-start.11) | collective-permute-done | bytes 294944 | tf_op jit(solution)/shard_map/ppermute | solution.py:24
  81.2 1.7 %collective-permute-done.18.refs_2_ = f32[1152,128]{1,0:T(8,128)S(1)} collective-permute-done((f32[1152,128]{1,0:T(8,128)S(1)}, f32[1152,128]{1,0:T(8,128)S(1)}, u32[]{:S(2)}, u32[]{:S(2)}) %collective-permute-start.18) | collective-permute-done | bytes 589856 | tf_op jit(solution)/shard_map/ppermute | solution.py:24
  82.8 29.2 %shard_map.44 = f32[1024,1024]{1,0:T(8,128)} custom-call(s32[1]{0:T(128)S(6)} %select_n.148.half_ref, f32[1152,128]{1,0:T(8,128)S(1)} %pad_maximum_fusion.refs_0_, f32[1152,128]{1,0:T(8,128)S(1)} %pad_maximum_fusion.1.refs_1_, f32[1152,128]{1,0:T(8,128)S(1)} %collective-permute-done.18.refs_2_, f32[1152,128]{1,0:T(8,128)S(1)} %collective-permute-done.19.refs_3_), custom_call_target="tpu_custom_call" | custom-call | tf_op jit(solution)/shard_map/pallas_call | solution.py:470
  (50 shorter events, 3.9 us)
Async XLA Ops:
  0.0 4.7 %copy-start.3 = (s32[512]{0:T(512)S(1)}, s32[512]{0:T(512)}, u32[]{:S(2)}) copy-start(s32[512]{0:T(512)} %param.4) | copy-start | bytes 6148
  0.0 2.2 %copy-start = (bf16[4096,512]{1,0:T(8,128)(2,1)S(1)}, bf16[4096,512]{1,0:T(8,128)(2,1)}, u32[]{:S(2)}) copy-start(bf16[4096,512]{1,0:T(8,128)(2,1)} %signals_ref.3) | copy-start | bytes 12582916
  2.2 0.7 copy-start.2
  2.9 2.2 %copy-start.1 = (bf16[4096,512]{1,0:T(8,128)(2,1)S(1)}, bf16[4096,512]{1,0:T(8,128)(2,1)}, u32[]{:S(2)}) copy-start(bf16[4096,512]{1,0:T(8,128)(2,1)} %signals_ref.3) | copy-start | bytes 12582916
  4.1 21.5 %copy-start.4 = (s32[8]{0:T(128)S(1)}, s32[8]{0:T(128)}, u32[]{:S(2)}) copy-start(s32[8]{0:T(128)} %all_lags_ref.3) | copy-start | bytes 100
  4.2 2.8 %collective-permute-start = (f32[2048,128]{1,0:T(8,128)S(1)}, f32[2048,128]{1,0:T(8,128)S(1)}, u32[]{:S(2)}, u32[]{:S(2)}) collective-permute-start(f32[2048,128]{1,0:T(8,128)S(1)} %shard_map.38), channel_id=1, source_target_pairs={{0,1},{1,0},{2,3},{3,2},{4,5},{5,4},{6,7},{7,6},{8,9},{9,8},{10,11... | collective-permute-start | bytes 3145736 | tf_op jit(solution)/shard_map/ppermute | solution.py:24
  7.1 15.2 %collective-permute-start.2 = (f32[1024,128]{1,0:T(8,128)S(1)}, f32[1024,128]{1,0:T(8,128)S(1)}, u32[]{:S(2)}, u32[]{:S(2)}) collective-permute-start(f32[1024,128]{1,0:T(8,128)S(1)} %get-tuple-element.10.left_ref), channel_id=1, source_target_pairs={{0,2},{1,3},{2,0},{3,1},{4,6},{5,7},{6,4},{7,5},{8,10},{9,11},{10,... | collective-permute-start | bytes 1572872 | tf_op jit(solution)/shard_map/ppermute | solution.py:24
  22.3 2.0 %collective-permute-start.3 = (f32[1024,128]{1,0:T(8,128)S(1)}, f32[1024,128]{1,0:T(8,128)S(1)}, u32[]{:S(2)}, u32[]{:S(2)}) collective-permute-start(f32[1024,128]{1,0:T(8,128)S(1)} %shard_map.40.refs_0_), channel_id=1, source_target_pairs={{0,1},{1,0},{2,3},{3,2},{4,5},{5,4},{6,7},{7,6},{8,9},{9,8},{10,11... | collective-permute-start | bytes 1572872 | tf_op jit(solution)/shard_map/ppermute | solution.py:24
  22.4 14.3 %collective-permute-start.1 = (f32[1024,128]{1,0:T(8,128)S(1)}, f32[1024,128]{1,0:T(8,128)S(1)}, u32[]{:S(2)}, u32[]{:S(2)}) collective-permute-start(f32[1024,128]{1,0:T(8,128)S(1)} %get-tuple-element.9.left_ref), channel_id=1, source_target_pairs={{0,2},{1,3},{2,0},{3,1},{4,6},{5,7},{6,4},{7,5},{8,10},{9,11},{10,... | collective-permute-start | bytes 1572872 | tf_op jit(solution)/shard_map/ppermute | solution.py:24
  24.3 12.4 %collective-permute-start.4 = (f32[512,128]{1,0:T(8,128)S(1)}, f32[512,128]{1,0:T(8,128)S(1)}, u32[]{:S(2)}, u32[]{:S(2)}) collective-permute-start(f32[512,128]{1,0:T(8,128)S(1)} %slice_select_fusion.refs_2_), channel_id=1, source_target_pairs={{4,0},{8,4},{12,8},{16,12},{20,16},{24,20},{28,24},{5,1},{9,5},{13... | collective-permute-start | bytes 786440 | tf_op jit(solution)/shard_map/ppermute | solution.py:119
  36.8 2.0 %collective-permute-start.5 = (f32[1024,128]{1,0:T(8,128)S(1)}, f32[1024,128]{1,0:T(8,128)S(1)}, u32[]{:S(2)}, u32[]{:S(2)}) collective-permute-start(f32[1024,128]{1,0:T(8,128)S(1)} %shard_map.42.refs_0_), channel_id=1, source_target_pairs={{0,1},{1,0},{2,3},{3,2},{4,5},{5,4},{6,7},{7,6},{8,9},{9,8},{10,11... | collective-permute-start | bytes 1572872 | tf_op jit(solution)/shard_map/ppermute | solution.py:24
  44.5 6.0 %collective-permute-start.12 = (f32[288,128]{1,0:T(8,128)S(1)}, f32[288,128]{1,0:T(8,128)S(1)}, u32[]{:S(2)}, u32[]{:S(2)}) collective-permute-start(f32[288,128]{1,0:T(8,128)S(1)} %constant_dynamic-slice_fusion.1), channel_id=1, source_target_pairs={{0,8},{4,12},{8,0},{12,4},{16,24},{20,28},{24,16},{28,20},{1,9},{5... | collective-permute-start | bytes 442376 | tf_op jit(solution)/shard_map/ppermute | solution.py:24
  46.4 5.9 %collective-permute-start.6 = (f32[288,128]{1,0:T(8,128)S(1)}, f32[288,128]{1,0:T(8,128)S(1)}, u32[]{:S(2)}, u32[]{:S(2)}) collective-permute-start(f32[288,128]{1,0:T(8,128)S(1)} %constant_dynamic-slice_fusion.3), channel_id=1, source_target_pairs={{0,4},{4,0},{8,12},{12,8},{16,20},{20,16},{24,28},{28,24},{1,5},{5... | collective-permute-start | bytes 442376 | tf_op jit(solution)/shard_map/ppermute | solution.py:24
  50.6 4.4 %collective-permute-start.13 = (f32[144,128]{1,0:T(8,128)S(1)}, f32[144,128]{1,0:T(8,128)S(1)}, u32[]{:S(2)}, u32[]{:S(2)}) collective-permute-start(f32[144,128]{1,0:T(8,128)S(1)} %constant_dynamic-slice_fusion), channel_id=1, source_target_pairs={{0,4},{4,0},{8,12},{12,8},{16,20},{20,16},{24,28},{28,24},{1,5},{5... | collective-permute-start | bytes 221192 | tf_op jit(solution)/shard_map/ppermute | solution.py:24
  52.4 5.5 %collective-permute-start.7 = (f32[144,128]{1,0:T(8,128)S(1)}, f32[144,128]{1,0:T(8,128)S(1)}, u32[]{:S(2)}, u32[]{:S(2)}) collective-permute-start(f32[144,128]{1,0:T(8,128)S(1)} %constant_dynamic-slice_fusion.2), channel_id=1, source_target_pairs={{0,8},{4,12},{8,0},{12,4},{16,24},{20,28},{24,16},{28,20},{1,9},{5... | collective-permute-start | bytes 221192 | tf_op jit(solution)/shard_map/ppermute | solution.py:24
  55.0 7.4 %collective-permute-start.14 = (f32[144,128]{1,0:T(8,128)S(1)}, f32[144,128]{1,0:T(8,128)S(1)}, u32[]{:S(2)}, u32[]{:S(2)}) collective-permute-start(f32[144,128]{1,0:T(8,128)S(1)} %dynamic-slice_add_fusion.2), channel_id=1, source_target_pairs={{0,16},{4,20},{8,24},{12,28},{16,0},{20,4},{24,8},{28,12},{1,17},{... | collective-permute-start | bytes 221192 | tf_op jit(solution)/shard_map/ppermute | solution.py:24
  57.9 6.3 %collective-permute-start.8 = (f32[144,128]{1,0:T(8,128)S(1)}, f32[144,128]{1,0:T(8,128)S(1)}, u32[]{:S(2)}, u32[]{:S(2)}) collective-permute-start(f32[144,128]{1,0:T(8,128)S(1)} %dynamic-slice_add_fusion.3), channel_id=1, source_target_pairs={{0,16},{4,20},{8,24},{12,28},{16,0},{20,4},{24,8},{28,12},{1,17},{... | collective-permute-start | bytes 221192 | tf_op jit(solution)/shard_map/ppermute | solution.py:24
  62.5 4.4 %collective-permute-start.15 = (f32[144,128]{1,0:T(8,128)S(1)}, f32[144,128]{1,0:T(8,128)S(1)}, u32[]{:S(2)}, u32[]{:S(2)}) collective-permute-start(f32[144,128]{1,0:T(8,128)S(1)} %add.85), channel_id=1, source_target_pairs={{0,4},{4,0},{8,12},{12,8},{16,20},{20,16},{24,28},{28,24},{1,5},{5... | collective-permute-start | bytes 221192 | tf_op jit(solution)/shard_map/ppermute | solution.py:24
  64.1 4.4 %collective-permute-start.9 = (f32[144,128]{1,0:T(8,128)S(1)}, f32[144,128]{1,0:T(8,128)S(1)}, u32[]{:S(2)}, u32[]{:S(2)}) collective-permute-start(f32[144,128]{1,0:T(8,128)S(1)} %add.78), channel_id=1, source_target_pairs={{0,8},{4,12},{8,0},{12,4},{16,24},{20,28},{24,16},{28,20},{1,9},{5... | collective-permute-start | bytes 221192 | tf_op jit(solution)/shard_map/ppermute | solution.py:24
  66.9 5.2 %collective-permute-start.16 = (f32[288,128]{1,0:T(8,128)S(1)}, f32[288,128]{1,0:T(8,128)S(1)}, u32[]{:S(2)}, u32[]{:S(2)}) collective-permute-start(f32[288,128]{1,0:T(8,128)S(1)} %pad_maximum_fusion.5), channel_id=1, source_target_pairs={{0,2},{1,3},{2,0},{3,1},{4,6},{5,7},{6,4},{7,5},{8,10},{9,11},{10,... | collective-permute-start | bytes 442376 | tf_op jit(solution)/shard_map/ppermute | solution.py:24
  68.6 5.2 %collective-permute-start.10 = (f32[288,128]{1,0:T(8,128)S(1)}, f32[288,128]{1,0:T(8,128)S(1)}, u32[]{:S(2)}, u32[]{:S(2)}) collective-permute-start(f32[288,128]{1,0:T(8,128)S(1)} %pad_maximum_fusion.4), channel_id=1, source_target_pairs={{0,4},{4,0},{8,12},{12,8},{16,20},{20,16},{24,28},{28,24},{1,5},{5... | collective-permute-start | bytes 442376 | tf_op jit(solution)/shard_map/ppermute | solution.py:24
  72.2 6.8 %collective-permute-start.17 = (f32[576,128]{1,0:T(8,128)S(1)}, f32[576,128]{1,0:T(8,128)S(1)}, u32[]{:S(2)}, u32[]{:S(2)}) collective-permute-start(f32[576,128]{1,0:T(8,128)S(1)} %pad_maximum_fusion.3), channel_id=1, source_target_pairs={{0,8},{4,12},{8,0},{12,4},{16,24},{20,28},{24,16},{28,20},{1,9},{5... | collective-permute-start | bytes 884744 | tf_op jit(solution)/shard_map/ppermute | solution.py:24
  73.9 6.8 %collective-permute-start.11 = (f32[576,128]{1,0:T(8,128)S(1)}, f32[576,128]{1,0:T(8,128)S(1)}, u32[]{:S(2)}, u32[]{:S(2)}) collective-permute-start(f32[576,128]{1,0:T(8,128)S(1)} %pad_maximum_fusion.2), channel_id=1, source_target_pairs={{0,2},{1,3},{2,0},{3,1},{4,6},{5,7},{6,4},{7,5},{8,10},{9,11},{10,... | collective-permute-start | bytes 884744 | tf_op jit(solution)/shard_map/ppermute | solution.py:24
  79.1 2.1 %collective-permute-start.19 = (f32[1152,128]{1,0:T(8,128)S(1)}, f32[1152,128]{1,0:T(8,128)S(1)}, u32[]{:S(2)}, u32[]{:S(2)}) collective-permute-start(f32[1152,128]{1,0:T(8,128)S(1)} %pad_maximum_fusion.1.refs_1_), channel_id=1, source_target_pairs={{0,1},{1,0},{2,3},{3,2},{4,5},{5,4},{6,7},{7,6},{8,9},{9,8},{10,11... | collective-permute-start | bytes 1769480 | tf_op jit(solution)/shard_map/ppermute | solution.py:24
  80.7 2.1 %collective-permute-start.18 = (f32[1152,128]{1,0:T(8,128)S(1)}, f32[1152,128]{1,0:T(8,128)S(1)}, u32[]{:S(2)}, u32[]{:S(2)}) collective-permute-start(f32[1152,128]{1,0:T(8,128)S(1)} %pad_maximum_fusion.refs_0_), channel_id=1, source_target_pairs={{0,1},{1,0},{2,3},{3,2},{4,5},{5,4},{6,7},{7,6},{8,9},{9,8},{10,11... | collective-permute-start | bytes 1769480 | tf_op jit(solution)/shard_map/ppermute | solution.py:24

commit v9 on v8

--- a/solution.py
+++ b/solution.py
@@ -122,7 +122,7 @@
 def project_kernel(half_ref, nodes_ref, signals_ref, out_ref, onehot_ref):
     @pl.when(pl.program_id(0) == 0)
     def _():
-        node = lax.broadcasted_iota(jnp.int32, onehot_ref.shape, 0)
+        node = lax.broadcasted_iota(jnp.int32, onehot_ref.shape, 0).astype(jnp.float32)
         scale = 1.0 / math.sqrt(CH // NODES)
         onehot_ref[...] = jnp.where(node == nodes_ref[...], scale, 0.0).astype(jnp.bfloat16)
 
@@ -135,7 +135,7 @@
     return [rows * quarters // sum(CHUNK_QUARTERS) for quarters in CHUNK_QUARTERS]
 
 
-def project(signals, channel_node, half):
+def project(signals, channel_nodes, half):
     rows, channels = signals.shape
     parts = [size // 2 for size in chunk_sizes(rows)]
     step = math.gcd(512, *parts)
@@ -164,42 +164,49 @@
         out_shape=jax.ShapeDtypeStruct((rows // 2, NODES), jnp.float32),
         grid_spec=grid_spec,
         compiler_params=pltpu.CompilerParams(vmem_limit_bytes=8 << 20),
-    )(half, channel_node.reshape(1, channels), signals)
-
-
-def gram_kernel(first, last, earlier, chan_ref, all_lags_ref, *refs):
+    )(half, channel_nodes, signals)
+
+
+def gram_kernel(stage, earlier, chan_ref, all_lags_ref, *refs):
     refs = list(refs)
-    mine_ref, other_ref = refs.pop(0), refs.pop(0)
-    sum_in_ref, tail_in_ref = (None, None) if first else (refs.pop(0), refs.pop(0))
-    after_ref = refs.pop(0) if last else None
+    mine_ref = refs.pop(0)
+    other_ref = None if stage == "own" else refs.pop(0)
+    sum_in_ref, tail_ref, after_ref = (None,) * 3 if stage == "first" else [refs.pop(0) for _ in range(3)]
     del refs[:earlier]
     out_ref = refs.pop(0)
-    tail_out_ref = None if last else refs.pop(0)
+    tail_out_ref = refs.pop(0) if stage == "first" else None
     ext_ref, high_ref, low_ref, sum_ref = refs
     half = mine_ref.shape[0]
-    lead = 0 if first else MAXLAG
     total_lags = all_lags_ref.shape[0]
     lag_count = sum_ref.shape[1] // NODES
     lags = [all_lags_ref[lax.rem(2 * chan_ref[0] + i, total_lags)] for i in range(lag_count)]
     own_half = lax.rem(chan_ref[0], 2)
     step_rows = high_ref.shape[0]
-    own = pl.multiple_of(lead + own_half * half, math.gcd(lead, half))
-    others = pl.multiple_of(lead + (1 - own_half) * half, math.gcd(lead, half))
-    ext_ref[pl.ds(own, half), :] = mine_ref[...]
-    ext_ref[pl.ds(others, half), :] = other_ref[...]
-    end = lead + 2 * half
-    if not first:
-        ext_ref[:lead, :] = tail_in_ref[...]
-    if last:
-        ext_ref[end:, :] = after_ref[...]
+
+    def rows_from(start, count):
+        return pl.ds(pl.multiple_of(start, math.gcd(MAXLAG, half)), count)
+
+    if stage == "own":
+        ext_ref[rows_from((1 - own_half) * MAXLAG, half), :] = mine_ref[...]
+        ext_ref[rows_from(own_half * half, MAXLAG), :] = jnp.where(own_half == 0, tail_ref[...], after_ref[...])
+        begin, steps = 0, half // step_rows
     else:
-        tail_out_ref[...] = ext_ref[end - MAXLAG : end, :]
-    steps = (end if last else end - MAXLAG) // step_rows
-    sum_ref[...] = jnp.zeros_like(sum_ref) if first else sum_in_ref[...]
+        lead = 0 if stage == "first" else MAXLAG
+        end = lead + 2 * half
+        ext_ref[rows_from(lead + own_half * half, half), :] = mine_ref[...]
+        ext_ref[rows_from(lead + (1 - own_half) * half, half), :] = other_ref[...]
+        if stage == "first":
+            tail_out_ref[...] = ext_ref[end - MAXLAG : end, :]
+            begin, steps = 0, (end - MAXLAG) // step_rows
+        else:
+            ext_ref[:lead, :] = tail_ref[...]
+            ext_ref[end:, :] = after_ref[...]
+            begin, steps = (1 - own_half) * half, (end - half) // step_rows
+    sum_ref[...] = jnp.zeros_like(sum_ref) if stage == "first" else sum_in_ref[...]
     part = 128
 
     def step(i, _):
-        start = i * step_rows
+        start = begin + i * step_rows
         for lag in range(lag_count):
             for row in range(0, step_rows, part):
                 value = ext_ref[pl.ds(start + row + lags[lag], part), :]
@@ -221,7 +228,7 @@
         return 0
 
     lax.fori_loop(0, steps, step, 0)
-    if last:
+    if stage == "rest":
         far = lag_count - 2
         for j in range(far):
             out_ref[j * NODES : (j + 1) * NODES, :] = sum_ref[:NODES, j * NODES : (j + 1) * NODES]
@@ -235,31 +242,29 @@
         out_ref[...] = sum_ref[...]
 
 
-def gram_part(chan, lags, mine, other, carried, after, earlier):
-    first, last = carried is None, after is not None
+def gram_part(stage, chan, lags, values, carried=(), earlier=()):
     count = lags.shape[0] // 2 + 2
-    blocks = 2 * (count - 2) + 1
-    operands = [chan, lags, mine, other]
-    if not first:
-        operands += list(carried)
-    if last:
-        operands.append(after)
-    if last:
-        out_shape = jax.ShapeDtypeStruct((blocks * NODES, NODES), jnp.float32)
-    else:
-        out_shape = (
-            jax.ShapeDtypeStruct((2 * NODES, count * NODES), jnp.float32),
-            jax.ShapeDtypeStruct((MAXLAG, NODES), jnp.float32),
-        )
-    rows = 2 * mine.shape[0] + (0 if first else MAXLAG) + (MAXLAG if last else 0)
+    half = values[0].shape[0]
+    sums = jax.ShapeDtypeStruct((2 * NODES, count * NODES), jnp.float32)
     vmem = pl.BlockSpec(memory_space=pltpu.VMEM)
     smem = pl.BlockSpec(memory_space=pltpu.SMEM)
+    if stage == "first":
+        rows = 2 * half
+        out_shape, out_specs = (sums, jax.ShapeDtypeStruct((MAXLAG, NODES), jnp.float32)), (vmem, vmem)
+    elif stage == "own":
+        rows = half + MAXLAG
+        out_shape, out_specs = sums, vmem
+    else:
+        rows = 2 * half + 2 * MAXLAG
+        out_shape, out_specs = jax.ShapeDtypeStruct(((2 * count - 3) * NODES, NODES), jnp.float32), vmem
     step_rows = 512
     return pl.pallas_call(
-        functools.partial(gram_kernel, first, last, len(earlier)),
+        functools.partial(gram_kernel, stage, len(earlier)),
         out_shape=out_shape,
-        in_specs=[smem, smem] + [vmem] * (len(operands) - 2) + [pl.BlockSpec(memory_space=pl.ANY)] * len(earlier),
-        out_specs=vmem if last else (vmem, vmem),
+        in_specs=[smem, smem]
+        + [vmem] * (len(values) + len(carried))
+        + [pl.BlockSpec(memory_space=pl.ANY)] * len(earlier),
+        out_specs=out_specs,
         scratch_shapes=[
             pltpu.VMEM((rows, NODES), jnp.float32),
             pltpu.VMEM((step_rows, count * NODES), jnp.bfloat16),
@@ -267,7 +272,7 @@
             pltpu.VMEM((2 * NODES, count * NODES), jnp.float32),
         ],
         compiler_params=pltpu.CompilerParams(vmem_limit_bytes=12 << 20),
-    )(*operands, *earlier)
+    )(chan, lags, *values, *carried, *earlier)
 
 
 def row_of(value, index):
@@ -487,22 +492,22 @@
 def on_device(signals, channel_node, lag_offsets):
     chan = lax.axis_index("chan").reshape(1)
     half = chan % 2
-    send = project(signals, channel_node, 1 - half)
+    channel_nodes = channel_node.astype(jnp.float32).reshape(1, -1)
+    send = project(signals, channel_nodes, 1 - half)
     received = swap(send, "chan", 1)
-    keep = project(signals, channel_node, half)
+    keep = project(signals, channel_nodes, half)
     sizes = chunk_sizes(signals.shape[0])
     totals = add_parts(keep, received, [size // 2 for size in sizes])
     sent = [swap(total, "chan", 2) for total in totals]
-    carried = after = None
-    for index in range(len(sizes)):
-        first, last = index == 0, index == len(sizes) - 1
-        value = add(totals[index], sent[index], *(() if first else (carried[1], after)))
-        other = swap(value, "chan", 1)
-        if first:
-            head = jnp.where(half[0] == 0, value[:MAXLAG], other[:MAXLAG])
-            after = first_rows_of_next(head)
-        earlier = (head,) if first else ()
-        carried = gram_part(chan, lag_offsets, value, other, carried, after if last else None, earlier)
+    value = add(totals[0], sent[0])
+    other = swap(value, "chan", 1)
+    head = jnp.where(half[0] == 0, value[:MAXLAG], other[:MAXLAG])
+    after = first_rows_of_next(head)
+    sums, tail = gram_part("first", chan, lag_offsets, (value, other), earlier=(head,))
+    value = add(totals[1], sent[1], tail, after)
+    other = swap(value, "chan", 1)
+    sums = gram_part("own", chan, lag_offsets, (value,), (sums, tail, after))
+    carried = gram_part("rest", chan, lag_offsets, (value, other), (sums, tail, after))
     rows = carried.shape[0] // 2
     mine = [route.reduce(part) for route, part in zip(routes(), (carried[:rows], carried[rows:]))]
     other = [swap(value, "chan", 1) for value in mine]

time: 112 us -> 112 us (level)
  waiting for transfers between devices: 40.8 us -> 39.5 us
    ppermute x19, waiting for transfers between devices: 40.8 us -> 39.5 us  [swap(): return lax.ppermute(value, axis, [(i, i ^ bit) for i in range(count)])]
    pallas_call x2 -> x3, Pallas kernels: 9.39 us -> 10.2 us  [gram_part(): pl.pallas_call(functools.partial(gram_kernel, stage, len(earlier)), out_s...]
    unnamed x10 -> x6, local copies, waits for them, and re-layouts: 3.29 us -> 2.61 us
  transfers between devices with their start and end apart: 20 -> 20, of which waited for: 15 -> 15; matrix products, arithmetic and copies ran while one was open for 0% -> 0% of each run, Pallas kernels for 4% -> 7%
where the time goes in v9:
time: 112 us
  Pallas kernels  42 us (38%)
  waiting for transfers between devices  39.5 us (35%)
  starting transfers between devices  25.8 us (23%)
  local copies, waits for them, and re-layouts  2.71 us (2%)
    ppermute x19, waiting for transfers between devices, swap(): return lax.ppermute(value, axis, [(i, i ^ bit) for i in range(count)])  39.5 us
    pallas_call x1, Pallas kernels, cholesky(): pl.pallas_call(functools.partial(cholesky_kernel, scale, layout), out_sha...  29.2 us
    ppermute x19, starting transfers between devices, swap(): return lax.ppermute(value, axis, [(i, i ^ bit) for i in range(count)])  24.5 us
    pallas_call x3, Pallas kernels, gram_part(): pl.pallas_call(functools.partial(gram_kernel, stage, len(earlier)), out_s...  10.2 us
    unnamed x6, local copies, waits for them, and re-layouts  2.61 us
    pallas_call x2, Pallas kernels, project(): pl.pallas_call(project_kernel, out_shape=jax.ShapeDtypeStruct((rows // 2,...  2.46 us
  transfers between devices with their start and end apart: 20, of which 15 were waited for; matrix products, arithmetic and copies ran while one was open for 0% of the time, Pallas kernels for 7%

profile of v9, /device:TPU:0, one launch (start us, length us, event | category | flops | bytes accessed | tf_op | source)
XLA Modules:
  0.0 111.6 jit_solution(6861577866357794585)
XLA Ops:
  0.0 0.7 convert_element_type.3
  0.7 2.2 %copy-done = bf16[4096,512]{1,0:T(8,128)(2,1)S(1)} copy-done((bf16[4096,512]{1,0:T(8,128)(2,1)S(1)}, bf16[4096,512]{1,0:T(8,128)(2,1)}, u32[]{:S(2)}) %copy-start) | copy-done | bytes 4194328
  2.9 1.2 %shard_map.38 = f32[2048,128]{1,0:T(8,128)S(1)} custom-call(s32[1]{0:T(128)S(6)} %sub.28.half_ref, f32[1,512]{1,0:T(1,128)S(1)} %bitcast.3, bf16[4096,512]{1,0:T(8,128)(2,1)S(1)} %copy-done), custom_call_target="tpu_custom_call" | custom-call | tf_op jit(solution)/shard_map/pallas_call | solution.py:162
  5.1 1.2 %shard_map.37.left_ref = f32[2048,128]{1,0:T(8,128)S(1)} custom-call(s32[1]{0:T(128)S(6)} %select_n.148.half_ref, f32[1,512]{1,0:T(1,128)S(1)} %bitcast.4, bf16[4096,512]{1,0:T(8,128)(2,1)S(1)} %copy-done.1), custom_call_target="tpu_custom_call" | custom-call | tf_op jit(solution)/shard_map/pallas_call | solution.py:162
  7.1 2.9 %collective-permute-start.2 = (f32[1024,128]{1,0:T(8,128)S(1)}, f32[1024,128]{1,0:T(8,128)S(1)}, u32[]{:S(2)}, u32[]{:S(2)}) collective-permute-start(f32[1024,128]{1,0:T(8,128)S(1)} %get-tuple-element.10.left_ref), channel_id=1, source_target_pairs={{0,2},{1,3},{2,0},{3,1},{4,6},{5,7},{6,4},{7,5},{8,10},{9,11},{10,... | collective-permute-start | bytes 1572872 | tf_op jit(solution)/shard_map/ppermute | solution.py:24
  10.0 12.2 %collective-permute-done.2.right_ref = f32[1024,128]{1,0:T(8,128)S(1)} collective-permute-done((f32[1024,128]{1,0:T(8,128)S(1)}, f32[1024,128]{1,0:T(8,128)S(1)}, u32[]{:S(2)}, u32[]{:S(2)}) %collective-permute-start.2) | collective-permute-done | bytes 524320 | tf_op jit(solution)/shard_map/ppermute | solution.py:24
  22.4 1.8 %collective-permute-start.1 = (f32[1024,128]{1,0:T(8,128)S(1)}, f32[1024,128]{1,0:T(8,128)S(1)}, u32[]{:S(2)}, u32[]{:S(2)}) collective-permute-start(f32[1024,128]{1,0:T(8,128)S(1)} %get-tuple-element.9.left_ref), channel_id=1, source_target_pairs={{0,2},{1,3},{2,0},{3,1},{4,6},{5,7},{6,4},{7,5},{8,10},{9,11},{10,... | collective-permute-start | bytes 1572872 | tf_op jit(solution)/shard_map/ppermute | solution.py:24
  24.3 1.3 %collective-permute-start.4 = (f32[512,128]{1,0:T(8,128)S(1)}, f32[512,128]{1,0:T(8,128)S(1)}, u32[]{:S(2)}, u32[]{:S(2)}) collective-permute-start(f32[512,128]{1,0:T(8,128)S(1)} %slice_select_fusion.refs_2_), channel_id=1, source_target_pairs={{4,0},{8,4},{12,8},{16,12},{20,16},{24,20},{28,24},{5,1},{9,5},{13... | collective-permute-start | bytes 786440 | tf_op jit(solution)/shard_map/ppermute | solution.py:119
  25.6 3.7 %shard_map.41 = (f32[256,768]{1,0:T(8,128)S(1)}, f32[512,128]{1,0:T(8,128)S(1)}) custom-call(s32[1]{0:T(128)} %bitcast.chan_ref, s32[8]{0:T(128)S(1)} %copy-done.2, f32[1024,128]{1,0:T(8,128)S(1)} %shard_map.40.refs_0_, f32[1024,128]{1,0:T(8,128)S(1)} %collective-permute-done.3.refs_1_, f32[512,128]{1,0:T(8,128)S(1)} %slice_select_fusion.refs_2_), custom_call_target="tpu_custom_call" | custom-call | tf_op jit(solution)/shard_map/pallas_call | solution.py:261
  29.3 7.4 %collective-permute-done.1.right_ref = f32[1024,128]{1,0:T(8,128)S(1)} collective-permute-done((f32[1024,128]{1,0:T(8,128)S(1)}, f32[1024,128]{1,0:T(8,128)S(1)}, u32[]{:S(2)}, u32[]{:S(2)}) %collective-permute-start.1) | collective-permute-done | bytes 524320 | tf_op jit(solution)/shard_map/ppermute | solution.py:24
  36.9 2.7 %shard_map.43.refs_2_ = f32[256,768]{1,0:T(8,128)S(1)} custom-call(s32[1]{0:T(128)} %bitcast.chan_ref, s32[8]{0:T(128)S(1)} %copy-done.2, f32[1024,128]{1,0:T(8,128)S(1)} %shard_map.42.refs_0_, f32[256,768]{1,0:T(8,128)S(1)} %get-tuple-element.12.refs_1_, f32[512,128]{1,0:T(8,128)S(1)} %get-tuple-element.11.refs_0_.refs_2_.refs_3_, ...), custom_call_target="tpu_custom_call" | custom-call | tf_op jit(solution)/shard_map/pallas_call | solution.py:261
  39.6 3.7 %shard_map.44 = f32[1152,128]{1,0:T(8,128)S(1)} custom-call(s32[1]{0:T(128)} %bitcast.chan_ref, s32[8]{0:T(128)S(1)} %copy-done.2, f32[1024,128]{1,0:T(8,128)S(1)} %shard_map.42.refs_0_, f32[1024,128]{1,0:T(8,128)S(1)} %collective-permute-done.5.refs_1_, f32[256,768]{1,0:T(8,128)S(1)} %shard_map.43.refs_2_, ...), custom_call_target="tpu_custom_call" | custom-call | tf_op jit(solution)/shard_map/pallas_call | solution.py:261
  43.4 1.9 %collective-permute-start.12 = (f32[288,128]{1,0:T(8,128)S(1)}, f32[288,128]{1,0:T(8,128)S(1)}, u32[]{:S(2)}, u32[]{:S(2)}) collective-permute-start(f32[288,128]{1,0:T(8,128)S(1)} %constant_dynamic-slice_fusion.1), channel_id=1, source_target_pairs={{0,8},{4,12},{8,0},{12,4},{16,24},{20,28},{24,16},{28,20},{1,9},{5... | collective-permute-start | bytes 442376 | tf_op jit(solution)/shard_map/ppermute | solution.py:24
  45.3 1.6 %collective-permute-start.6 = (f32[288,128]{1,0:T(8,128)S(1)}, f32[288,128]{1,0:T(8,128)S(1)}, u32[]{:S(2)}, u32[]{:S(2)}) collective-permute-start(f32[288,128]{1,0:T(8,128)S(1)} %constant_dynamic-slice_fusion.3), channel_id=1, source_target_pairs={{0,4},{4,0},{8,12},{12,8},{16,20},{20,16},{24,28},{28,24},{1,5},{5... | collective-permute-start | bytes 442376 | tf_op jit(solution)/shard_map/ppermute | solution.py:24
  46.9 2.7 %collective-permute-done.12 = f32[288,128]{1,0:T(8,128)S(1)} collective-permute-done((f32[288,128]{1,0:T(8,128)S(1)}, f32[288,128]{1,0:T(8,128)S(1)}, u32[]{:S(2)}, u32[]{:S(2)}) %collective-permute-start.12) | collective-permute-done | bytes 147488 | tf_op jit(solution)/shard_map/ppermute | solution.py:24
  49.7 1.8 %collective-permute-start.13 = (f32[144,128]{1,0:T(8,128)S(1)}, f32[144,128]{1,0:T(8,128)S(1)}, u32[]{:S(2)}, u32[]{:S(2)}) collective-permute-start(f32[144,128]{1,0:T(8,128)S(1)} %constant_dynamic-slice_fusion), channel_id=1, source_target_pairs={{0,4},{4,0},{8,12},{12,8},{16,20},{20,16},{24,28},{28,24},{1,5},{5... | collective-permute-start | bytes 221192 | tf_op jit(solution)/shard_map/ppermute | solution.py:24
  51.5 1.6 %collective-permute-start.7 = (f32[144,128]{1,0:T(8,128)S(1)}, f32[144,128]{1,0:T(8,128)S(1)}, u32[]{:S(2)}, u32[]{:S(2)}) collective-permute-start(f32[144,128]{1,0:T(8,128)S(1)} %constant_dynamic-slice_fusion.2), channel_id=1, source_target_pairs={{0,8},{4,12},{8,0},{12,4},{16,24},{20,28},{24,16},{28,20},{1,9},{5... | collective-permute-start | bytes 221192 | tf_op jit(solution)/shard_map/ppermute | solution.py:24
  53.1 1.0 collective-permute-done.13
  54.1 2.8 %collective-permute-start.14 = (f32[144,128]{1,0:T(8,128)S(1)}, f32[144,128]{1,0:T(8,128)S(1)}, u32[]{:S(2)}, u32[]{:S(2)}) collective-permute-start(f32[144,128]{1,0:T(8,128)S(1)} %dynamic-slice_add_fusion.2), channel_id=1, source_target_pairs={{0,16},{4,20},{8,24},{12,28},{16,0},{20,4},{24,8},{28,12},{1,17},{... | collective-permute-start | bytes 221192 | tf_op jit(solution)/shard_map/ppermute | solution.py:24
  57.0 2.3 %collective-permute-start.8 = (f32[144,128]{1,0:T(8,128)S(1)}, f32[144,128]{1,0:T(8,128)S(1)}, u32[]{:S(2)}, u32[]{:S(2)}) collective-permute-start(f32[144,128]{1,0:T(8,128)S(1)} %dynamic-slice_add_fusion.3), channel_id=1, source_target_pairs={{0,16},{4,20},{8,24},{12,28},{16,0},{20,4},{24,8},{28,12},{1,17},{... | collective-permute-start | bytes 221192 | tf_op jit(solution)/shard_map/ppermute | solution.py:24
  59.3 2.6 %collective-permute-done.14 = f32[144,128]{1,0:T(8,128)S(1)} collective-permute-done((f32[144,128]{1,0:T(8,128)S(1)}, f32[144,128]{1,0:T(8,128)S(1)}, u32[]{:S(2)}, u32[]{:S(2)}) %collective-permute-start.14) | collective-permute-done | bytes 73760 | tf_op jit(solution)/shard_map/ppermute | solution.py:24
  61.9 1.5 %collective-permute-start.15 = (f32[144,128]{1,0:T(8,128)S(1)}, f32[144,128]{1,0:T(8,128)S(1)}, u32[]{:S(2)}, u32[]{:S(2)}) collective-permute-start(f32[144,128]{1,0:T(8,128)S(1)} %add.85), channel_id=1, source_target_pairs={{0,4},{4,0},{8,12},{12,8},{16,20},{20,16},{24,28},{28,24},{1,5},{5... | collective-permute-start | bytes 221192 | tf_op jit(solution)/shard_map/ppermute | solution.py:24
  64.0 2.3 %collective-permute-done.15 = f32[144,128]{1,0:T(8,128)S(1)} collective-permute-done((f32[144,128]{1,0:T(8,128)S(1)}, f32[144,128]{1,0:T(8,128)S(1)}, u32[]{:S(2)}, u32[]{:S(2)}) %collective-permute-start.15) | collective-permute-done | bytes 73760 | tf_op jit(solution)/shard_map/ppermute | solution.py:24
  66.3 1.7 %collective-permute-start.16 = (f32[288,128]{1,0:T(8,128)S(1)}, f32[288,128]{1,0:T(8,128)S(1)}, u32[]{:S(2)}, u32[]{:S(2)}) collective-permute-start(f32[288,128]{1,0:T(8,128)S(1)} %pad_maximum_fusion.5), channel_id=1, source_target_pairs={{0,2},{1,3},{2,0},{3,1},{4,6},{5,7},{6,4},{7,5},{8,10},{9,11},{10,... | collective-permute-start | bytes 442376 | tf_op jit(solution)/shard_map/ppermute | solution.py:24
  68.1 1.6 %collective-permute-start.10 = (f32[288,128]{1,0:T(8,128)S(1)}, f32[288,128]{1,0:T(8,128)S(1)}, u32[]{:S(2)}, u32[]{:S(2)}) collective-permute-start(f32[288,128]{1,0:T(8,128)S(1)} %pad_maximum_fusion.4), channel_id=1, source_target_pairs={{0,4},{4,0},{8,12},{12,8},{16,20},{20,16},{24,28},{28,24},{1,5},{5... | collective-permute-start | bytes 442376 | tf_op jit(solution)/shard_map/ppermute | solution.py:24
  69.7 1.9 %collective-permute-done.16 = f32[288,128]{1,0:T(8,128)S(1)} collective-permute-done((f32[288,128]{1,0:T(8,128)S(1)}, f32[288,128]{1,0:T(8,128)S(1)}, u32[]{:S(2)}, u32[]{:S(2)}) %collective-permute-start.16) | collective-permute-done | bytes 147488 | tf_op jit(solution)/shard_map/ppermute | solution.py:24
  71.7 1.6 %collective-permute-done.10 = f32[288,128]{1,0:T(8,128)S(1)} collective-permute-done((f32[288,128]{1,0:T(8,128)S(1)}, f32[288,128]{1,0:T(8,128)S(1)}, u32[]{:S(2)}, u32[]{:S(2)}) %collective-permute-start.10) | collective-permute-done | bytes 147488 | tf_op jit(solution)/shard_map/ppermute | solution.py:24
  73.4 1.6 %collective-permute-start.11 = (f32[576,128]{1,0:T(8,128)S(1)}, f32[576,128]{1,0:T(8,128)S(1)}, u32[]{:S(2)}, u32[]{:S(2)}) collective-permute-start(f32[576,128]{1,0:T(8,128)S(1)} %pad_maximum_fusion.2), channel_id=1, source_target_pairs={{0,2},{1,3},{2,0},{3,1},{4,6},{5,7},{6,4},{7,5},{8,10},{9,11},{10,... | collective-permute-start | bytes 884744 | tf_op jit(solution)/shard_map/ppermute | solution.py:24
  74.9 3.5 %collective-permute-done.17 = f32[576,128]{1,0:T(8,128)S(1)} collective-permute-done((f32[576,128]{1,0:T(8,128)S(1)}, f32[576,128]{1,0:T(8,128)S(1)}, u32[]{:S(2)}, u32[]{:S(2)}) %collective-permute-start.17) | collective-permute-done | bytes 294944 | tf_op jit(solution)/shard_map/ppermute | solution.py:24
  78.6 1.6 %collective-permute-done.11 = f32[576,128]{1,0:T(8,128)S(1)} collective-permute-done((f32[576,128]{1,0:T(8,128)S(1)}, f32[576,128]{1,0:T(8,128)S(1)}, u32[]{:S(2)}, u32[]{:S(2)}) %collective-permute-start.11) | collective-permute-done | bytes 294944 | tf_op jit(solution)/shard_map/ppermute | solution.py:24
  80.6 1.8 %collective-permute-done.18.refs_2_ = f32[1152,128]{1,0:T(8,128)S(1)} collective-permute-done((f32[1152,128]{1,0:T(8,128)S(1)}, f32[1152,128]{1,0:T(8,128)S(1)}, u32[]{:S(2)}, u32[]{:S(2)}) %collective-permute-start.18) | collective-permute-done | bytes 589856 | tf_op jit(solution)/shard_map/ppermute | solution.py:24
  82.3 29.2 %shard_map.45 = f32[1024,1024]{1,0:T(8,128)} custom-call(s32[1]{0:T(128)S(6)} %select_n.148.half_ref, f32[1152,128]{1,0:T(8,128)S(1)} %pad_maximum_fusion.refs_0_, f32[1152,128]{1,0:T(8,128)S(1)} %pad_maximum_fusion.1.refs_1_, f32[1152,128]{1,0:T(8,128)S(1)} %collective-permute-done.18.refs_2_, f32[1152,128]{1,0:T(8,128)S(1)} %collective-permute-done.19.refs_3_), custom_call_target="tpu_custom_call" | custom-call | tf_op jit(solution)/shard_map/pallas_call | solution.py:475
  (48 shorter events, 3.7 us)
Async XLA Ops:
  0.7 2.2 %copy-start = (bf16[4096,512]{1,0:T(8,128)(2,1)S(1)}, bf16[4096,512]{1,0:T(8,128)(2,1)}, u32[]{:S(2)}) copy-start(bf16[4096,512]{1,0:T(8,128)(2,1)} %signals_ref.3) | copy-start | bytes 12582916
  2.9 2.2 %copy-start.1 = (bf16[4096,512]{1,0:T(8,128)(2,1)S(1)}, bf16[4096,512]{1,0:T(8,128)(2,1)}, u32[]{:S(2)}) copy-start(bf16[4096,512]{1,0:T(8,128)(2,1)} %signals_ref.3) | copy-start | bytes 12582916
  4.1 21.5 %copy-start.2 = (s32[8]{0:T(128)S(1)}, s32[8]{0:T(128)}, u32[]{:S(2)}) copy-start(s32[8]{0:T(128)} %all_lags_ref.5) | copy-start | bytes 100
  4.1 2.8 %collective-permute-start = (f32[2048,128]{1,0:T(8,128)S(1)}, f32[2048,128]{1,0:T(8,128)S(1)}, u32[]{:S(2)}, u32[]{:S(2)}) collective-permute-start(f32[2048,128]{1,0:T(8,128)S(1)} %shard_map.38), channel_id=1, source_target_pairs={{0,1},{1,0},{2,3},{3,2},{4,5},{5,4},{6,7},{7,6},{8,9},{9,8},{10,11... | collective-permute-start | bytes 3145736 | tf_op jit(solution)/shard_map/ppermute | solution.py:24
  7.1 15.2 %collective-permute-start.2 = (f32[1024,128]{1,0:T(8,128)S(1)}, f32[1024,128]{1,0:T(8,128)S(1)}, u32[]{:S(2)}, u32[]{:S(2)}) collective-permute-start(f32[1024,128]{1,0:T(8,128)S(1)} %get-tuple-element.10.left_ref), channel_id=1, source_target_pairs={{0,2},{1,3},{2,0},{3,1},{4,6},{5,7},{6,4},{7,5},{8,10},{9,11},{10,... | collective-permute-start | bytes 1572872 | tf_op jit(solution)/shard_map/ppermute | solution.py:24
  22.3 2.0 %collective-permute-start.3 = (f32[1024,128]{1,0:T(8,128)S(1)}, f32[1024,128]{1,0:T(8,128)S(1)}, u32[]{:S(2)}, u32[]{:S(2)}) collective-permute-start(f32[1024,128]{1,0:T(8,128)S(1)} %shard_map.40.refs_0_), channel_id=1, source_target_pairs={{0,1},{1,0},{2,3},{3,2},{4,5},{5,4},{6,7},{7,6},{8,9},{9,8},{10,11... | collective-permute-start | bytes 1572872 | tf_op jit(solution)/shard_map/ppermute | solution.py:24
  22.4 14.3 %collective-permute-start.1 = (f32[1024,128]{1,0:T(8,128)S(1)}, f32[1024,128]{1,0:T(8,128)S(1)}, u32[]{:S(2)}, u32[]{:S(2)}) collective-permute-start(f32[1024,128]{1,0:T(8,128)S(1)} %get-tuple-element.9.left_ref), channel_id=1, source_target_pairs={{0,2},{1,3},{2,0},{3,1},{4,6},{5,7},{6,4},{7,5},{8,10},{9,11},{10,... | collective-permute-start | bytes 1572872 | tf_op jit(solution)/shard_map/ppermute | solution.py:24
  24.3 12.4 %collective-permute-start.4 = (f32[512,128]{1,0:T(8,128)S(1)}, f32[512,128]{1,0:T(8,128)S(1)}, u32[]{:S(2)}, u32[]{:S(2)}) collective-permute-start(f32[512,128]{1,0:T(8,128)S(1)} %slice_select_fusion.refs_2_), channel_id=1, source_target_pairs={{4,0},{8,4},{12,8},{16,12},{20,16},{24,20},{28,24},{5,1},{9,5},{13... | collective-permute-start | bytes 786440 | tf_op jit(solution)/shard_map/ppermute | solution.py:119
  36.8 2.8 %collective-permute-start.5 = (f32[1024,128]{1,0:T(8,128)S(1)}, f32[1024,128]{1,0:T(8,128)S(1)}, u32[]{:S(2)}, u32[]{:S(2)}) collective-permute-start(f32[1024,128]{1,0:T(8,128)S(1)} %shard_map.42.refs_0_), channel_id=1, source_target_pairs={{0,1},{1,0},{2,3},{3,2},{4,5},{5,4},{6,7},{7,6},{8,9},{9,8},{10,11... | collective-permute-start | bytes 1572872 | tf_op jit(solution)/shard_map/ppermute | solution.py:24
  43.4 6.2 %collective-permute-start.12 = (f32[288,128]{1,0:T(8,128)S(1)}, f32[288,128]{1,0:T(8,128)S(1)}, u32[]{:S(2)}, u32[]{:S(2)}) collective-permute-start(f32[288,128]{1,0:T(8,128)S(1)} %constant_dynamic-slice_fusion.1), channel_id=1, source_target_pairs={{0,8},{4,12},{8,0},{12,4},{16,24},{20,28},{24,16},{28,20},{1,9},{5... | collective-permute-start | bytes 442376 | tf_op jit(solution)/shard_map/ppermute | solution.py:24
  45.3 6.1 %collective-permute-start.6 = (f32[288,128]{1,0:T(8,128)S(1)}, f32[288,128]{1,0:T(8,128)S(1)}, u32[]{:S(2)}, u32[]{:S(2)}) collective-permute-start(f32[288,128]{1,0:T(8,128)S(1)} %constant_dynamic-slice_fusion.3), channel_id=1, source_target_pairs={{0,4},{4,0},{8,12},{12,8},{16,20},{20,16},{24,28},{28,24},{1,5},{5... | collective-permute-start | bytes 442376 | tf_op jit(solution)/shard_map/ppermute | solution.py:24
  49.7 4.4 %collective-permute-start.13 = (f32[144,128]{1,0:T(8,128)S(1)}, f32[144,128]{1,0:T(8,128)S(1)}, u32[]{:S(2)}, u32[]{:S(2)}) collective-permute-start(f32[144,128]{1,0:T(8,128)S(1)} %constant_dynamic-slice_fusion), channel_id=1, source_target_pairs={{0,4},{4,0},{8,12},{12,8},{16,20},{20,16},{24,28},{28,24},{1,5},{5... | collective-permute-start | bytes 221192 | tf_op jit(solution)/shard_map/ppermute | solution.py:24
  51.5 5.4 %collective-permute-start.7 = (f32[144,128]{1,0:T(8,128)S(1)}, f32[144,128]{1,0:T(8,128)S(1)}, u32[]{:S(2)}, u32[]{:S(2)}) collective-permute-start(f32[144,128]{1,0:T(8,128)S(1)} %constant_dynamic-slice_fusion.2), channel_id=1, source_target_pairs={{0,8},{4,12},{8,0},{12,4},{16,24},{20,28},{24,16},{28,20},{1,9},{5... | collective-permute-start | bytes 221192 | tf_op jit(solution)/shard_map/ppermute | solution.py:24
  54.1 7.7 %collective-permute-start.14 = (f32[144,128]{1,0:T(8,128)S(1)}, f32[144,128]{1,0:T(8,128)S(1)}, u32[]{:S(2)}, u32[]{:S(2)}) collective-permute-start(f32[144,128]{1,0:T(8,128)S(1)} %dynamic-slice_add_fusion.2), channel_id=1, source_target_pairs={{0,16},{4,20},{8,24},{12,28},{16,0},{20,4},{24,8},{28,12},{1,17},{... | collective-permute-start | bytes 221192 | tf_op jit(solution)/shard_map/ppermute | solution.py:24
  57.0 6.5 %collective-permute-start.8 = (f32[144,128]{1,0:T(8,128)S(1)}, f32[144,128]{1,0:T(8,128)S(1)}, u32[]{:S(2)}, u32[]{:S(2)}) collective-permute-start(f32[144,128]{1,0:T(8,128)S(1)} %dynamic-slice_add_fusion.3), channel_id=1, source_target_pairs={{0,16},{4,20},{8,24},{12,28},{16,0},{20,4},{24,8},{28,12},{1,17},{... | collective-permute-start | bytes 221192 | tf_op jit(solution)/shard_map/ppermute | solution.py:24
  61.9 4.4 %collective-permute-start.15 = (f32[144,128]{1,0:T(8,128)S(1)}, f32[144,128]{1,0:T(8,128)S(1)}, u32[]{:S(2)}, u32[]{:S(2)}) collective-permute-start(f32[144,128]{1,0:T(8,128)S(1)} %add.85), channel_id=1, source_target_pairs={{0,4},{4,0},{8,12},{12,8},{16,20},{20,16},{24,28},{28,24},{1,5},{5... | collective-permute-start | bytes 221192 | tf_op jit(solution)/shard_map/ppermute | solution.py:24
  63.5 4.6 %collective-permute-start.9 = (f32[144,128]{1,0:T(8,128)S(1)}, f32[144,128]{1,0:T(8,128)S(1)}, u32[]{:S(2)}, u32[]{:S(2)}) collective-permute-start(f32[144,128]{1,0:T(8,128)S(1)} %add.78), channel_id=1, source_target_pairs={{0,8},{4,12},{8,0},{12,4},{16,24},{20,28},{24,16},{28,20},{1,9},{5... | collective-permute-start | bytes 221192 | tf_op jit(solution)/shard_map/ppermute | solution.py:24
  66.3 5.2 %collective-permute-start.16 = (f32[288,128]{1,0:T(8,128)S(1)}, f32[288,128]{1,0:T(8,128)S(1)}, u32[]{:S(2)}, u32[]{:S(2)}) collective-permute-start(f32[288,128]{1,0:T(8,128)S(1)} %pad_maximum_fusion.5), channel_id=1, source_target_pairs={{0,2},{1,3},{2,0},{3,1},{4,6},{5,7},{6,4},{7,5},{8,10},{9,11},{10,... | collective-permute-start | bytes 442376 | tf_op jit(solution)/shard_map/ppermute | solution.py:24
  68.1 5.2 %collective-permute-start.10 = (f32[288,128]{1,0:T(8,128)S(1)}, f32[288,128]{1,0:T(8,128)S(1)}, u32[]{:S(2)}, u32[]{:S(2)}) collective-permute-start(f32[288,128]{1,0:T(8,128)S(1)} %pad_maximum_fusion.4), channel_id=1, source_target_pairs={{0,4},{4,0},{8,12},{12,8},{16,20},{20,16},{24,28},{28,24},{1,5},{5... | collective-permute-start | bytes 442376 | tf_op jit(solution)/shard_map/ppermute | solution.py:24
  71.6 6.8 %collective-permute-start.17 = (f32[576,128]{1,0:T(8,128)S(1)}, f32[576,128]{1,0:T(8,128)S(1)}, u32[]{:S(2)}, u32[]{:S(2)}) collective-permute-start(f32[576,128]{1,0:T(8,128)S(1)} %pad_maximum_fusion.3), channel_id=1, source_target_pairs={{0,8},{4,12},{8,0},{12,4},{16,24},{20,28},{24,16},{28,20},{1,9},{5... | collective-permute-start | bytes 884744 | tf_op jit(solution)/shard_map/ppermute | solution.py:24
  73.4 6.8 %collective-permute-start.11 = (f32[576,128]{1,0:T(8,128)S(1)}, f32[576,128]{1,0:T(8,128)S(1)}, u32[]{:S(2)}, u32[]{:S(2)}) collective-permute-start(f32[576,128]{1,0:T(8,128)S(1)} %pad_maximum_fusion.2), channel_id=1, source_target_pairs={{0,2},{1,3},{2,0},{3,1},{4,6},{5,7},{6,4},{7,5},{8,10},{9,11},{10,... | collective-permute-start | bytes 884744 | tf_op jit(solution)/shard_map/ppermute | solution.py:24
  78.5 2.1 %collective-permute-start.19 = (f32[1152,128]{1,0:T(8,128)S(1)}, f32[1152,128]{1,0:T(8,128)S(1)}, u32[]{:S(2)}, u32[]{:S(2)}) collective-permute-start(f32[1152,128]{1,0:T(8,128)S(1)} %pad_maximum_fusion.1.refs_1_), channel_id=1, source_target_pairs={{0,1},{1,0},{2,3},{3,2},{4,5},{5,4},{6,7},{7,6},{8,9},{9,8},{10,11... | collective-permute-start | bytes 1769480 | tf_op jit(solution)/shard_map/ppermute | solution.py:24
  80.2 2.1 %collective-permute-start.18 = (f32[1152,128]{1,0:T(8,128)S(1)}, f32[1152,128]{1,0:T(8,128)S(1)}, u32[]{:S(2)}, u32[]{:S(2)}) collective-permute-start(f32[1152,128]{1,0:T(8,128)S(1)} %pad_maximum_fusion.refs_0_), channel_id=1, source_target_pairs={{0,1},{1,0},{2,3},{3,2},{4,5},{5,4},{6,7},{7,6},{8,9},{9,8},{10,11... | collective-permute-start | bytes 1769480 | tf_op jit(solution)/shard_map/ppermute | solution.py:24

commit v10 on v9

--- a/solution.py
+++ b/solution.py
@@ -14,7 +14,7 @@
 BLOCK = 128
 GROUP = 8
 SPAN = 4
-CHUNK_QUARTERS = (1, 1)
+CHUNK_QUARTERS = (1, 3)
 HIGHEST = lax.Precision.HIGHEST
 CONTRACT_ROWS = (((0,), (0,)), ((), ()))
 

time: 112 us -> 111 us (level)
    ppermute x1, waiting for transfers between devices: 0.01 us -> 7.71 us  [first_rows_of_next(): return lax.ppermute(rows, 'tm', [(i, i - 1) for i in range(1, count)])]
    ppermute x19, waiting for transfers between devices: 39.5 us -> 31.9 us  [swap(): return lax.ppermute(value, axis, [(i, i ^ bit) for i in range(count)])]
    ppermute x19, starting transfers between devices: 24.5 us -> 23.4 us  [swap(): return lax.ppermute(value, axis, [(i, i ^ bit) for i in range(count)])]
  transfers between devices with their start and end apart: 20 -> 20, of which waited for: 15 -> 16; matrix products, arithmetic and copies ran while one was open for 0% -> 0% of each run, Pallas kernels for 7% -> 6%
where the time goes in v10:
time: 111 us; the launch traced here: 110 us
  Pallas kernels  41.8 us (38%)
  waiting for transfers between devices  39.6 us (36%)
  starting transfers between devices  24.7 us (22%)
  local copies, waits for them, and re-layouts  2.71 us (2%)
    ppermute x19, waiting for transfers between devices, swap(): return lax.ppermute(value, axis, [(i, i ^ bit) for i in range(count)])  31.9 us
    pallas_call x1, Pallas kernels, cholesky(): pl.pallas_call(functools.partial(cholesky_kernel, scale, layout), out_sha...  29.2 us
    ppermute x19, starting transfers between devices, swap(): return lax.ppermute(value, axis, [(i, i ^ bit) for i in range(count)])  23.4 us
    pallas_call x3, Pallas kernels, gram_part(): pl.pallas_call(functools.partial(gram_kernel, stage, len(earlier)), out_s...  9.95 us
    ppermute x1, waiting for transfers between devices, first_rows_of_next(): return lax.ppermute(rows, 'tm', [(i, i - 1) for i in range(1, count)])  7.71 us
    unnamed x6, local copies, waits for them, and re-layouts  2.61 us
    pallas_call x2, Pallas kernels, project(): pl.pallas_call(project_kernel, out_shape=jax.ShapeDtypeStruct((rows // 2,...  2.46 us
  transfers between devices with their start and end apart: 20, of which 16 were waited for; matrix products, arithmetic and copies ran while one was open for 0% of the time, Pallas kernels for 6%

profile of v10, /device:TPU:0, one launch (start us, length us, event | category | flops | bytes accessed | tf_op | source)
XLA Modules:
  0.0 110.3 jit_solution(7726681799965347945)
XLA Ops:
  0.7 2.2 %copy-done = bf16[4096,512]{1,0:T(8,128)(2,1)S(1)} copy-done((bf16[4096,512]{1,0:T(8,128)(2,1)S(1)}, bf16[4096,512]{1,0:T(8,128)(2,1)}, u32[]{:S(2)}) %copy-start) | copy-done | bytes 4194328
  2.9 1.2 %shard_map.38 = f32[2048,128]{1,0:T(8,128)S(1)} custom-call(s32[1]{0:T(128)S(6)} %sub.28.half_ref, f32[1,512]{1,0:T(1,128)S(1)} %bitcast.3, bf16[4096,512]{1,0:T(8,128)(2,1)S(1)} %copy-done), custom_call_target="tpu_custom_call" | custom-call | tf_op jit(solution)/shard_map/pallas_call | solution.py:162
  5.1 1.2 %shard_map.37.left_ref = f32[2048,128]{1,0:T(8,128)S(1)} custom-call(s32[1]{0:T(128)S(6)} %select_n.148.half_ref, f32[1,512]{1,0:T(1,128)S(1)} %bitcast.4, bf16[4096,512]{1,0:T(8,128)(2,1)S(1)} %copy-done.1), custom_call_target="tpu_custom_call" | custom-call | tf_op jit(solution)/shard_map/pallas_call | solution.py:162
  7.1 2.9 %collective-permute-start.2 = (f32[512,128]{1,0:T(8,128)S(1)}, f32[512,128]{1,0:T(8,128)S(1)}, u32[]{:S(2)}, u32[]{:S(2)}) collective-permute-start(f32[512,128]{1,0:T(8,128)S(1)} %get-tuple-element.10.left_ref), channel_id=1, source_target_pairs={{0,2},{1,3},{2,0},{3,1},{4,6},{5,7},{6,4},{7,5},{8,10},{9,11},{10,... | collective-permute-start | bytes 786440 | tf_op jit(solution)/shard_map/ppermute | solution.py:24
  10.1 7.0 %collective-permute-done.2.right_ref = f32[512,128]{1,0:T(8,128)S(1)} collective-permute-done((f32[512,128]{1,0:T(8,128)S(1)}, f32[512,128]{1,0:T(8,128)S(1)}, u32[]{:S(2)}, u32[]{:S(2)}) %collective-permute-start.2) | collective-permute-done | bytes 262176 | tf_op jit(solution)/shard_map/ppermute | solution.py:24
  17.2 1.5 %collective-permute-done.3.refs_1_ = f32[512,128]{1,0:T(8,128)S(1)} collective-permute-done((f32[512,128]{1,0:T(8,128)S(1)}, f32[512,128]{1,0:T(8,128)S(1)}, u32[]{:S(2)}, u32[]{:S(2)}) %collective-permute-start.3) | collective-permute-done | bytes 262176 | tf_op jit(solution)/shard_map/ppermute | solution.py:24
  18.8 1.3 %collective-permute-start.4 = (f32[512,128]{1,0:T(8,128)S(1)}, f32[512,128]{1,0:T(8,128)S(1)}, u32[]{:S(2)}, u32[]{:S(2)}) collective-permute-start(f32[512,128]{1,0:T(8,128)S(1)} %broadcast_select_fusion.4.refs_2_), channel_id=1, source_target_pairs={{4,0},{8,4},{12,8},{16,12},{20,16},{24,20},{28,24},{5,1},{9,5},{13... | collective-permute-start | bytes 786440 | tf_op jit(solution)/shard_map/ppermute | solution.py:119
  20.1 1.6 %shard_map.41 = (f32[256,768]{1,0:T(8,128)S(1)}, f32[512,128]{1,0:T(8,128)S(1)}) custom-call(s32[1]{0:T(128)} %bitcast.chan_ref, s32[8]{0:T(128)S(1)} %copy-done.2, f32[512,128]{1,0:T(8,128)S(1)} %shard_map.40.refs_0_, f32[512,128]{1,0:T(8,128)S(1)} %collective-permute-done.3.refs_1_, f32[512,128]{1,0:T(8,128)S(1)} %broadcast_select_fusion.4.refs_2_), custom_call_target="tpu_custom_call" | custom-call | tf_op jit(solution)/shard_map/pallas_call | solution.py:261
  21.6 7.7 %collective-permute-done.4.refs_1_.refs_3_.refs_4_ = f32[512,128]{1,0:T(8,128)S(1)} collective-permute-done((f32[512,128]{1,0:T(8,128)S(1)}, f32[512,128]{1,0:T(8,128)S(1)}, u32[]{:S(2)}, u32[]{:S(2)}) %collective-permute-start.4) | collective-permute-done | bytes 262176 | tf_op jit(solution)/shard_map/ppermute | solution.py:119
  29.4 4.1 %collective-permute-done.1.right_ref = f32[1536,128]{1,0:T(8,128)S(1)} collective-permute-done((f32[1536,128]{1,0:T(8,128)S(1)}, f32[1536,128]{1,0:T(8,128)S(1)}, u32[]{:S(2)}, u32[]{:S(2)}) %collective-permute-start.1) | collective-permute-done | bytes 786464 | tf_op jit(solution)/shard_map/ppermute | solution.py:24
  33.7 3.7 %shard_map.43.refs_2_ = f32[256,768]{1,0:T(8,128)S(1)} custom-call(s32[1]{0:T(128)} %bitcast.chan_ref, s32[8]{0:T(128)S(1)} %copy-done.2, f32[1536,128]{1,0:T(8,128)S(1)} %shard_map.42.refs_0_, f32[256,768]{1,0:T(8,128)S(1)} %get-tuple-element.12.refs_1_, f32[512,128]{1,0:T(8,128)S(1)} %get-tuple-element.11.refs_0_.refs_2_.refs_3_, ...), custom_call_target="tpu_custom_call" | custom-call | tf_op jit(solution)/shard_map/pallas_call | solution.py:261
  37.4 4.7 %shard_map.44 = f32[1152,128]{1,0:T(8,128)S(1)} custom-call(s32[1]{0:T(128)} %bitcast.chan_ref, s32[8]{0:T(128)S(1)} %copy-done.2, f32[1536,128]{1,0:T(8,128)S(1)} %shard_map.42.refs_0_, f32[1536,128]{1,0:T(8,128)S(1)} %collective-permute-done.5.refs_1_, f32[256,768]{1,0:T(8,128)S(1)} %shard_map.43.refs_2_, ...), custom_call_target="tpu_custom_call" | custom-call | tf_op jit(solution)/shard_map/pallas_call | solution.py:261
  42.2 1.9 %collective-permute-start.12 = (f32[288,128]{1,0:T(8,128)S(1)}, f32[288,128]{1,0:T(8,128)S(1)}, u32[]{:S(2)}, u32[]{:S(2)}) collective-permute-start(f32[288,128]{1,0:T(8,128)S(1)} %constant_dynamic-slice_fusion.1), channel_id=1, source_target_pairs={{0,8},{4,12},{8,0},{12,4},{16,24},{20,28},{24,16},{28,20},{1,9},{5... | collective-permute-start | bytes 442376 | tf_op jit(solution)/shard_map/ppermute | solution.py:24
  44.1 1.6 %collective-permute-start.6 = (f32[288,128]{1,0:T(8,128)S(1)}, f32[288,128]{1,0:T(8,128)S(1)}, u32[]{:S(2)}, u32[]{:S(2)}) collective-permute-start(f32[288,128]{1,0:T(8,128)S(1)} %constant_dynamic-slice_fusion.3), channel_id=1, source_target_pairs={{0,4},{4,0},{8,12},{12,8},{16,20},{20,16},{24,28},{28,24},{1,5},{5... | collective-permute-start | bytes 442376 | tf_op jit(solution)/shard_map/ppermute | solution.py:24
  45.6 2.7 %collective-permute-done.12 = f32[288,128]{1,0:T(8,128)S(1)} collective-permute-done((f32[288,128]{1,0:T(8,128)S(1)}, f32[288,128]{1,0:T(8,128)S(1)}, u32[]{:S(2)}, u32[]{:S(2)}) %collective-permute-start.12) | collective-permute-done | bytes 147488 | tf_op jit(solution)/shard_map/ppermute | solution.py:24
  48.4 1.7 %collective-permute-start.13 = (f32[144,128]{1,0:T(8,128)S(1)}, f32[144,128]{1,0:T(8,128)S(1)}, u32[]{:S(2)}, u32[]{:S(2)}) collective-permute-start(f32[144,128]{1,0:T(8,128)S(1)} %constant_dynamic-slice_fusion), channel_id=1, source_target_pairs={{0,4},{4,0},{8,12},{12,8},{16,20},{20,16},{24,28},{28,24},{1,5},{5... | collective-permute-start | bytes 221192 | tf_op jit(solution)/shard_map/ppermute | solution.py:24
  50.2 1.6 %collective-permute-start.7 = (f32[144,128]{1,0:T(8,128)S(1)}, f32[144,128]{1,0:T(8,128)S(1)}, u32[]{:S(2)}, u32[]{:S(2)}) collective-permute-start(f32[144,128]{1,0:T(8,128)S(1)} %constant_dynamic-slice_fusion.2), channel_id=1, source_target_pairs={{0,8},{4,12},{8,0},{12,4},{16,24},{20,28},{24,16},{28,20},{1,9},{5... | collective-permute-start | bytes 221192 | tf_op jit(solution)/shard_map/ppermute | solution.py:24
  51.8 1.0 collective-permute-done.13
  52.8 2.8 %collective-permute-start.14 = (f32[144,128]{1,0:T(8,128)S(1)}, f32[144,128]{1,0:T(8,128)S(1)}, u32[]{:S(2)}, u32[]{:S(2)}) collective-permute-start(f32[144,128]{1,0:T(8,128)S(1)} %dynamic-slice_add_fusion.2), channel_id=1, source_target_pairs={{0,16},{4,20},{8,24},{12,28},{16,0},{20,4},{24,8},{28,12},{1,17},{... | collective-permute-start | bytes 221192 | tf_op jit(solution)/shard_map/ppermute | solution.py:24
  55.7 2.4 %collective-permute-start.8 = (f32[144,128]{1,0:T(8,128)S(1)}, f32[144,128]{1,0:T(8,128)S(1)}, u32[]{:S(2)}, u32[]{:S(2)}) collective-permute-start(f32[144,128]{1,0:T(8,128)S(1)} %dynamic-slice_add_fusion.3), channel_id=1, source_target_pairs={{0,16},{4,20},{8,24},{12,28},{16,0},{20,4},{24,8},{28,12},{1,17},{... | collective-permute-start | bytes 221192 | tf_op jit(solution)/shard_map/ppermute | solution.py:24
  58.0 2.5 %collective-permute-done.14 = f32[144,128]{1,0:T(8,128)S(1)} collective-permute-done((f32[144,128]{1,0:T(8,128)S(1)}, f32[144,128]{1,0:T(8,128)S(1)}, u32[]{:S(2)}, u32[]{:S(2)}) %collective-permute-start.14) | collective-permute-done | bytes 73760 | tf_op jit(solution)/shard_map/ppermute | solution.py:24
  60.6 1.5 %collective-permute-start.15 = (f32[144,128]{1,0:T(8,128)S(1)}, f32[144,128]{1,0:T(8,128)S(1)}, u32[]{:S(2)}, u32[]{:S(2)}) collective-permute-start(f32[144,128]{1,0:T(8,128)S(1)} %add.85), channel_id=1, source_target_pairs={{0,4},{4,0},{8,12},{12,8},{16,20},{20,16},{24,28},{28,24},{1,5},{5... | collective-permute-start | bytes 221192 | tf_op jit(solution)/shard_map/ppermute | solution.py:24
  62.8 2.2 %collective-permute-done.15 = f32[144,128]{1,0:T(8,128)S(1)} collective-permute-done((f32[144,128]{1,0:T(8,128)S(1)}, f32[144,128]{1,0:T(8,128)S(1)}, u32[]{:S(2)}, u32[]{:S(2)}) %collective-permute-start.15) | collective-permute-done | bytes 73760 | tf_op jit(solution)/shard_map/ppermute | solution.py:24
  65.0 1.7 %collective-permute-start.16 = (f32[288,128]{1,0:T(8,128)S(1)}, f32[288,128]{1,0:T(8,128)S(1)}, u32[]{:S(2)}, u32[]{:S(2)}) collective-permute-start(f32[288,128]{1,0:T(8,128)S(1)} %pad_maximum_fusion.5), channel_id=1, source_target_pairs={{0,2},{1,3},{2,0},{3,1},{4,6},{5,7},{6,4},{7,5},{8,10},{9,11},{10,... | collective-permute-start | bytes 442376 | tf_op jit(solution)/shard_map/ppermute | solution.py:24
  66.8 1.6 %collective-permute-start.10 = (f32[288,128]{1,0:T(8,128)S(1)}, f32[288,128]{1,0:T(8,128)S(1)}, u32[]{:S(2)}, u32[]{:S(2)}) collective-permute-start(f32[288,128]{1,0:T(8,128)S(1)} %pad_maximum_fusion.4), channel_id=1, source_target_pairs={{0,4},{4,0},{8,12},{12,8},{16,20},{20,16},{24,28},{28,24},{1,5},{5... | collective-permute-start | bytes 442376 | tf_op jit(solution)/shard_map/ppermute | solution.py:24
  68.4 1.8 %collective-permute-done.16 = f32[288,128]{1,0:T(8,128)S(1)} collective-permute-done((f32[288,128]{1,0:T(8,128)S(1)}, f32[288,128]{1,0:T(8,128)S(1)}, u32[]{:S(2)}, u32[]{:S(2)}) %collective-permute-start.16) | collective-permute-done | bytes 147488 | tf_op jit(solution)/shard_map/ppermute | solution.py:24
  70.8 1.2 %collective-permute-done.10 = f32[288,128]{1,0:T(8,128)S(1)} collective-permute-done((f32[288,128]{1,0:T(8,128)S(1)}, f32[288,128]{1,0:T(8,128)S(1)}, u32[]{:S(2)}, u32[]{:S(2)}) %collective-permute-start.10) | collective-permute-done | bytes 147488 | tf_op jit(solution)/shard_map/ppermute | solution.py:24
  72.1 1.6 %collective-permute-start.11 = (f32[576,128]{1,0:T(8,128)S(1)}, f32[576,128]{1,0:T(8,128)S(1)}, u32[]{:S(2)}, u32[]{:S(2)}) collective-permute-start(f32[576,128]{1,0:T(8,128)S(1)} %pad_maximum_fusion.2), channel_id=1, source_target_pairs={{0,2},{1,3},{2,0},{3,1},{4,6},{5,7},{6,4},{7,5},{8,10},{9,11},{10,... | collective-permute-start | bytes 884744 | tf_op jit(solution)/shard_map/ppermute | solution.py:24
  73.6 3.4 %collective-permute-done.17 = f32[576,128]{1,0:T(8,128)S(1)} collective-permute-done((f32[576,128]{1,0:T(8,128)S(1)}, f32[576,128]{1,0:T(8,128)S(1)}, u32[]{:S(2)}, u32[]{:S(2)}) %collective-permute-start.17) | collective-permute-done | bytes 294944 | tf_op jit(solution)/shard_map/ppermute | solution.py:24
  77.2 1.6 %collective-permute-done.11 = f32[576,128]{1,0:T(8,128)S(1)} collective-permute-done((f32[576,128]{1,0:T(8,128)S(1)}, f32[576,128]{1,0:T(8,128)S(1)}, u32[]{:S(2)}, u32[]{:S(2)}) %collective-permute-start.11) | collective-permute-done | bytes 294944 | tf_op jit(solution)/shard_map/ppermute | solution.py:24
  79.2 1.8 %collective-permute-done.18.refs_2_ = f32[1152,128]{1,0:T(8,128)S(1)} collective-permute-done((f32[1152,128]{1,0:T(8,128)S(1)}, f32[1152,128]{1,0:T(8,128)S(1)}, u32[]{:S(2)}, u32[]{:S(2)}) %collective-permute-start.18) | collective-permute-done | bytes 589856 | tf_op jit(solution)/shard_map/ppermute | solution.py:24
  81.0 29.2 %shard_map.45 = f32[1024,1024]{1,0:T(8,128)} custom-call(s32[1]{0:T(128)S(6)} %select_n.148.half_ref, f32[1152,128]{1,0:T(8,128)S(1)} %pad_maximum_fusion.refs_0_, f32[1152,128]{1,0:T(8,128)S(1)} %pad_maximum_fusion.1.refs_1_, f32[1152,128]{1,0:T(8,128)S(1)} %collective-permute-done.18.refs_2_, f32[1152,128]{1,0:T(8,128)S(1)} %collective-permute-done.19.refs_3_), custom_call_target="tpu_custom_call" | custom-call | tf_op jit(solution)/shard_map/pallas_call | solution.py:475
  (48 shorter events, 4.8 us)
Async XLA Ops:
  0.7 2.2 %copy-start = (bf16[4096,512]{1,0:T(8,128)(2,1)S(1)}, bf16[4096,512]{1,0:T(8,128)(2,1)}, u32[]{:S(2)}) copy-start(bf16[4096,512]{1,0:T(8,128)(2,1)} %signals_ref.3) | copy-start | bytes 12582916
  2.9 2.2 %copy-start.1 = (bf16[4096,512]{1,0:T(8,128)(2,1)S(1)}, bf16[4096,512]{1,0:T(8,128)(2,1)}, u32[]{:S(2)}) copy-start(bf16[4096,512]{1,0:T(8,128)(2,1)} %signals_ref.3) | copy-start | bytes 12582916
  4.1 16.0 %copy-start.2 = (s32[8]{0:T(128)S(1)}, s32[8]{0:T(128)}, u32[]{:S(2)}) copy-start(s32[8]{0:T(128)} %all_lags_ref.5) | copy-start | bytes 100
  4.1 2.8 %collective-permute-start = (f32[2048,128]{1,0:T(8,128)S(1)}, f32[2048,128]{1,0:T(8,128)S(1)}, u32[]{:S(2)}, u32[]{:S(2)}) collective-permute-start(f32[2048,128]{1,0:T(8,128)S(1)} %shard_map.38), channel_id=1, source_target_pairs={{0,1},{1,0},{2,3},{3,2},{4,5},{5,4},{6,7},{7,6},{8,9},{9,8},{10,11... | collective-permute-start | bytes 3145736 | tf_op jit(solution)/shard_map/ppermute | solution.py:24
  7.1 10.0 %collective-permute-start.2 = (f32[512,128]{1,0:T(8,128)S(1)}, f32[512,128]{1,0:T(8,128)S(1)}, u32[]{:S(2)}, u32[]{:S(2)}) collective-permute-start(f32[512,128]{1,0:T(8,128)S(1)} %get-tuple-element.10.left_ref), channel_id=1, source_target_pairs={{0,2},{1,3},{2,0},{3,1},{4,6},{5,7},{6,4},{7,5},{8,10},{9,11},{10,... | collective-permute-start | bytes 786440 | tf_op jit(solution)/shard_map/ppermute | solution.py:24
  10.0 23.5 %collective-permute-start.1 = (f32[1536,128]{1,0:T(8,128)S(1)}, f32[1536,128]{1,0:T(8,128)S(1)}, u32[]{:S(2)}, u32[]{:S(2)}) collective-permute-start(f32[1536,128]{1,0:T(8,128)S(1)} %get-tuple-element.9.left_ref), channel_id=1, source_target_pairs={{0,2},{1,3},{2,0},{3,1},{4,6},{5,7},{6,4},{7,5},{8,10},{9,11},{10,... | collective-permute-start | bytes 2359304 | tf_op jit(solution)/shard_map/ppermute | solution.py:24
  17.1 1.6 %collective-permute-start.3 = (f32[512,128]{1,0:T(8,128)S(1)}, f32[512,128]{1,0:T(8,128)S(1)}, u32[]{:S(2)}, u32[]{:S(2)}) collective-permute-start(f32[512,128]{1,0:T(8,128)S(1)} %shard_map.40.refs_0_), channel_id=1, source_target_pairs={{0,1},{1,0},{2,3},{3,2},{4,5},{5,4},{6,7},{7,6},{8,9},{9,8},{10,11... | collective-permute-start | bytes 786440 | tf_op jit(solution)/shard_map/ppermute | solution.py:24
  18.8 10.6 %collective-permute-start.4 = (f32[512,128]{1,0:T(8,128)S(1)}, f32[512,128]{1,0:T(8,128)S(1)}, u32[]{:S(2)}, u32[]{:S(2)}) collective-permute-start(f32[512,128]{1,0:T(8,128)S(1)} %broadcast_select_fusion.4.refs_2_), channel_id=1, source_target_pairs={{4,0},{8,4},{12,8},{16,12},{20,16},{24,20},{28,24},{5,1},{9,5},{13... | collective-permute-start | bytes 786440 | tf_op jit(solution)/shard_map/ppermute | solution.py:119
  33.5 3.8 %collective-permute-start.5 = (f32[1536,128]{1,0:T(8,128)S(1)}, f32[1536,128]{1,0:T(8,128)S(1)}, u32[]{:S(2)}, u32[]{:S(2)}) collective-permute-start(f32[1536,128]{1,0:T(8,128)S(1)} %shard_map.42.refs_0_), channel_id=1, source_target_pairs={{0,1},{1,0},{2,3},{3,2},{4,5},{5,4},{6,7},{7,6},{8,9},{9,8},{10,11... | collective-permute-start | bytes 2359304 | tf_op jit(solution)/shard_map/ppermute | solution.py:24
  42.2 6.2 %collective-permute-start.12 = (f32[288,128]{1,0:T(8,128)S(1)}, f32[288,128]{1,0:T(8,128)S(1)}, u32[]{:S(2)}, u32[]{:S(2)}) collective-permute-start(f32[288,128]{1,0:T(8,128)S(1)} %constant_dynamic-slice_fusion.1), channel_id=1, source_target_pairs={{0,8},{4,12},{8,0},{12,4},{16,24},{20,28},{24,16},{28,20},{1,9},{5... | collective-permute-start | bytes 442376 | tf_op jit(solution)/shard_map/ppermute | solution.py:24
  44.1 6.1 %collective-permute-start.6 = (f32[288,128]{1,0:T(8,128)S(1)}, f32[288,128]{1,0:T(8,128)S(1)}, u32[]{:S(2)}, u32[]{:S(2)}) collective-permute-start(f32[288,128]{1,0:T(8,128)S(1)} %constant_dynamic-slice_fusion.3), channel_id=1, source_target_pairs={{0,4},{4,0},{8,12},{12,8},{16,20},{20,16},{24,28},{28,24},{1,5},{5... | collective-permute-start | bytes 442376 | tf_op jit(solution)/shard_map/ppermute | solution.py:24
  48.4 4.4 %collective-permute-start.13 = (f32[144,128]{1,0:T(8,128)S(1)}, f32[144,128]{1,0:T(8,128)S(1)}, u32[]{:S(2)}, u32[]{:S(2)}) collective-permute-start(f32[144,128]{1,0:T(8,128)S(1)} %constant_dynamic-slice_fusion), channel_id=1, source_target_pairs={{0,4},{4,0},{8,12},{12,8},{16,20},{20,16},{24,28},{28,24},{1,5},{5... | collective-permute-start | bytes 221192 | tf_op jit(solution)/shard_map/ppermute | solution.py:24
  50.2 5.4 %collective-permute-start.7 = (f32[144,128]{1,0:T(8,128)S(1)}, f32[144,128]{1,0:T(8,128)S(1)}, u32[]{:S(2)}, u32[]{:S(2)}) collective-permute-start(f32[144,128]{1,0:T(8,128)S(1)} %constant_dynamic-slice_fusion.2), channel_id=1, source_target_pairs={{0,8},{4,12},{8,0},{12,4},{16,24},{20,28},{24,16},{28,20},{1,9},{5... | collective-permute-start | bytes 221192 | tf_op jit(solution)/shard_map/ppermute | solution.py:24
  52.8 7.7 %collective-permute-start.14 = (f32[144,128]{1,0:T(8,128)S(1)}, f32[144,128]{1,0:T(8,128)S(1)}, u32[]{:S(2)}, u32[]{:S(2)}) collective-permute-start(f32[144,128]{1,0:T(8,128)S(1)} %dynamic-slice_add_fusion.2), channel_id=1, source_target_pairs={{0,16},{4,20},{8,24},{12,28},{16,0},{20,4},{24,8},{28,12},{1,17},{... | collective-permute-start | bytes 221192 | tf_op jit(solution)/shard_map/ppermute | solution.py:24
  55.7 6.5 %collective-permute-start.8 = (f32[144,128]{1,0:T(8,128)S(1)}, f32[144,128]{1,0:T(8,128)S(1)}, u32[]{:S(2)}, u32[]{:S(2)}) collective-permute-start(f32[144,128]{1,0:T(8,128)S(1)} %dynamic-slice_add_fusion.3), channel_id=1, source_target_pairs={{0,16},{4,20},{8,24},{12,28},{16,0},{20,4},{24,8},{28,12},{1,17},{... | collective-permute-start | bytes 221192 | tf_op jit(solution)/shard_map/ppermute | solution.py:24
  60.6 4.4 %collective-permute-start.15 = (f32[144,128]{1,0:T(8,128)S(1)}, f32[144,128]{1,0:T(8,128)S(1)}, u32[]{:S(2)}, u32[]{:S(2)}) collective-permute-start(f32[144,128]{1,0:T(8,128)S(1)} %add.85), channel_id=1, source_target_pairs={{0,4},{4,0},{8,12},{12,8},{16,20},{20,16},{24,28},{28,24},{1,5},{5... | collective-permute-start | bytes 221192 | tf_op jit(solution)/shard_map/ppermute | solution.py:24
  62.1 4.6 %collective-permute-start.9 = (f32[144,128]{1,0:T(8,128)S(1)}, f32[144,128]{1,0:T(8,128)S(1)}, u32[]{:S(2)}, u32[]{:S(2)}) collective-permute-start(f32[144,128]{1,0:T(8,128)S(1)} %add.78), channel_id=1, source_target_pairs={{0,8},{4,12},{8,0},{12,4},{16,24},{20,28},{24,16},{28,20},{1,9},{5... | collective-permute-start | bytes 221192 | tf_op jit(solution)/shard_map/ppermute | solution.py:24
  65.0 5.2 %collective-permute-start.16 = (f32[288,128]{1,0:T(8,128)S(1)}, f32[288,128]{1,0:T(8,128)S(1)}, u32[]{:S(2)}, u32[]{:S(2)}) collective-permute-start(f32[288,128]{1,0:T(8,128)S(1)} %pad_maximum_fusion.5), channel_id=1, source_target_pairs={{0,2},{1,3},{2,0},{3,1},{4,6},{5,7},{6,4},{7,5},{8,10},{9,11},{10,... | collective-permute-start | bytes 442376 | tf_op jit(solution)/shard_map/ppermute | solution.py:24
  66.8 5.2 %collective-permute-start.10 = (f32[288,128]{1,0:T(8,128)S(1)}, f32[288,128]{1,0:T(8,128)S(1)}, u32[]{:S(2)}, u32[]{:S(2)}) collective-permute-start(f32[288,128]{1,0:T(8,128)S(1)} %pad_maximum_fusion.4), channel_id=1, source_target_pairs={{0,4},{4,0},{8,12},{12,8},{16,20},{20,16},{24,28},{28,24},{1,5},{5... | collective-permute-start | bytes 442376 | tf_op jit(solution)/shard_map/ppermute | solution.py:24
  70.3 6.8 %collective-permute-start.17 = (f32[576,128]{1,0:T(8,128)S(1)}, f32[576,128]{1,0:T(8,128)S(1)}, u32[]{:S(2)}, u32[]{:S(2)}) collective-permute-start(f32[576,128]{1,0:T(8,128)S(1)} %pad_maximum_fusion.3), channel_id=1, source_target_pairs={{0,8},{4,12},{8,0},{12,4},{16,24},{20,28},{24,16},{28,20},{1,9},{5... | collective-permute-start | bytes 884744 | tf_op jit(solution)/shard_map/ppermute | solution.py:24
  72.1 6.8 %collective-permute-start.11 = (f32[576,128]{1,0:T(8,128)S(1)}, f32[576,128]{1,0:T(8,128)S(1)}, u32[]{:S(2)}, u32[]{:S(2)}) collective-permute-start(f32[576,128]{1,0:T(8,128)S(1)} %pad_maximum_fusion.2), channel_id=1, source_target_pairs={{0,2},{1,3},{2,0},{3,1},{4,6},{5,7},{6,4},{7,5},{8,10},{9,11},{10,... | collective-permute-start | bytes 884744 | tf_op jit(solution)/shard_map/ppermute | solution.py:24
  77.2 2.1 %collective-permute-start.19 = (f32[1152,128]{1,0:T(8,128)S(1)}, f32[1152,128]{1,0:T(8,128)S(1)}, u32[]{:S(2)}, u32[]{:S(2)}) collective-permute-start(f32[1152,128]{1,0:T(8,128)S(1)} %pad_maximum_fusion.1.refs_1_), channel_id=1, source_target_pairs={{0,1},{1,0},{2,3},{3,2},{4,5},{5,4},{6,7},{7,6},{8,9},{9,8},{10,11... | collective-permute-start | bytes 1769480 | tf_op jit(solution)/shard_map/ppermute | solution.py:24
  78.9 2.1 %collective-permute-start.18 = (f32[1152,128]{1,0:T(8,128)S(1)}, f32[1152,128]{1,0:T(8,128)S(1)}, u32[]{:S(2)}, u32[]{:S(2)}) collective-permute-start(f32[1152,128]{1,0:T(8,128)S(1)} %pad_maximum_fusion.refs_0_), channel_id=1, source_target_pairs={{0,1},{1,0},{2,3},{3,2},{4,5},{5,4},{6,7},{7,6},{8,9},{9,8},{10,11... | collective-permute-start | bytes 1769480 | tf_op jit(solution)/shard_map/ppermute | solution.py:24
